TPU v7x, 128 devices: a whole 4x4x4 slice. The times are simulated.
128 devices in a mesh: dp: 8 (over y_lo, x), ctx: 16 (over y_hi, z, core).
Axes of the slice: x: 4, y: 4 (y_hi: 2, y_lo: 2; y = y_hi * 2 + y_lo), z: 4, core: 2. Of those that a mesh axis runs over, the one named last changes fastest.
Arguments:
- tokens: bfloat16 [32768, 1024], P(('dp', 'ctx')), may hold values from -6 to 6
- cotangent: bfloat16 [32768, 1024], P(('dp', 'ctx')), may hold values from -6 to 6
- in_proj: bfloat16 [1024, 2048], replicated, may hold values from -0.1875 to 0.1875
- out_proj: bfloat16 [512, 1024], replicated, may hold values from -0.25 to 0.25
- rab_time: float32 [12, 4], replicated, may hold values from -3 to 3
- seq_lengths: int32 [8, 3], P('dp'), may hold values from 1 to 2048, 4096 in all within a row
- block_mask: int32 [8, 32, 32], P('dp', 'ctx'), may hold values 0 or 1
- time_bucket: int32 [32768], P(('dp', 'ctx')), may hold values from 0 to 28665, as said below
Outputs:
- output: bfloat16 [32768, 1024], P(('dp', 'ctx'))
- grad_in: bfloat16 [32768, 1024], P(('dp', 'ctx'))
- proj_grad: float32 [512, 1024], P(('dp', 'ctx'))
- rab_grad: float32 [12, 4], replicated
Inputs may be any that keep to these rules, and one draw needn't show every extreme that they name: `seq_lengths`: each row holds the lengths of the 3 sequences of one group, laid end to end from the group's position 0; a row sums to 4096. `time_bucket`: within each group the values never fall as the position pos(r) rises; position 0 has 0 and position 4095 has 28665.
All inputs are finite; a program needn't handle non-finite values. No bound on the sum of `block_mask` on one device may be relied on, other than what follows from the above.
Results may differ from a plain program's by a relative error of at most 0.009.
Values may be sent and summed in bfloat16 or wider, within the bound.
No kernel may reach another device: no remote copies, remote signals or barrier semaphores. Data moves between devices by JAX's collectives and lax.ppermute only.
A program may use at most 128 MiB of HBM per device.

v0:
```python
import math

import jax
import jax.numpy as jnp
from jax import lax
from jax.sharding import PartitionSpec as P

TILE = 128


norm_eps = 1e-05
key_block = 512


def norm_rows(values):
    centre = jnp.mean(values, axis=-1, keepdims=True)
    shifted = values - centre
    spread = jnp.mean(shifted * shifted, axis=-1, keepdims=True)
    inverse = lax.rsqrt(spread + norm_eps)
    return (shifted * inverse, inverse)


def norm_back(upstream, normed, inverse):
    first_mean = jnp.mean(upstream, axis=-1, keepdims=True)
    second_mean = jnp.mean(upstream * normed, axis=-1, keepdims=True)
    return inverse * (upstream - first_mean - normed * second_mean)


def silu_slope(values):
    sigmoid = jax.nn.sigmoid(values)
    return sigmoid * (1.0 + values * (1.0 - sigmoid))


def row_position(rows, dev_rows, dev_count):
    half_rows = dev_rows // 2
    device_id = rows // dev_rows
    within = rows % dev_rows
    early = device_id * half_rows + within
    late = (2 * dev_count - 1 - device_id) * half_rows + within - half_rows
    return jnp.where(within < half_rows, early, late)


def segment_of(positions, seq_ends):
    return jnp.sum((positions[:, None] >= seq_ends[None, :]).astype(jnp.int32), axis=1)


def gap_level(query_time, key_time, bucket_count):
    time_gap = jnp.maximum(query_time[:, None] - key_time[None, :], 0)
    bucket_ids = jnp.zeros(time_gap.shape, jnp.int32)
    for doubling in range(1, bucket_count):
        bucket_ids = bucket_ids + (time_gap + 1 >= 2**doubling).astype(jnp.int32)
    return bucket_ids


def pair_mask(query_pos, query_seg, query_tiles, key_pos, key_rows, key_seg):
    tile_count = query_tiles.shape[1]
    key_pick = (
        key_rows[:, None] // TILE == jnp.arange(tile_count, dtype=jnp.int32)[None, :]
    ).astype(jnp.bfloat16)
    allowed = lax.dot_general(
        query_tiles, key_pick, (((1,), (1,)), ((), ())), preferred_element_type=jnp.float32
    )
    causal = (key_pos[None, :] <= query_pos[:, None]) & (key_seg[None, :] == query_seg[:, None])
    return jnp.where(causal, allowed, 0.0)


def pair_bias(bucket_ids, rab_time):
    head_count = rab_time.shape[1]
    shape_out = (head_count,) + bucket_ids.shape
    bias_terms = jnp.broadcast_to(rab_time[0][:, None, None], shape_out)
    for bucket_id in range(1, rab_time.shape[0]):
        bias_terms = jnp.where(
            bucket_ids[None] == bucket_id, rab_time[bucket_id][:, None, None], bias_terms
        )
    return bias_terms


def pair_scores(query_heads, key_heads, bucket_ids, rab_time, score_scale):
    dots = jnp.einsum("qhd,khd->hqk", query_heads, key_heads, preferred_element_type=jnp.float32)
    return dots * score_scale + pair_bias(bucket_ids, rab_time)


def pair_forward(query_heads, key_heads, value_heads, keep_mask, bucket_ids, rab_time, score_scale):
    scores = pair_scores(query_heads, key_heads, bucket_ids, rab_time, score_scale)
    weights = (jax.nn.silu(scores) * keep_mask[None]).astype(jnp.bfloat16)
    return jnp.einsum("hqk,khd->qhd", weights, value_heads, preferred_element_type=jnp.float32)


def pair_back(
    query_heads,
    grad_heads,
    key_heads,
    value_heads,
    keep_mask,
    bucket_ids,
    rab_time,
    score_scale,
    want_query,
    want_key,
):
    scores = pair_scores(query_heads, key_heads, bucket_ids, rab_time, score_scale)
    d_weight = jnp.einsum(
        "qhd,khd->hqk", grad_heads, value_heads, preferred_element_type=jnp.float32
    )
    d_score = d_weight * keep_mask[None] * silu_slope(scores)
    score_half = d_score.astype(jnp.bfloat16)
    parts = ()
    if want_query:
        onehot = (bucket_ids[:, :, None] == jnp.arange(rab_time.shape[0], dtype=jnp.int32)).astype(
            jnp.float32
        )
        rab_part = jnp.einsum("hqk,qkb->bh", d_score, onehot, precision=lax.Precision.HIGHEST)
        grad_query = jnp.einsum(
            "hqk,khd->qhd", score_half, key_heads, preferred_element_type=jnp.float32
        )
        parts = (grad_query, rab_part)
    if want_key:
        weights = (jax.nn.silu(scores) * keep_mask[None]).astype(jnp.bfloat16)
        grad_key = jnp.einsum(
            "hqk,qhd->khd", score_half, query_heads, preferred_element_type=jnp.float32
        )
        grad_value = jnp.einsum(
            "hqk,qhd->khd", weights, grad_heads, preferred_element_type=jnp.float32
        )
        parts = parts + (grad_key, grad_value)
    return parts


def over_blocks(total_rows, step_fn, carried):
    return lax.fori_loop(
        0,
        total_rows // key_block,
        lambda block_id, running: step_fn(running, block_id * key_block, key_block),
        carried,
    )


def on_device(tokens, cotangent, in_proj, out_proj, rab_time, seq_lengths, block_mask, time_bucket):
    tok_rows = tokens.shape[0]
    inner_width = out_proj.shape[0]
    head_count = rab_time.shape[1]
    head_width = inner_width // head_count
    bucket_count = rab_time.shape[0]
    score_scale = 1.0 / math.sqrt(head_width)
    ctx_count = lax.axis_size("ctx")
    first_row = lax.axis_index("ctx") * tok_rows
    seq_ends = jnp.cumsum(seq_lengths[0], dtype=jnp.int32)
    local_pos = jnp.arange(tok_rows, dtype=jnp.int32)
    own_rows = first_row + local_pos
    query_pos = row_position(own_rows, tok_rows, ctx_count)
    query_seg = segment_of(query_pos, seq_ends)
    tile_pick = (
        local_pos[:, None] // TILE == jnp.arange(block_mask.shape[1], dtype=jnp.int32)[None, :]
    ).astype(jnp.bfloat16)
    query_tiles = jnp.dot(
        tile_pick, block_mask[0].astype(jnp.bfloat16), preferred_element_type=jnp.float32
    ).astype(jnp.bfloat16)
    token_wide = tokens.astype(jnp.float32)
    normed, inverse_x = norm_rows(token_wide)
    pre_act = jnp.dot(normed.astype(jnp.bfloat16), in_proj, preferred_element_type=jnp.float32)
    activated = jax.nn.silu(pre_act).astype(jnp.bfloat16)
    gate_u = activated[:, :inner_width]
    value_act = activated[:, inner_width : 2 * inner_width]
    query_act = activated[:, 2 * inner_width : 3 * inner_width]
    key_act = activated[:, 3 * inner_width :]
    query_heads = query_act.reshape(tok_rows, head_count, head_width)
    local_keys = key_act.reshape(tok_rows, head_count, head_width)
    local_values = value_act.reshape(tok_rows, head_count, head_width)
    kv_local = (key_act, value_act, time_bucket)
    empty_out = jnp.zeros((tok_rows, inner_width), jnp.float32)
    key_piece = lax.all_gather(kv_local[0], "ctx", axis=0, tiled=True)
    value_piece = lax.all_gather(kv_local[1], "ctx", axis=0, tiled=True)
    time_piece = lax.all_gather(kv_local[2], "ctx", axis=0, tiled=True)

    def forward_step(running, offset, span_rows):
        key_heads = lax.dynamic_slice_in_dim(key_piece, offset, span_rows, 0).reshape(
            span_rows, head_count, head_width
        )
        value_heads = lax.dynamic_slice_in_dim(value_piece, offset, span_rows, 0).reshape(
            span_rows, head_count, head_width
        )
        key_time = lax.dynamic_slice_in_dim(time_piece, offset, span_rows, 0)
        key_rows = offset + jnp.arange(span_rows, dtype=jnp.int32)
        key_pos = row_position(key_rows, tok_rows, ctx_count)
        keep_mask = pair_mask(
            query_pos, query_seg, query_tiles, key_pos, key_rows, segment_of(key_pos, seq_ends)
        )
        bucket_ids = gap_level(time_bucket, key_time, bucket_count)
        added = pair_forward(
            query_heads, key_heads, value_heads, keep_mask, bucket_ids, rab_time, score_scale
        )
        return running + added.reshape(tok_rows, inner_width)

    attention = over_blocks(key_piece.shape[0], forward_step, empty_out)
    attn_norm, inverse_a = norm_rows(attention)
    mixed = (attn_norm * gate_u.astype(jnp.float32)).astype(jnp.bfloat16)
    output = (token_wide + jnp.dot(mixed, out_proj, preferred_element_type=jnp.float32)).astype(
        jnp.bfloat16
    )
    proj_grad = lax.psum_scatter(
        lax.dot_general(
            mixed, cotangent, (((0,), (0,)), ((), ())), preferred_element_type=jnp.float32
        ),
        ("dp", "ctx"),
        scatter_dimension=0,
        tiled=True,
    )
    grad_mix = lax.dot_general(
        cotangent, out_proj, (((1,), (1,)), ((), ())), preferred_element_type=jnp.float32
    )
    grad_gate = grad_mix * attn_norm
    grad_attn = norm_back(grad_mix * gate_u.astype(jnp.float32), attn_norm, inverse_a).astype(
        jnp.bfloat16
    )
    grad_heads = grad_attn.reshape(tok_rows, head_count, head_width)
    start_totals = (empty_out, jnp.zeros(rab_time.shape, jnp.float32))
    back_key_piece = lax.all_gather(kv_local[0], "ctx", axis=0, tiled=True)
    back_value_piece = lax.all_gather(kv_local[1], "ctx", axis=0, tiled=True)
    back_time_piece = lax.all_gather(kv_local[2], "ctx", axis=0, tiled=True)

    def back_step(running, offset, span_rows):
        key_heads = lax.dynamic_slice_in_dim(back_key_piece, offset, span_rows, 0).reshape(
            span_rows, head_count, head_width
        )
        value_heads = lax.dynamic_slice_in_dim(back_value_piece, offset, span_rows, 0).reshape(
            span_rows, head_count, head_width
        )
        key_time = lax.dynamic_slice_in_dim(back_time_piece, offset, span_rows, 0)
        key_rows = offset + jnp.arange(span_rows, dtype=jnp.int32)
        key_pos = row_position(key_rows, tok_rows, ctx_count)
        keep_mask = pair_mask(
            query_pos, query_seg, query_tiles, key_pos, key_rows, segment_of(key_pos, seq_ends)
        )
        bucket_ids = gap_level(time_bucket, key_time, bucket_count)
        parts = pair_back(
            query_heads,
            grad_heads,
            key_heads,
            value_heads,
            keep_mask,
            bucket_ids,
            rab_time,
            score_scale,
            True,
            False,
        )
        query_total = running[0] + parts[0].reshape(tok_rows, inner_width)
        rab_total = running[1] + parts[1]
        return (query_total, rab_total)

    back_totals = over_blocks(back_key_piece.shape[0], back_step, start_totals)
    query_sum, rab_sum = back_totals
    remote_query = lax.all_gather(query_act, "ctx", axis=0, tiled=True)
    remote_grad = lax.all_gather(grad_attn, "ctx", axis=0, tiled=True)
    remote_time = lax.all_gather(time_bucket, "ctx", axis=0, tiled=True)
    remote_tiles = lax.all_gather(query_tiles, "ctx", axis=0, tiled=True)

    def key_step(running, offset, span_rows):
        far_query = lax.dynamic_slice_in_dim(remote_query, offset, span_rows, 0).reshape(
            span_rows, head_count, head_width
        )
        far_grad = lax.dynamic_slice_in_dim(remote_grad, offset, span_rows, 0).reshape(
            span_rows, head_count, head_width
        )
        far_time = lax.dynamic_slice_in_dim(remote_time, offset, span_rows, 0)
        far_tiles = lax.dynamic_slice_in_dim(remote_tiles, offset, span_rows, 0)
        far_rows = offset + jnp.arange(span_rows, dtype=jnp.int32)
        far_pos = row_position(far_rows, tok_rows, ctx_count)
        keep_mask = pair_mask(
            far_pos, segment_of(far_pos, seq_ends), far_tiles, query_pos, own_rows, query_seg
        )
        bucket_ids = gap_level(far_time, time_bucket, bucket_count)
        parts = pair_back(
            far_query,
            far_grad,
            local_keys,
            local_values,
            keep_mask,
            bucket_ids,
            rab_time,
            score_scale,
            False,
            True,
        )
        return (
            running[0] + parts[0].reshape(tok_rows, inner_width),
            running[1] + parts[1].reshape(tok_rows, inner_width),
        )

    key_sum, value_sum = over_blocks(remote_query.shape[0], key_step, (empty_out, empty_out))
    rab_grad = lax.psum(rab_sum, ("dp", "ctx"))
    grad_act = jnp.concatenate(
        [grad_gate, value_sum, query_sum * score_scale, key_sum * score_scale], axis=1
    )
    grad_pre = (grad_act * silu_slope(pre_act)).astype(jnp.bfloat16)
    grad_normed = lax.dot_general(
        grad_pre, in_proj, (((1,), (1,)), ((), ())), preferred_element_type=jnp.float32
    )
    grad_in = (cotangent.astype(jnp.float32) + norm_back(grad_normed, normed, inverse_x)).astype(
        jnp.bfloat16
    )
    return (output, grad_in, proj_grad, rab_grad)


def solution(mesh):
    placed = (
        P(("dp", "ctx"), None),
        P(("dp", "ctx"), None),
        P(),
        P(),
        P(),
        P("dp", None),
        P("dp", "ctx", None),
        P(("dp", "ctx")),
    )
    return jax.shard_map(
        on_device,
        mesh=mesh,
        in_specs=placed,
        out_specs=(P(("dp", "ctx"), None), P(("dp", "ctx"), None), P(("dp", "ctx"), None), P()),
        check_vma=False,
    )
```

profile of v0, /device:TPU:24, one launch (start us, length us, event | category | flops | bytes accessed | tf_op | source)
XLA Modules:
  0.0 685.3 jit_solution(16091054040238819520)
XLA Ops:
  9.9 5.1 multiply_convert_fusion.4
  20.0 24.4 %all-gather = s32[16,1,256]{2,1,0:T(1,128)} all-gather(s32[1,1,256]{2,1,0:T(1,128)S(1)} %bitcast.249), channel_id=1, replica_groups=mesh['dp'=8,'ctx'=16] {'ctx'}, dimensions={0}, use_global_device_ids=true | all-gather | bytes 17408 | tf_op jit(solution)/shard_map/all_gather | solution.py:173
  45.1 28.2 %all-gather.6.cloned.1.call-done = bf16[4096,512]{1,0:T(8,128)(2,1)} async-done(((bf16[256,512]{1,0:T(8,128)(2,1)}), bf16[4096,512]{1,0:T(8,128)(2,1)}) %all-gather.6.cloned.1.call-update) | async-done | bytes 4194320 | tf_op jit(solution)/shard_map/all_gather | solution.py:172
  73.3 6.5 copy.125
  79.8 49.7 %all-gather.8.cloned.1.call-done = bf16[4096,512]{1,0:T(8,128)(2,1)} async-done(((bf16[256,512]{1,0:T(8,128)(2,1)}), bf16[4096,512]{1,0:T(8,128)(2,1)}) %all-gather.8.cloned.1.call-update) | async-done | bytes 4194320 | tf_op jit(solution)/shard_map/all_gather | solution.py:171
  129.5 6.4 copy.126
  135.9 91.9 %while.57 = (s32[]{:T(128)}, f32[256,512]{0,1:T(8,128)S(1)}, bf16[4096,512]{0,1:T(8,128)(2,1)}, bf16[4096,512]{0,1:T(8,128)(2,1)}, bf16[256,4,128]{2,0,1:T(8,128...) while((s32[]{:T(128)}, f32[256,512]{0,1:T(8,128)S(1)}, ...), condition=%wide.region_6.7_spmd.clone, body=%wide.region_4.6_spmd.clone.sunk | while | flops 293648384 | bytes 9478953 | solution.py:130
  143.0 4.2 fusion.197
  166.0 4.2 fusion.197
  189.0 4.2 fusion.197
  200.5 4.2 fusion.197
  235.0 23.9 %all_gather.27 = bf16[4096,32]{0,1:T(8,128)(2,1)} all-gather(bf16[256,32]{0,1:T(8,128)(2,1)S(1)} %copy-done.20), channel_id=1, replica_groups=mesh['dp'=8,'ctx'=16] {'ctx'}, dimensions={0}, use_global_device_ids=true | all-gather | bytes 278528 | tf_op jit(solution)/shard_map/all_gather | solution.py:256
  259.9 145.2 %while.58 = (s32[]{:T(128)}, f32[256,512]{0,1:T(8,128)}, f32[12,4]{0,1:T(4,128)S(1)}, bf16[4096,512]{0,1:T(8,128)(2,1)}, bf16[4096,512]{0,1:T(8,128)(2,1)}, /*in...) while((s32[]{:T(128)}, f32[256,512]{0,1:T(8,128)}, ...), condition=%wide.region_16.17_spmd.clone, body=%wide.region_14.16_spmd.clone.sunk | while | flops 511621216 | bytes 22851796 | solution.py:130
  271.8 6.1 fusion.210
  290.0 6.1 fusion.210
  308.2 6.1 fusion.210
  326.3 6.1 fusion.210
  344.5 6.1 fusion.210
  362.6 6.1 fusion.210
  380.8 6.1 fusion.210
  399.0 6.1 fusion.210
  406.5 84.3 %psum.7 = f32[12,4]{0,1:T(4,128)} all-reduce(f32[12,4]{0,1:T(4,128)S(1)} %get-tuple-element.1141), channel_id=1, replica_groups=mesh['dp'=8,'ctx'=16] {'dp','ctx'}, use_global_device_ids=true, to_apply=%region_20.21 | all-reduce | flops 48 | bytes 384 | tf_op jit(solution)/shard_map/psum | solution.py:291
  495.2 174.8 %while.59 = (s32[]{:T(128)}, f32[256,512]{0,1:T(8,128)S(1)}, f32[256,512]{0,1:T(8,128)S(1)}, bf16[4096,512]{1,0:T(8,128)(2,1)}, bf16[4096,512]{1,0:T(8,128)(2,1)...) while((s32[]{:T(128)}, f32[256,512]{0,1:T(8,128)S(1)}, ...), condition=%wide.region_13.14_spmd.clone.clone.clone, body=%wide.region_11.13_spmd.clone.clone.clone.sunk | while | flops 567580160 | bytes 27059616 | solution.py:130
  499.7 4.6 select_add_fusion.2
  521.6 4.6 select_add_fusion.2
  543.4 4.6 select_add_fusion.2
  565.3 4.6 select_add_fusion.2
  587.2 4.6 select_add_fusion.2
  609.0 4.6 select_add_fusion.2
  630.9 4.6 select_add_fusion.2
  652.7 4.6 select_add_fusion.2
  671.6 6.0 fusion.135
  (480 shorter events, 332.5 us)
Async XLA Ops:
  7.2 221.2 %copy-start = (bf16[512,1024]{1,0:T(8,128)(2,1)S(1)}, bf16[512,1024]{1,0:T(8,128)(2,1)}, u32[]{:S(2)}) copy-start(bf16[512,1024]{1,0:T(8,128)(2,1)} %param.17) | copy-start | bytes 3145732
  7.2 66.1 %all-gather.6.cloned.1.call-start = ((), (), s32[]{:S(2)}) async-start(), calls=%async_computation | async-start | bytes 4456448 | tf_op jit(solution)/shard_map/all_gather | solution.py:172
  8.5 6.4 copy-start.21
  9.8 5.1 copy-start.23
  14.9 3.9 copy-start.26
  15.0 4.9 copy-start.25
  15.0 5.0 copy-start.16
  17.1 112.4 %all-gather.8.cloned.1.call-start = ((), (), s32[]{:S(2)}) async-start(), calls=%async_computation.1 | async-start | bytes 4456448 | tf_op jit(solution)/shard_map/all_gather | solution.py:171
  17.9 475.1 %all-reduce.3.cloned.1.call-start = ((), (), s32[]{:S(2)}) async-start(), calls=%async_computation.4 | async-start | bytes 4194304
  19.1 60.6 %copy-start.19 = (bf16[256,32]{0,1:T(8,128)(2,1)}, bf16[256,32]{0,1:T(8,128)(2,1)S(1)}, u32[]{:S(2)}) copy-start(bf16[256,32]{0,1:T(8,128)(2,1)S(1)} %convolution_convert_fusion) | copy-start | bytes 49156
  232.5 27.4 %copy-start.9 = (bf16[256,512]{1,0:T(8,128)(2,1)}, bf16[256,512]{1,0:T(8,128)(2,1)S(1)}, u32[]{:S(2)}) copy-start(bf16[256,512]{1,0:T(8,128)(2,1)S(1)} %get-tuple-element.1728) | copy-start | bytes 786436
  232.5 26.4 %copy-start.13 = (bf16[32,4,8,128]{3,2,1,0:T(8,128)(2,1)S(1)}, bf16[32,4,8,128]{3,2,1,0:T(8,128)(2,1)}, u32[]{:S(2)}) copy-start(bf16[32,4,8,128]{3,2,1,0:T(8,128)(2,1)} %get-tuple-element.1731) | copy-start | bytes 786436
  232.5 26.4 %copy-start.14 = (bf16[32,4,8,128]{3,2,1,0:T(8,128)(2,1)S(1)}, bf16[32,4,8,128]{3,2,1,0:T(8,128)(2,1)}, u32[]{:S(2)}) copy-start(bf16[32,4,8,128]{3,2,1,0:T(8,128)(2,1)} %get-tuple-element.1733) | copy-start | bytes 786436
  234.3 260.0 %all-gather.10.cloned.1.call-start = ((), (), s32[]{:S(2)}) async-start(), calls=%async_computation.2 | async-start | bytes 4456448 | tf_op jit(solution)/shard_map/all_gather | solution.py:253
  234.9 260.3 %all-gather.12.cloned.1.call-start = ((), (), s32[]{:S(2)}) async-start(), calls=%async_computation.3 | async-start | bytes 4456448 | tf_op jit(solution)/shard_map/all_gather | solution.py:254
  405.1 86.6 %copy-start.5 = (bf16[256,1024]{1,0:T(8,128)(2,1)S(1)}, bf16[256,1024]{1,0:T(8,128)(2,1)}, u32[]{:S(2)}) copy-start(bf16[256,1024]{1,0:T(8,128)(2,1)} %param.14) | copy-start | bytes 1572868
  405.1 86.6 %copy-start.11 = (bf16[256,512]{1,0:T(8,128)(2,1)S(1)}, bf16[256,512]{1,0:T(8,128)(2,1)}, u32[]{:S(2)}) copy-start(bf16[256,512]{1,0:T(8,128)(2,1)} %copy-done.10) | copy-start | bytes 786436
  405.1 90.1 %copy-start.1 = (f32[256,512]{0,1:T(8,128)S(1)}, f32[256,512]{0,1:T(8,128)}, u32[]{:S(2)}) copy-start(f32[256,512]{0,1:T(8,128)} %custom-call.1) | copy-start | bytes 1572868
  405.1 90.1 %copy-start.2 = (f32[256,512]{0,1:T(8,128)S(1)}, f32[256,512]{0,1:T(8,128)}, u32[]{:S(2)}) copy-start(f32[256,512]{0,1:T(8,128)} %custom-call.2) | copy-start | bytes 1572868
  504.4 4.2 copy-start.18
  508.6 3.8 copy-start.3
  526.2 4.2 copy-start.18
  530.4 3.8 copy-start.3
  548.1 4.2 copy-start.18
  569.9 4.2 copy-start.18
  591.8 4.2 copy-start.18
  596.0 3.8 copy-start.3
  613.7 4.2 copy-start.18
  617.8 3.8 copy-start.3
  635.5 4.2 copy-start.18
  657.4 4.2 copy-start.18
  671.6 6.0 copy-start.8
  (29 other events, 72.3 us)
Sparse Core Ops, SparseCore 0:
  17.2 55.9 all-gather.5
  76.3 53.1 all-gather.7
  234.4 149.1 all-reduce.2
  385.9 53.2 all-gather.9
  441.6 53.6 all-gather.11
where the time goes:
time: 693 us; the launch traced here: 685 us
  matrix products  267 us (39%)
  blocking collectives  133 us (19%)
  other arithmetic  96.9 us (14%)
  local copies, waits for them, and re-layouts  93.3 us (13%)
  waiting for transfers between devices  80.1 us (12%)
  between operations  14.2 us (2%)
    psum x1, blocking collectives, on_device(): rab_grad = lax.psum(rab_sum, ('dp', 'ctx'))  84.3 us
    dot_general x16, matrix products, pair_scores(): jnp.einsum('qhd,khd->hqk', query_heads, key_heads, preferred_element_type...  58.5 us
    eq x24, other arithmetic, pair_bias(): bucket_ids[None] == bucket_id  51.7 us
    all_gather x1, waiting for transfers between devices, on_device(): key_piece = lax.all_gather(kv_local[0], 'ctx', axis=0, tiled=True)  49.7 us
    dot_general x8, matrix products, pair_back(): jnp.einsum('hqk,qkb->bh', d_score, onehot, precision=lax.Precision.HIGHEST)  48.8 us
    dot_general x24, matrix products, pair_mask(): lax.dot_general(query_tiles, key_pick, (((1,), (1,)), ((), ())), preferre...  39.5 us
    dot_general x8, matrix products, pair_forward(): jnp.einsum('hqk,khd->qhd', weights, value_heads, preferred_element_type=j...  33.6 us
    dot_general x8, matrix products, pair_back(): jnp.einsum('hqk,qhd->khd', score_half, query_heads, preferred_element_typ...  30.5 us
  transfers between devices with their start and end apart: 5, of which 3 were waited for; matrix products, arithmetic and copies ran while one was open for 23% of the time, Pallas kernels for 0%

commit v1 on v0

v1 whole, which is shorter than its diff:
```python
import math

import jax
import jax.numpy as jnp
from jax import lax
from jax.experimental import pallas as pl
from jax.experimental.pallas import tpu as pltpu
from jax.sharding import PartitionSpec as P

f32 = jnp.float32
bf16 = jnp.bfloat16
i32 = jnp.int32
T = 128
EPS = 1e-05
HEADS = 4
BUCKETS = 12
DEVS = 16
TILES = 32
QT = 8
SCALE = 1.0 / math.sqrt(128.0)
LIST = 160
UNROLL = 2
VMEM = pl.BlockSpec(memory_space=pltpu.VMEM)
SMEM = pl.BlockSpec(memory_space=pltpu.SMEM)
NT_DIMS = (((1,), (1,)), ((), ()))
TN_DIMS = (((0,), (0,)), ((), ()))


def params(mib=56):
    return pltpu.CompilerParams(vmem_limit_bytes=mib * 1024 * 1024)


def cost(flops, size):
    return pl.CostEstimate(flops=int(flops), bytes_accessed=int(size), transcendentals=0)


def sds(shape, dtype):
    return jax.ShapeDtypeStruct(shape, dtype)


def norm_rows(values):
    centre = jnp.mean(values, axis=-1, keepdims=True)
    shifted = values - centre
    spread = jnp.mean(shifted * shifted, axis=-1, keepdims=True)
    inverse = lax.rsqrt(spread + EPS)
    return shifted * inverse, inverse


def norm_back(upstream, normed, inverse):
    first = jnp.mean(upstream, axis=-1, keepdims=True)
    second = jnp.mean(upstream * normed, axis=-1, keepdims=True)
    return inverse * (upstream - first - normed * second)


def project_kernel(ids, tokens, w_gate, w_value, w_query, w_key, gate, slope, *rest):
    outs, normed = rest[:8], rest[8]
    step = pl.program_id(0)

    @pl.when(step == 0)
    def _():
        normed[...] = norm_rows(tokens[...].astype(f32))[0].astype(bf16)

    weights = jnp.concatenate([w_gate[...], w_value[...], w_query[...], w_key[...]], axis=1)
    pre = jnp.dot(normed[...], weights, preferred_element_type=f32)
    sig = 0.5 * jnp.tanh(0.5 * pre) + 0.5
    act = (pre * sig).astype(bf16)
    slopes = (sig * (1.0 + pre * (1.0 - sig))).astype(bf16)
    for kind in range(4):
        slope[kind, 0] = slopes[:, kind * T : (kind + 1) * T]
    gate[0] = act[:, :T]
    value, query, key = act[:, T : 2 * T], act[:, 2 * T : 3 * T], act[:, 3 * T :]
    for which in range(4):

        @pl.when(step == which)
        def _(which=which):
            outs[which][:, 0:T] = key
            outs[which][:, T : 2 * T] = value
            outs[which][:, 2 * T :] = query
            outs[4 + which][:, 0:T] = key
            outs[4 + which][:, T : 2 * T] = value


def project(ids, tokens, in_proj):
    def column(kind):
        return pl.BlockSpec((1024, T), lambda s, ids: (0, kind * HEADS + (ids[1] + s) % HEADS))

    whole = lambda shape: pl.BlockSpec(shape, lambda s, ids: (0,) * len(shape))
    head_of = lambda s, ids: (ids[1] + s) % HEADS
    return pl.pallas_call(
        project_kernel,
        grid_spec=pltpu.PrefetchScalarGridSpec(
            num_scalar_prefetch=1,
            grid=(4,),
            in_specs=[whole((256, 1024))] + [column(kind) for kind in range(4)],
            out_specs=[
                pl.BlockSpec((1, 256, T), lambda s, ids: (head_of(s, ids), 0, 0)),
                pl.BlockSpec((4, 1, 256, T), lambda s, ids: (0, head_of(s, ids), 0, 0)),
            ]
            + [whole((256, 384))] * 4
            + [whole((256, 256))] * 4,
            scratch_shapes=[pltpu.VMEM((256, 1024), bf16)],
        ),
        out_shape=[sds((4, 256, T), bf16), sds((4, 4, 256, T), bf16)]
        + [sds((256, 384), bf16)] * 4
        + [sds((256, 256), bf16)] * 4,
        compiler_params=params(),
        cost_estimate=cost(2 * 256 * 1024 * 2048, 7 << 20),
        name="project",
    )(ids, tokens, in_proj, in_proj, in_proj, in_proj)


def list_kernel(ids, meta, lengths, far, near, counts):
    y, z, core = ids[0], ids[1], ids[2]
    end0 = lengths[0]
    end1 = lengths[0] + lengths[1]

    def start_of(pos):
        return jnp.where(pos >= end1, end1, jnp.where(pos >= end0, end0, 0))

    def time_at(tile, lane):
        first = tile < DEVS
        dev = jnp.where(first, tile, 2 * DEVS - 1 - tile)
        return meta[dev * 384 + jnp.where(first, 0, T) + lane]

    def level(gap):
        total = jnp.int32(0)
        for j in range(1, BUCKETS):
            total = total + jnp.where(gap + 1 >= 2**j, 1, 0).astype(i32)
        return total

    counts[0] = 0
    counts[1] = 0

    def query_step(jj, _):
        dev = y * 8 + (jj // 2) * 2 + core
        half = jj % 2
        tile = jnp.where(half == 0, dev, 2 * DEVS - 1 - dev)
        low = start_of(tile * T)
        high = start_of(tile * T + T - 1)
        q_first = time_at(tile, 0)
        q_last = time_at(tile, T - 1)
        base = dev * 384 + 256 + half * TILES

        def key_step(k, _):
            row_tile = jnp.where(k < DEVS, 2 * k, 2 * (2 * DEVS - 1 - k) + 1)

            @pl.when(meta[base + row_tile] != 0)
            def _():
                bottom = level(jnp.maximum(q_first - time_at(k, T - 1), 0))
                top = level(q_last - time_at(k, 0))
                entry = jj + 16 * k
                plain = (k < tile) & (k * T >= high) & (top - bottom <= 2)

                @pl.when(plain)
                def _():
                    n = counts[0]
                    far[n] = entry + 1024 * bottom
                    counts[0] = n + 1

                @pl.when(jnp.logical_not(plain))
                def _():
                    n = counts[1]
                    near[n] = entry
                    counts[1] = n + 1

            return 0

        lax.fori_loop(low // T, tile + 1, key_step, 0)
        return 0

    lax.fori_loop(0, QT, query_step, 0)
    for index, ref in ((0, far), (1, near)):
        for pad in range(UNROLL - 1):
            ref[counts[index] + pad] = QT + 16 * TILES
        counts[index] = (counts[index] + UNROLL - 1) // UNROLL


def make_lists(ids, meta, lengths):
    return pl.pallas_call(
        list_kernel,
        in_specs=[SMEM] * 3,
        out_specs=[SMEM] * 3,
        out_shape=[sds((LIST,), i32), sds((LIST,), i32), sds((8,), i32)],
        cost_estimate=cost(1 << 20, 1 << 20),
        name="pair_lists",
    )(ids, meta, lengths)


def bias_far(gap, table, bottom):
    first = table[bottom]
    second = table[bottom + 1]
    third = table[bottom + 2]
    limit1 = table[16 + bottom + 1]
    limit2 = table[16 + bottom + 2]
    over1 = gap >= limit1
    over2 = gap >= limit2
    return jnp.where(over2, third, jnp.where(over1, second, first)), over1, over2


def bias_near(gap, table):
    bias = jnp.full(gap.shape, table[0], f32)
    for j in range(1, BUCKETS):
        bias = jnp.where(gap >= float(2**j - 1), table[j], bias)
    return bias


def keep_near(ids, start, jj, k):
    dev = ids[0] * 8 + (jj // 2) * 2 + ids[2]
    tile = jnp.where(jj % 2 == 0, dev, 2 * DEVS - 1 - dev)
    row = lax.broadcasted_iota(i32, (T, T), 0)
    col = lax.broadcasted_iota(i32, (T, T), 1)
    later = (col - row) <= (tile - k) * T
    return later & ((col + k * T) >= start)


def forward_kernel(ids, table, far, near, counts, lengths, times, *refs):
    ins, outs = refs[:16], refs[16:]
    o_refs, (keys, values, queries, tq, tk, start, acc) = outs[:4], outs[4:]
    y, z, core = ids[0], ids[1], ids[2]
    end0 = lengths[0]
    end1 = lengths[0] + lengths[1]
    for group in range(4):
        for t in range(4):
            ref = ins[group * 4 + t]
            zz = (z + 4 - t) % 4
            dev = (y if group < 2 else 1 - y) * 8 + zz * 2 + (core if group % 2 == 0 else 1 - core)
            keys[dev] = ref[0:T, 0:T]
            values[dev] = ref[0:T, T : 2 * T]
            keys[2 * DEVS - 1 - dev] = ref[T:, 0:T]
            values[2 * DEVS - 1 - dev] = ref[T:, T : 2 * T]
            if group == 0:
                queries[2 * zz] = ref[0:T, 2 * T :]
                queries[2 * zz + 1] = ref[T:, 2 * T :]
    keys[TILES] = jnp.zeros((T, T), bf16)
    values[TILES] = jnp.zeros((T, T), bf16)
    queries[QT] = jnp.zeros((T, T), bf16)
    for dev in range(DEVS):
        tk[dev] = jnp.broadcast_to(times[dev : dev + 1, 0:T].astype(f32), (8, T))
        tk[2 * DEVS - 1 - dev] = jnp.broadcast_to(times[dev : dev + 1, T : 2 * T].astype(f32), (8, T))
    tk[TILES] = jnp.zeros((8, T), f32)
    tq[QT] = jnp.zeros((T, T), f32)
    start[QT] = jnp.zeros((T, T), i32)
    rows = lax.broadcasted_iota(i32, (T, T), 0)
    for jj in range(QT):
        dev = y * 8 + (jj // 2) * 2 + core
        tile = dev if jj % 2 == 0 else 2 * DEVS - 1 - dev
        tq[jj] = jnp.transpose(jnp.broadcast_to(tk[tile][0:1, :], (T, T)))
        pos = rows + tile * T
        start[jj] = jnp.where(pos >= end1, end1, jnp.where(pos >= end0, end0, 0))
    acc[...] = jnp.zeros(acc.shape, f32)

    def far_step(i, _):
        for u in range(UNROLL):
            entry = far[i * UNROLL + u]
            jj = entry % 16
            k = (entry // 16) % 64
            dots = lax.dot_general(queries[jj], keys[k], NT_DIMS, preferred_element_type=f32)
            gap = tq[jj] - tk[k][0:1, :]
            bias, _, _ = bias_far(gap, table, entry // 1024)
            half = dots * (0.5 * SCALE) + bias
            weight = (half * jnp.tanh(half) + half).astype(bf16)
            acc[jj] += jnp.dot(weight, values[k], preferred_element_type=f32)
        return 0

    def near_step(i, _):
        for u in range(UNROLL):
            entry = near[i * UNROLL + u]
            jj = entry % 16
            k = entry // 16
            dots = lax.dot_general(queries[jj], keys[k], NT_DIMS, preferred_element_type=f32)
            gap = tq[jj] - tk[k][0:1, :]
            half = dots * (0.5 * SCALE) + bias_near(gap, table)
            weight = half * jnp.tanh(half) + half
            weight = jnp.where(keep_near(ids, start[jj], jj, k), weight, 0.0).astype(bf16)
            acc[jj] += jnp.dot(weight, values[k], preferred_element_type=f32)
        return 0

    lax.fori_loop(0, counts[0], far_step, 0)
    lax.fori_loop(0, counts[1], near_step, 0)
    for s in range(4):
        zz = (z + s) % 4
        o_refs[s][0:T] = acc[2 * zz]
        o_refs[s][T:] = acc[2 * zz + 1]


def attend(ids, table, far, near, counts, lengths, times, parts):
    return pl.pallas_call(
        forward_kernel,
        in_specs=[SMEM] * 6 + [VMEM] * 17,
        out_specs=[VMEM] * 10,
        out_shape=[sds((256, T), f32)] * 4
        + [
            sds((TILES + 1, T, T), bf16),
            sds((TILES + 1, T, T), bf16),
            sds((QT + 1, T, T), bf16),
            sds((QT + 1, T, T), f32),
            sds((TILES + 1, 8, T), f32),
            sds((QT + 1, T, T), i32),
        ],
        scratch_shapes=[pltpu.VMEM((QT + 1, T, T), f32)],
        compiler_params=params(),
        cost_estimate=cost(1e9 * 6, 6 << 20),
        name="attend",
    )(ids, table, far, near, counts, lengths, times, *parts)


def middle_kernel(ids, cot, out_proj, gate, slope, *refs):
    ins, (mixed, grad_gate), g_refs = refs[:4], refs[4:6], refs[6:10]
    att, back = refs[10], refs[11]
    z = ids[1]
    for t in range(4):
        att[(z + 4 - t) % 4] = ins[t][...]
    whole = jnp.concatenate([att[h] for h in range(4)], axis=1)
    normed, inverse = norm_rows(whole)
    gates = jnp.concatenate([gate[h] for h in range(4)], axis=1).astype(f32)
    mixed[...] = (normed * gates).astype(bf16)
    grad_mix = lax.dot_general(cot[...], out_proj[...], NT_DIMS, preferred_element_type=f32)
    gate_slope = jnp.concatenate([slope[h] for h in range(4)], axis=1).astype(f32)
    grad_gate[...] = (grad_mix * normed * gate_slope).astype(bf16)
    grad = norm_back(grad_mix * gates, normed, inverse).astype(bf16)
    for h in range(4):
        back[h] = grad[:, h * T : (h + 1) * T]
    for s in range(4):
        g_refs[s][...] = back[(z + s) % 4]


def middle(ids, cot, out_proj, gate, slope, parts):
    return pl.pallas_call(
        middle_kernel,
        grid=(1,),
        in_specs=[
            SMEM,
            pl.BlockSpec((256, 1024), lambda i: (0, 0)),
            pl.BlockSpec((512, 1024), lambda i: (0, 0)),
            pl.BlockSpec((4, 256, T), lambda i: (0, 0, 0)),
            pl.BlockSpec((None, 4, 256, T), lambda i: (0, 0, 0, 0)),
        ]
        + [pl.BlockSpec((256, T), lambda i: (0, 0))] * 4,
        out_specs=[pl.BlockSpec((256, 512), lambda i: (0, 0))] * 2
        + [pl.BlockSpec((256, T), lambda i: (0, 0))] * 4,
        out_shape=[sds((256, 512), bf16)] * 2 + [sds((256, T), bf16)] * 4,
        scratch_shapes=[pltpu.VMEM((4, 256, T), f32), pltpu.VMEM((4, 256, T), bf16)],
        compiler_params=params(),
        cost_estimate=cost(2 * 256 * 512 * 1024, 4 << 20),
        name="middle",
    )(ids, cot, out_proj, gate, slope, *parts)


def output_kernel(ids, tokens, cot, out_proj, mixed, output, mine, theirs):
    y, z, core, dp = ids[0], ids[1], ids[2], ids[3]
    output[...] = (
        tokens[...].astype(f32) + jnp.dot(mixed[...], out_proj[...], preferred_element_type=f32)
    ).astype(bf16)
    r = lax.broadcasted_iota(i32, (512, 512), 1)
    c = lax.broadcasted_iota(i32, (512, 512), 0)
    r_core = (r // 256) ^ core
    r_z = (((r // 64) % 4) + z) % 4
    r_y = ((r // 32) % 2) ^ y
    r_dp = ((r // 4) % 8) ^ dp
    source = r_dp * 64 + r_y * 32 + r_z * 8 + r_core * 4 + r % 4
    pick = jnp.where(c == source, 1.0, 0.0).astype(bf16)
    moved = jnp.dot(mixed[...], pick, preferred_element_type=f32).astype(bf16)
    part = lax.dot_general(moved, cot[...], TN_DIMS, preferred_element_type=f32)
    mine[...] = part[:256]
    theirs[...] = part[256:].astype(bf16)


def finish_output(ids, tokens, cot, out_proj, mixed):
    return pl.pallas_call(
        output_kernel,
        in_specs=[SMEM] + [VMEM] * 4,
        out_specs=[VMEM] * 3,
        out_shape=[sds((256, 1024), bf16), sds((256, 1024), f32), sds((256, 1024), bf16)],
        compiler_params=params(),
        cost_estimate=cost(6 * 256 * 512 * 1024, 5 << 20),
        name="finish_output",
    )(ids, tokens, cot, out_proj, mixed)


def backward_kernel(ids, table, far, near, counts, keys, values, queries, tq, tk, start, *refs):
    ins, outs = refs[:4], refs[4:10]
    mine_s, mine_o, theirs_s, theirs_o, dq_out, rab_out = outs
    grads, grads_t, queries_t, dq, dkt, dvt, rab = refs[10:]
    y, z, core = ids[0], ids[1], ids[2]
    for t in range(4):
        zz = (z + 4 - t) % 4
        for half in range(2):
            block = ins[t][half * T : (half + 1) * T, :].astype(f32) * 0.5
            grads[2 * zz + half] = block.astype(bf16)
            grads_t[2 * zz + half] = jnp.transpose(block).astype(bf16)
    for jj in range(QT):
        queries_t[jj] = jnp.transpose(queries[jj].astype(f32)).astype(bf16)
    grads[QT] = jnp.zeros((T, T), bf16)
    grads_t[QT] = jnp.zeros((T, T), bf16)
    queries_t[QT] = jnp.zeros((T, T), bf16)
    dq[...] = jnp.zeros(dq.shape, f32)
    dkt[...] = jnp.zeros(dkt.shape, f32)
    dvt[...] = jnp.zeros(dvt.shape, f32)
    rab[...] = jnp.zeros(rab.shape, f32)

    def fold(values_):
        return jnp.sum(values_.reshape(T // 8, 8, T), axis=0)

    def pair(jj, k, half, keep):
        t = jnp.tanh(half)
        weight = half * t + half
        d_weight = lax.dot_general(grads[jj], values[k], NT_DIMS, preferred_element_type=f32)
        d_score = d_weight * ((1.0 + t) * (1.0 + half * (1.0 - t)))
        if keep is not None:
            weight = jnp.where(keep, weight, 0.0)
            d_score = jnp.where(keep, d_score, 0.0)
        score_half = d_score.astype(bf16)
        dq[jj] += jnp.dot(score_half, keys[k], preferred_element_type=f32)
        dkt[k] += jnp.dot(queries_t[jj], score_half, preferred_element_type=f32)
        dvt[k] += jnp.dot(grads_t[jj], weight.astype(bf16), preferred_element_type=f32)
        return d_score

    def far_step(i, _):
        for u in range(UNROLL):
            entry = far[i * UNROLL + u]
            jj = entry % 16
            k = (entry // 16) % 64
            bottom = entry // 1024
            dots = lax.dot_general(queries[jj], keys[k], NT_DIMS, preferred_element_type=f32)
            gap = tq[jj] - tk[k][0:1, :]
            bias, over1, over2 = bias_far(gap, table, bottom)
            d_score = pair(jj, k, dots * (0.5 * SCALE) + bias, None)
            sum0 = fold(d_score)
            sum1 = fold(jnp.where(over1, d_score, 0.0))
            sum2 = fold(jnp.where(over2, d_score, 0.0))
            rab[bottom] += sum0 - sum1
            rab[bottom + 1] += sum1 - sum2
            rab[bottom + 2] += sum2
        return 0

    def near_step(i, _):
        for u in range(UNROLL):
            entry = near[i * UNROLL + u]
            jj = entry % 16
            k = entry // 16
            dots = lax.dot_general(queries[jj], keys[k], NT_DIMS, preferred_element_type=f32)
            gap = tq[jj] - tk[k][0:1, :]
            half = dots * (0.5 * SCALE) + bias_near(gap, table)
            d_score = pair(jj, k, half, keep_near(ids, start[jj], jj, k))
            last = fold(d_score)
            for j in range(1, BUCKETS):
                now = fold(jnp.where(gap >= float(2**j - 1), d_score, 0.0))
                rab[j - 1] += last - now
                last = now
            rab[BUCKETS - 1] += last
        return 0

    lax.fori_loop(0, counts[0], far_step, 0)
    lax.fori_loop(0, counts[1], near_step, 0)
    for other in range(2):
        for s in range(4):
            base = (y if other == 0 else 1 - y) * 8 + ((z + s) % 4) * 2
            for side in range(2):
                dev = base + (core if side == 0 else 1 - core)
                ref = ((mine_s, theirs_s), (mine_o, theirs_o))[other][side]
                for half in range(2):
                    tile = dev if half == 0 else 2 * DEVS - 1 - dev
                    ref[s, 0:T, half * T : (half + 1) * T] = (dkt[tile] * SCALE).astype(bf16)
                    ref[s, T:, half * T : (half + 1) * T] = (dvt[tile] * 2.0).astype(bf16)
    for s in range(4):
        zz = (z + s) % 4
        for half in range(2):
            dq_out[s, :, half * T : (half + 1) * T] = (dq[2 * zz + half] * SCALE).astype(bf16)
    for b in range(16):
        if b < BUCKETS:
            rab_out[b : b + 1, :] = jnp.sum(rab[b], axis=0, keepdims=True)
        else:
            rab_out[b : b + 1, :] = jnp.zeros((1, T), f32)


def attend_back(ids, table, far, near, counts, saved, parts):
    return pl.pallas_call(
        backward_kernel,
        in_specs=[SMEM] * 5 + [VMEM] * 10,
        out_specs=[VMEM] * 6,
        out_shape=[sds((4, 256, 256), bf16)] * 4 + [sds((4, T, 256), bf16), sds((16, T), f32)],
        scratch_shapes=[
            pltpu.VMEM((QT + 1, T, T), bf16),
            pltpu.VMEM((QT + 1, T, T), bf16),
            pltpu.VMEM((QT + 1, T, T), bf16),
            pltpu.VMEM((QT + 1, T, T), f32),
            pltpu.VMEM((TILES + 1, T, T), f32),
            pltpu.VMEM((TILES + 1, T, T), f32),
            pltpu.VMEM((16, 8, T), f32),
        ],
        compiler_params=params(),
        cost_estimate=cost(1e9 * 12, 8 << 20),
        name="attend_back",
    )(ids, table, far, near, counts, *saved, *parts)


def combine_kernel(mine_s, mine_o, got_s, got_o, dq, *outs):
    for s in range(4):
        outs[s][0:256, :] = (mine_s[s].astype(f32) + got_s[s].astype(f32)).astype(bf16)
        outs[s][256:, :] = dq[s]
        outs[4 + s][...] = (mine_o[s].astype(f32) + got_o[s].astype(f32)).astype(bf16)


def combine(mine_s, mine_o, got_s, got_o, dq):
    return pl.pallas_call(
        combine_kernel,
        in_specs=[VMEM] * 5,
        out_specs=[VMEM] * 8,
        out_shape=[sds((384, 256), bf16)] * 4 + [sds((256, 256), bf16)] * 4,
        compiler_params=params(),
        cost_estimate=cost(1 << 20, 5 << 20),
        name="combine",
    )(mine_s, mine_o, got_s, got_o, dq)


def final_kernel(ids, tokens, cot, in_proj, slope, grad_gate, *refs):
    same, other, grad_in, grad_pre, grad_normed = refs[:4], refs[4:8], refs[8], refs[9], refs[10]
    step = pl.program_id(0)
    z = ids[1]

    @pl.when(step == 0)
    def _():
        grad_pre[:, 0:512] = grad_gate[...]
        for t in range(4):
            head = (z + 4 - t) % 4
            column = lambda kind: pl.ds(pl.multiple_of(kind * 512 + head * T, T), T)
            total = same[t][0:256, :].astype(f32) + other[t][...].astype(f32)
            for half in range(2):
                rows = slice(half * T, (half + 1) * T)
                key = jnp.transpose(total[0:T, rows])
                value = jnp.transpose(total[T:, rows])
                query = same[t][256:, rows].astype(f32)
                for kind, part in ((1, value), (2, query), (3, key)):
                    grad_pre[rows, column(kind)] = (
                        part * slope[kind, head, rows, :].astype(f32)
                    ).astype(bf16)

    grad_normed[step] = lax.dot_general(
        grad_pre[...], in_proj[...], NT_DIMS, preferred_element_type=f32
    )

    @pl.when(step == 3)
    def _():
        normed, inverse = norm_rows(tokens[...].astype(f32))
        upstream = jnp.concatenate([grad_normed[i] for i in range(4)], axis=1)
        grad_in[...] = (cot[...].astype(f32) + norm_back(upstream, normed, inverse)).astype(bf16)


def finish_grad(ids, tokens, cot, in_proj, slope, grad_gate, same, other):
    whole = lambda shape: pl.BlockSpec(shape, lambda s: (0,) * len(shape))
    return pl.pallas_call(
        final_kernel,
        grid=(4,),
        in_specs=[
            SMEM,
            whole((256, 1024)),
            whole((256, 1024)),
            pl.BlockSpec((256, 2048), lambda s: (s, 0)),
            whole((4, 4, 256, T)),
            whole((256, 512)),
        ]
        + [whole((384, 256))] * 4
        + [whole((256, 256))] * 4,
        out_specs=whole((256, 1024)),
        out_shape=sds((256, 1024), bf16),
        scratch_shapes=[pltpu.VMEM((256, 2048), bf16), pltpu.VMEM((4, 256, 256), f32)],
        compiler_params=params(),
        cost_estimate=cost(2 * 256 * 1024 * 2048, 8 << 20),
        name="finish_grad",
    )(ids, tokens, cot, in_proj, slope, grad_gate, *same, *other)


def move(y_xor, z_shift, core_xor):
    pairs = []
    for dev in range(DEVS):
        y, z, core = dev // 8, (dev // 2) % 4, dev % 2
        target = (y ^ y_xor) * 8 + ((z + z_shift) % 4) * 2 + (core ^ core_xor)
        pairs.append((dev, target))
    return pairs


def send(x, y_xor, z_shift, core_xor):
    return lax.ppermute(x, "ctx", move(y_xor, z_shift, core_xor))


def send_dp(x, mask):
    return lax.ppermute(x, "dp", [(dev, dev ^ mask) for dev in range(8)])


def gather_meta(payload, y, z, core):
    other = send(payload, 0, 0, 1)
    pair = jnp.where(core == 0, jnp.stack([payload, other]), jnp.stack([other, payload]))
    line = [pair] + [send(pair, 0, s, 0) for s in (1, 2, 3)]
    column = jnp.zeros((4, 2, 384), i32)
    index = jnp.arange(4, dtype=i32)[:, None, None]
    for t in range(4):
        column = column + jnp.where(index == (z + 4 - t) % 4, line[t][None], 0)
    column = column.reshape(8, 384)
    far_side = send(column, 1, 0, 0)
    return jnp.where(
        y == 0,
        jnp.concatenate([column, far_side], axis=0),
        jnp.concatenate([far_side, column], axis=0),
    )


def sum_rab(part, z):
    part = part + send(part, 0, 0, 1)
    terms = [part] + [send_dp(part, mask) for mask in range(1, 8)]
    while len(terms) > 1:
        terms = [terms[i] + terms[i + 1] for i in range(0, len(terms), 2)]
    part = terms[0]
    part = part + send(part, 1, 0, 0)
    line = [part] + [send(part, 0, s, 0) for s in (1, 2, 3)]
    sums = jnp.sum(jnp.stack(line), axis=-1)[:, :BUCKETS]
    slot = (z + 4 - jnp.arange(4, dtype=i32)) % 4
    pick = slot[None, :, None] == jnp.arange(4, dtype=i32)[:, None, None]
    return jnp.sum(jnp.where(pick, sums[None], 0.0), axis=1).T


def sum_proj(mine, theirs):
    total = mine + send(theirs, 0, 0, 1).astype(f32)
    pieces = total.reshape(4, 64, 1024)
    total = pieces[0]
    for s in (1, 2, 3):
        total = total + send(pieces[s].astype(bf16), 0, s, 0).astype(f32)
    pieces = total.reshape(2, 32, 1024)
    total = pieces[0] + send(pieces[1].astype(bf16), 1, 0, 0).astype(f32)
    pieces = total.reshape(8, 4, 1024)
    total = pieces[0]
    for mask in range(1, 8):
        total = total + send_dp(pieces[mask], mask)
    return total


def on_device(tokens, cotangent, in_proj, out_proj, rab_time, seq_lengths, block_mask, time_bucket):
    ctx = lax.axis_index("ctx")
    dp = lax.axis_index("dp")
    y, z, core = ctx // 8, (ctx // 2) % 4, ctx % 2
    ids = jnp.stack([y, z, core, dp]).astype(i32)
    lengths = seq_lengths.reshape(3)
    payload = jnp.concatenate([time_bucket, block_mask.reshape(64), jnp.zeros((64,), i32)])
    meta = gather_meta(payload, y, z, core)
    limits = [2.0**j - 1.0 for j in range(BUCKETS)] + [1e9] * 4
    head_bias = lax.dynamic_slice_in_dim(rab_time, z, 1, 1).reshape(BUCKETS) * 0.5
    table = jnp.concatenate([head_bias, jnp.zeros((4,), f32), jnp.array(limits, f32)])
    far, near, counts = make_lists(ids, meta.reshape(-1), lengths)

    made = project(ids, tokens, in_proj)
    gate, slope, full, pairs = made[0], made[1], made[2:6], made[6:10]
    own = [full[0]] + [send(full[s], 0, s, 0) for s in (1, 2, 3)]
    across = [send(pairs[s], 1, s, 0) for s in range(4)]
    own_twin = [send(part, 0, 0, 1) for part in own]
    across_twin = [send(part, 0, 0, 1) for part in across]
    parts = own + own_twin + across + across_twin
    done = attend(ids, table, far, near, counts, lengths, meta[:, :256], parts)
    blocks, saved = done[:4], done[4:]

    heads = [blocks[0]] + [send(blocks[s], 0, s, 0) for s in (1, 2, 3)]
    between = middle(ids, cotangent, out_proj, gate, slope, heads)
    mixed, grad_gate, grads = between[0], between[1], between[2:]
    grads = [grads[0]] + [send(grads[s], 0, s, 0) for s in (1, 2, 3)]
    output, proj_mine, proj_theirs = finish_output(ids, tokens, cotangent, out_proj, mixed)
    proj_grad = sum_proj(proj_mine, proj_theirs)

    mine_s, mine_o, theirs_s, theirs_o, dq, rab = attend_back(
        ids, table, far, near, counts, saved, grads
    )
    got_o = send(theirs_o, 0, 0, 1)
    got_s = send(theirs_s, 0, 0, 1)
    messages = combine(mine_s, mine_o, got_s, got_o, dq)
    same = [messages[0]] + [send(messages[s], 0, s, 0) for s in (1, 2, 3)]
    other = [send(messages[4 + s], 1, s, 0) for s in range(4)]
    rab_grad = sum_rab(rab, z)
    grad_in = finish_grad(ids, tokens, cotangent, in_proj, slope, grad_gate, same, other)
    return output, grad_in, proj_grad, rab_grad


def solution(mesh):
    rows = P(("dp", "ctx"), None)
    placed = (rows, rows, P(), P(), P(), P("dp", None), P("dp", "ctx", None), P(("dp", "ctx")))
    return jax.shard_map(
        on_device,
        mesh=mesh,
        in_specs=placed,
        out_specs=(rows, rows, rows, P()),
        check_vma=False,
    )
```

time: 693 us -> 194 us (0.28)
  matrix products: 267 us -> 0 us
  blocking collectives: 133 us -> 0 us
  other arithmetic: 96.9 us -> 5.12 us
  local copies, waits for them, and re-layouts: 93.3 us -> 6.49 us
  starting transfers between devices: 0.2 us -> 78 us
  Pallas kernels: 0 us -> 68.5 us
  waiting for transfers between devices: 80.1 us -> 31.8 us
  between operations: 14.2 us -> 1.23 us
    dot_general x94 -> x0, matrix products: 267 us -> none  [the longest x16 58.5 us: pair_scores(): jnp.einsum('qhd,khd->hqk', query_heads, key_heads, preferred_element_type...]
    psum x1 -> x0, blocking collectives: 84.3 us -> none  [on_device(): rab_grad = lax.psum(rab_sum, ('dp', 'ctx'))]
    all_gather x4 -> x0, waiting for transfers between devices: 78.8 us -> none  [the longest x1 49.7 us: on_device(): key_piece = lax.all_gather(kv_local[0], 'ctx', axis=0, tiled=True)]
    ppermute x0 -> x59, starting transfers between devices: none -> 78 us  [the longest x45 58.2 us: send(): return lax.ppermute(x, 'ctx', move(y_xor, z_shift, core_xor))]
    pallas_call x0 -> x8, Pallas kernels: none -> 68.5 us  [the longest x1 21.8 us: attend_back(): pl.pallas_call(backward_kernel, in_specs=[SMEM] * 5 + [VMEM] * 10, out_sp...]
    dynamic_slice x72 -> x0, local copies, waits for them, and re-layouts: 66.3 us -> none  [the longest x16 17.1 us: key_step(): lax.dynamic_slice_in_dim(remote_grad, offset, span_rows, 0)]
    eq x24 -> x5, other arithmetic: 51.7 us -> 0.03 us  [the longest x4 0.02 us: gather_meta(): column = column + jnp.where(index == (z + 4 - t) % 4, line[t][None], 0)]
    all_gather x2 -> x0, blocking collectives: 48.3 us -> none  [the longest x1 24.4 us: on_device(): time_piece = lax.all_gather(kv_local[2], 'ctx', axis=0, tiled=True)]
  transfers between devices with their start and end apart: 5 -> 59, of which waited for: 3 -> 17; matrix products, arithmetic and copies ran while one was open for 23% -> 3% of each run, Pallas kernels for 0% -> 21%
where the time goes in v1:
time: 194 us; the launch traced here: 191 us
  starting transfers between devices  78 us (40%)
  Pallas kernels  68.5 us (35%)
  waiting for transfers between devices  31.8 us (16%)
  local copies, waits for them, and re-layouts  6.49 us (3%)
  other arithmetic  5.12 us (3%)
    ppermute x45, starting transfers between devices, send(): return lax.ppermute(x, 'ctx', move(y_xor, z_shift, core_xor))  58.2 us
    ppermute x45, waiting for transfers between devices, send(): return lax.ppermute(x, 'ctx', move(y_xor, z_shift, core_xor))  31.8 us
    pallas_call x1, Pallas kernels, attend_back(): pl.pallas_call(backward_kernel, in_specs=[SMEM] * 5 + [VMEM] * 10, out_sp...  21.8 us
    ppermute x14, starting transfers between devices, send_dp(): return lax.ppermute(x, 'dp', [(dev, dev ^ mask) for dev in range(8)])  19.8 us
    pallas_call x1, Pallas kernels, attend(): pl.pallas_call(forward_kernel, in_specs=[SMEM] * 6 + [VMEM] * 17, out_spe...  17.5 us
    pallas_call x1, Pallas kernels, project(): pl.pallas_call(project_kernel, grid_spec=pltpu.PrefetchScalarGridSpec(num...  7.21 us
    pallas_call x1, Pallas kernels, finish_grad(): pl.pallas_call(final_kernel, grid=(4,), in_specs=[SMEM, whole((256, 1024)...  6.98 us
    pallas_call x1, Pallas kernels, make_lists(): pl.pallas_call(list_kernel, in_specs=[SMEM] * 3, out_specs=[SMEM] * 3, ou...  5.41 us
  transfers between devices with their start and end apart: 59, of which 17 were waited for; matrix products, arithmetic and copies ran while one was open for 3% of the time, Pallas kernels for 21%

profile of v1, /device:TPU:24, one launch (start us, length us, event | category | flops | bytes accessed | tf_op | source)
XLA Modules:
  0.0 191.1 jit_solution(16389693747322939016)
XLA Ops:
  2.8 7.2 %project.1 = (bf16[4,256,128]{2,1,0:T(8,128)(2,1)}, bf16[4,4,256,128]{3,2,1,0:T(8,128)(2,1)}, bf16[256,384]{1,0:T(8,128)(2,1)}, bf16[256,384]{1,0:T(8,128)(2,1)}...) custom-call(s32[4]{0:T(128)} %pad_add_fusion.1.ids, ...), custom_call_target="tpu_custom_call" | custom-call | flops 1073741824 | bytes 7340032 | tf_op jit(solution)/shard_map/project/pallas_call | solution.py:89
  11.3 3.6 %collective-permute-start.13 = (bf16[256,256]{1,0:T(8,128)(2,1)}, bf16[256,256]{1,0:T(8,128)(2,1)S(1)}, u32[]{:S(2)}, u32[]{:S(2)}) collective-permute-start(bf16[256,256]{1,0:T(8,128)(2,1)} %get-tuple-element.60), channel_id=1, source_target_pairs={{0,10},{1,11},{2,12},{3,13},{4,14},{5,15},{6,8},{7,9},{8,2},{9,3},... | collective-permute-start | bytes 393224 | tf_op jit(solution)/shard_map/ppermute | solution.py:583
  16.4 2.7 %collective-permute-start.2 = (s32[2,384]{1,0:T(2,128)S(1)}, s32[2,384]{1,0:T(2,128)S(1)}, u32[]{:S(2)}, u32[]{:S(2)}) collective-permute-start(s32[2,384]{1,0:T(2,128)S(1)} %add_select_fusion.1), channel_id=1, source_target_pairs={{0,4},{1,5},{2,6},{3,7},{4,0},{5,1},{6,2},{7,3},{8,12},{9,13},{10,... | collective-permute-start | bytes 9224 | tf_op jit(solution)/shard_map/ppermute | solution.py:583
  20.8 2.2 %collective-permute-start.14 = (bf16[256,256]{1,0:T(8,128)(2,1)}, bf16[256,256]{1,0:T(8,128)(2,1)S(1)}, u32[]{:S(2)}, u32[]{:S(2)}) collective-permute-start(bf16[256,256]{1,0:T(8,128)(2,1)} %get-tuple-element.61), channel_id=1, source_target_pairs={{0,12},{1,13},{2,14},{3,15},{4,8},{5,9},{6,10},{7,11},{8,4},{9,5},... | collective-permute-start | bytes 393224 | tf_op jit(solution)/shard_map/ppermute | solution.py:583
  24.9 2.3 %collective-permute-start.4 = (s32[8,384]{1,0:T(8,128)S(1)}, s32[8,384]{1,0:T(8,128)S(1)}, u32[]{:S(2)}, u32[]{:S(2)}) collective-permute-start(s32[8,384]{1,0:T(8,128)S(1)} %select_add_fusion), channel_id=1, source_target_pairs={{0,8},{1,9},{2,10},{3,11},{4,12},{5,13},{6,14},{7,15},{8,0},{9,1},... | collective-permute-start | bytes 36872 | tf_op jit(solution)/shard_map/ppermute | solution.py:583
  27.2 2.9 %collective-permute-done.4 = s32[8,384]{1,0:T(8,128)S(1)} collective-permute-done((s32[8,384]{1,0:T(8,128)S(1)}, s32[8,384]{1,0:T(8,128)S(1)}, u32[]{:S(2)}, u32[]{:S(2)}) %collective-permute-start.4) | collective-permute-done | bytes 12320 | tf_op jit(solution)/shard_map/ppermute | solution.py:583
  30.1 3.3 %collective-permute-start.15 = (bf16[256,256]{1,0:T(8,128)(2,1)}, bf16[256,256]{1,0:T(8,128)(2,1)S(1)}, u32[]{:S(2)}, u32[]{:S(2)}) collective-permute-start(bf16[256,256]{1,0:T(8,128)(2,1)} %get-tuple-element.62), channel_id=1, source_target_pairs={{0,14},{1,15},{2,8},{3,9},{4,10},{5,11},{6,12},{7,13},{8,6},{9,7},... | collective-permute-start | bytes 393224 | tf_op jit(solution)/shard_map/ppermute | solution.py:583
  34.3 2.2 %collective-permute-start.7 = (bf16[256,384]{1,0:T(8,128)(2,1)}, bf16[256,384]{1,0:T(8,128)(2,1)S(1)}, u32[]{:S(2)}, u32[]{:S(2)}) collective-permute-start(bf16[256,384]{1,0:T(8,128)(2,1)} %get-tuple-element.58), channel_id=1, source_target_pairs={{0,6},{1,7},{2,0},{3,1},{4,2},{5,3},{6,4},{7,5},{8,14},{9,15},{10,... | collective-permute-start | bytes 589832 | tf_op jit(solution)/shard_map/ppermute | solution.py:583
  40.8 3.3 %collective-permute-done.7.refs_3_ = bf16[256,384]{1,0:T(8,128)(2,1)S(1)} collective-permute-done((bf16[256,384]{1,0:T(8,128)(2,1)}, bf16[256,384]{1,0:T(8,128)(2,1)S(1)}, u32[]{:S(2)}, u32[]{:S(2)}) %collective-permute-start.7) | collective-permute-done | bytes 196640 | tf_op jit(solution)/shard_map/ppermute | solution.py:583
  47.0 5.4 %pair_lists.1 = (s32[160]{0:T(256)}, s32[160]{0:T(256)}, s32[8]{0:T(128)}) custom-call(s32[4]{0:T(128)} %pad_add_fusion.1.ids, s32[6144]{0:T(1024)} %select_n.109.meta, s32[3]{0:T(128)} %bitcast.19), custom_call_target="tpu_custom_call" | custom-call | flops 1048576 | bytes 1048576 | tf_op jit(solution)/shard_map/pair_lists/pallas_call | solution.py:179
  53.4 17.5 %attend.1 = (f32[256,128]{1,0:T(8,128)}, f32[256,128]{1,0:T(8,128)}, f32[256,128]{1,0:T(8,128)}, f32[256,128]{1,0:T(8,128)}, bf16[33,128,128]{2,1,0:T(8,128)(2,1...) custom-call(s32[4]{0:T(128)} %pad_add_fusion.1.ids, ...), custom_call_target="tpu_custom_call" | custom-call | flops 6000000000 | bytes 6291456 | tf_op jit(solution)/shard_map/attend/pallas_call | solution.py:287
  71.5 3.7 %collective-permute-start.21 = (f32[256,128]{1,0:T(8,128)}, f32[256,128]{1,0:T(8,128)S(1)}, u32[]{:S(2)}, u32[]{:S(2)}) collective-permute-start(f32[256,128]{1,0:T(8,128)} %get-tuple-element.65), channel_id=1, source_target_pairs={{0,4},{1,5},{2,6},{3,7},{4,0},{5,1},{6,2},{7,3},{8,12},{9,13},{10,... | collective-permute-start | bytes 393224 | tf_op jit(solution)/shard_map/ppermute | solution.py:583
  75.5 2.8 %collective-permute-done.20.refs_1_ = f32[256,128]{1,0:T(8,128)S(1)} collective-permute-done((f32[256,128]{1,0:T(8,128)}, f32[256,128]{1,0:T(8,128)S(1)}, u32[]{:S(2)}, u32[]{:S(2)}) %collective-permute-start.20) | collective-permute-done | bytes 131104 | tf_op jit(solution)/shard_map/ppermute | solution.py:583
  78.3 3.7 %collective-permute-done.21.refs_2_ = f32[256,128]{1,0:T(8,128)S(1)} collective-permute-done((f32[256,128]{1,0:T(8,128)}, f32[256,128]{1,0:T(8,128)S(1)}, u32[]{:S(2)}, u32[]{:S(2)}) %collective-permute-start.21) | collective-permute-done | bytes 131104 | tf_op jit(solution)/shard_map/ppermute | solution.py:583
  82.8 3.1 %middle.1 = (bf16[256,512]{1,0:T(8,128)(2,1)}, bf16[256,512]{1,0:T(8,128)(2,1)}, bf16[256,128]{1,0:T(8,128)(2,1)}, bf16[256,128]{1,0:T(8,128)(2,1)}, bf16[256,128]{1,0:T(8,128)(2,1)}, /*index=5*/bf16[256,128]{1,0:T(8,128)(2,1)}) custom-call(s32[4]{0:T(128)} %pad_add_fusion.1.ids, bf16[256,1024]{1,0:T(8,128)(2,1)} %cot.5, bf16[512,1024]{1,0:T(8,128)(2,1)} %out_proj.3, ...), custom_call_target="tpu_custom_call" | custom-call | flops 268435456 | bytes 4194304 | tf_op jit(solution)/shard_map/middle/pallas_call | solution.py:328
  87.5 2.8 %collective-permute-start.24 = (bf16[256,128]{1,0:T(8,128)(2,1)}, bf16[256,128]{1,0:T(8,128)(2,1)S(1)}, u32[]{:S(2)}, u32[]{:S(2)}) collective-permute-start(bf16[256,128]{1,0:T(8,128)(2,1)} %get-tuple-element.78), channel_id=1, source_target_pairs={{0,4},{1,5},{2,6},{3,7},{4,0},{5,1},{6,2},{7,3},{8,12},{9,13},{10,... | collective-permute-start | bytes 196616 | tf_op jit(solution)/shard_map/ppermute | solution.py:583
  90.5 3.7 %finish_output.1 = (bf16[256,1024]{1,0:T(8,128)(2,1)}, f32[256,1024]{1,0:T(8,128)}, bf16[256,1024]{1,0:T(8,128)(2,1)}) custom-call(s32[4]{0:T(128)} %pad_add_fusion.1.ids, bf16[256,1024]{1,0:T(8,128)(2,1)} %tokens.5, bf16[256,1024]{1,0:T(8,128)(2,1)} %cot.5, bf16[512,1024]{1,0:T(8,128)(2,1)} %out_proj.3, bf16[256,512]{1,0:T(8,128)(2,1)} %get-tuple-element.67.mixed), custom_call_target="tpu_custom_call" | custom-call | flops 805306368 | bytes 5242880 | tf_op jit(solution)/shard_map/finish_output/pallas_call | solution.py:369
  95.4 21.8 %attend_back.1 = (bf16[4,256,256]{2,1,0:T(8,128)(2,1)}, bf16[4,256,256]{2,1,0:T(8,128)(2,1)}, bf16[4,256,256]{2,1,0:T(8,128)(2,1)}, bf16[4,256,256]{2,1,0:T(8,12...) custom-call(s32[4]{0:T(128)} %pad_add_fusion.1.ids, f32[32]{0:T(128)} %pad_maximum_fusion.table, ...), custom_call_target="tpu_custom_call" | custom-call | flops 12000000000 | bytes 8388608 | tf_op jit(solution)/shard_map/attend_back/pallas_call | solution.py:477
  120.0 1.9 %collective-permute-start.53 = (f32[16,128]{1,0:T(8,128)S(1)}, f32[16,128]{1,0:T(8,128)S(1)}, u32[]{:S(2)}, u32[]{:S(2)}) collective-permute-start(f32[16,128]{1,0:T(8,128)S(1)} %add.146), channel_id=1, source_target_pairs={{0,96},{16,112},{32,64},{48,80},{64,32},{80,48},{96,0},{112,16},{1... | collective-permute-start | bytes 24584 | tf_op jit(solution)/shard_map/ppermute | solution.py:587
  122.0 3.4 %collective-permute-start.52 = (f32[16,128]{1,0:T(8,128)S(1)}, f32[16,128]{1,0:T(8,128)S(1)}, u32[]{:S(2)}, u32[]{:S(2)}) collective-permute-start(f32[16,128]{1,0:T(8,128)S(1)} %add.146), channel_id=1, source_target_pairs={{0,80},{16,64},{32,112},{48,96},{64,16},{80,0},{96,48},{112,32},{1... | collective-permute-start | bytes 24584 | tf_op jit(solution)/shard_map/ppermute | solution.py:587
  128.3 2.6 %collective-permute-start.48 = (f32[16,128]{1,0:T(8,128)S(1)}, f32[16,128]{1,0:T(8,128)S(1)}, u32[]{:S(2)}, u32[]{:S(2)}) collective-permute-start(f32[16,128]{1,0:T(8,128)S(1)} %add.146), channel_id=1, source_target_pairs={{0,16},{16,0},{32,48},{48,32},{64,80},{80,64},{96,112},{112,96},{1... | collective-permute-start | bytes 24584 | tf_op jit(solution)/shard_map/ppermute | solution.py:587
  135.8 2.4 %collective-permute-done.36 = bf16[64,1024]{1,0:T(8,128)(2,1)S(1)} collective-permute-done((bf16[64,1024]{1,0:T(8,128)(2,1)S(1)}, bf16[64,1024]{1,0:T(8,128)(2,1)S(1)}, u32[]{:S(2)}, u32[]{:S(2)}) %collective-permute-start.36) | collective-permute-done | bytes 131104 | tf_op jit(solution)/shard_map/ppermute | solution.py:583
  144.3 2.6 %collective-permute-start.57 = (f32[16,128]{1,0:T(8,128)S(1)}, f32[16,128]{1,0:T(8,128)S(1)}, u32[]{:S(2)}, u32[]{:S(2)}) collective-permute-start(f32[16,128]{1,0:T(8,128)S(1)} %add.154), channel_id=1, source_target_pairs={{0,4},{1,5},{2,6},{3,7},{4,0},{5,1},{6,2},{7,3},{8,12},{9,13},{10,... | collective-permute-start | bytes 24584 | tf_op jit(solution)/shard_map/ppermute | solution.py:583
  147.9 2.8 %combine.1 = (bf16[384,256]{1,0:T(8,128)(2,1)}, bf16[384,256]{1,0:T(8,128)(2,1)}, bf16[384,256]{1,0:T(8,128)(2,1)}, bf16[384,256]{1,0:T(8,128)(2,1)}, bf16[256,2...) custom-call(bf16[4,256,256]{2,1,0:T(8,128)(2,1)} %get-tuple-element.80.mine_s, ...), custom_call_target="tpu_custom_call" | custom-call | flops 1048576 | bytes 5242880 | tf_op jit(solution)/shard_map/combine/pallas_call | solution.py:505
  152.4 2.0 %collective-permute-start.32 = (bf16[256,256]{1,0:T(8,128)(2,1)}, bf16[256,256]{1,0:T(8,128)(2,1)S(1)}, u32[]{:S(2)}, u32[]{:S(2)}) collective-permute-start(bf16[256,256]{1,0:T(8,128)(2,1)} %get-tuple-element.90), channel_id=1, source_target_pairs={{0,10},{1,11},{2,12},{3,13},{4,14},{5,15},{6,8},{7,9},{8,2},{9,3},... | collective-permute-start | bytes 393224 | tf_op jit(solution)/shard_map/ppermute | solution.py:583
  154.6 2.5 %collective-permute-start.46 = (f32[4,1024]{1,0:T(4,128)S(1)}, f32[4,1024]{1,0:T(4,128)S(1)}, u32[]{:S(2)}, u32[]{:S(2)}) collective-permute-start(f32[4,1024]{1,0:T(4,128)S(1)} %get-tuple-element.102), channel_id=1, source_target_pairs={{0,112},{16,96},{32,80},{48,64},{64,48},{80,32},{96,16},{112,0},{1... | collective-permute-start | bytes 49160 | tf_op jit(solution)/shard_map/ppermute | solution.py:587
  157.1 2.6 %collective-permute-start.45 = (f32[4,1024]{1,0:T(4,128)S(1)}, f32[4,1024]{1,0:T(4,128)S(1)}, u32[]{:S(2)}, u32[]{:S(2)}) collective-permute-start(f32[4,1024]{1,0:T(4,128)S(1)} %get-tuple-element.103), channel_id=1, source_target_pairs={{0,96},{16,112},{32,64},{48,80},{64,32},{80,48},{96,0},{112,16},{1... | collective-permute-start | bytes 49160 | tf_op jit(solution)/shard_map/ppermute | solution.py:587
  165.9 4.2 %collective-permute-start.33 = (bf16[256,256]{1,0:T(8,128)(2,1)}, bf16[256,256]{1,0:T(8,128)(2,1)S(1)}, u32[]{:S(2)}, u32[]{:S(2)}) collective-permute-start(bf16[256,256]{1,0:T(8,128)(2,1)} %get-tuple-element.91), channel_id=1, source_target_pairs={{0,12},{1,13},{2,14},{3,15},{4,8},{5,9},{6,10},{7,11},{8,4},{9,5},... | collective-permute-start | bytes 393224 | tf_op jit(solution)/shard_map/ppermute | solution.py:583
  170.1 2.6 %collective-permute-start.34 = (bf16[256,256]{1,0:T(8,128)(2,1)}, bf16[256,256]{1,0:T(8,128)(2,1)S(1)}, u32[]{:S(2)}, u32[]{:S(2)}) collective-permute-start(bf16[256,256]{1,0:T(8,128)(2,1)} %get-tuple-element.92), channel_id=1, source_target_pairs={{0,14},{1,15},{2,8},{3,9},{4,10},{5,11},{6,12},{7,13},{8,6},{9,7},... | collective-permute-start | bytes 393224 | tf_op jit(solution)/shard_map/ppermute | solution.py:583
  174.1 2.8 %collective-permute-start.30 = (bf16[384,256]{1,0:T(8,128)(2,1)}, bf16[384,256]{1,0:T(8,128)(2,1)S(1)}, u32[]{:S(2)}, u32[]{:S(2)}) collective-permute-start(bf16[384,256]{1,0:T(8,128)(2,1)} %get-tuple-element.88), channel_id=1, source_target_pairs={{0,6},{1,7},{2,0},{3,1},{4,2},{5,3},{6,4},{7,5},{8,14},{9,15},{10,... | collective-permute-start | bytes 589832 | tf_op jit(solution)/shard_map/ppermute | solution.py:583
  177.8 4.1 %collective-permute-done.28.refs_1_ = bf16[384,256]{1,0:T(8,128)(2,1)S(1)} collective-permute-done((bf16[384,256]{1,0:T(8,128)(2,1)}, bf16[384,256]{1,0:T(8,128)(2,1)S(1)}, u32[]{:S(2)}, u32[]{:S(2)}) %collective-permute-start.28) | collective-permute-done | bytes 196640 | tf_op jit(solution)/shard_map/ppermute | solution.py:583
  184.1 7.0 %finish_grad.1 = bf16[256,1024]{1,0:T(8,128)(2,1)} custom-call(s32[4]{0:T(128)} %pad_add_fusion.1.ids, bf16[256,1024]{1,0:T(8,128)(2,1)} %tokens.5, bf16[256,1024]{1,0:T(8,128)(2,1)} %cot.5, bf16[1024,2048]{1,0:T(8,128)(2,1)} %in_proj.1, bf16[4,4,256,128]{3,2,1,0:T(8,128)(2,1)} %get-tuple-element.51.slope, bf16[256,512]{1,0:T(8,128)(2,1)} %get-tuple-element.69.grad_gate, ...), custom_call_target="tpu_custom_call" | custom-call | flops 1073741824 | bytes 8388608 | tf_op jit(solution)/shard_map/finish_grad/pallas_call | solution.py:551
  (210 shorter events, 52.4 us)
Async XLA Ops:
  2.1 12.9 %collective-permute-start = (s32[384]{0:T(512)S(1)}, s32[384]{0:T(512)S(1)}, u32[]{:S(2)}, u32[]{:S(2)}) collective-permute-start(s32[384]{0:T(512)S(1)} %pad_add_fusion), channel_id=1, source_target_pairs={{0,1},{1,0},{2,3},{3,2},{4,5},{5,4},{6,7},{7,6},{8,9},{9,8},{10,11... | collective-permute-start | bytes 4616 | tf_op jit(solution)/shard_map/ppermute | solution.py:583
  10.0 23.4 %collective-permute-start.12 = (bf16[256,256]{1,0:T(8,128)(2,1)}, bf16[256,256]{1,0:T(8,128)(2,1)S(1)}, u32[]{:S(2)}, u32[]{:S(2)}) collective-permute-start(bf16[256,256]{1,0:T(8,128)(2,1)} %get-tuple-element.59), channel_id=1, source_target_pairs={{0,8},{1,9},{2,10},{3,11},{4,12},{5,13},{6,14},{7,15},{8,0},{9,1},... | collective-permute-start | bytes 393224 | tf_op jit(solution)/shard_map/ppermute | solution.py:583
  11.3 23.0 %collective-permute-start.13 = (bf16[256,256]{1,0:T(8,128)(2,1)}, bf16[256,256]{1,0:T(8,128)(2,1)S(1)}, u32[]{:S(2)}, u32[]{:S(2)}) collective-permute-start(bf16[256,256]{1,0:T(8,128)(2,1)} %get-tuple-element.60), channel_id=1, source_target_pairs={{0,10},{1,11},{2,12},{3,13},{4,14},{5,15},{6,8},{7,9},{8,2},{9,3},... | collective-permute-start | bytes 393224 | tf_op jit(solution)/shard_map/ppermute | solution.py:583
  20.8 15.7 %collective-permute-start.14 = (bf16[256,256]{1,0:T(8,128)(2,1)}, bf16[256,256]{1,0:T(8,128)(2,1)S(1)}, u32[]{:S(2)}, u32[]{:S(2)}) collective-permute-start(bf16[256,256]{1,0:T(8,128)(2,1)} %get-tuple-element.61), channel_id=1, source_target_pairs={{0,12},{1,13},{2,14},{3,15},{4,8},{5,9},{6,10},{7,11},{8,4},{9,5},... | collective-permute-start | bytes 393224 | tf_op jit(solution)/shard_map/ppermute | solution.py:583
  23.0 14.8 %collective-permute-start.5 = (bf16[256,384]{1,0:T(8,128)(2,1)}, bf16[256,384]{1,0:T(8,128)(2,1)S(1)}, u32[]{:S(2)}, u32[]{:S(2)}) collective-permute-start(bf16[256,384]{1,0:T(8,128)(2,1)} %get-tuple-element.56), channel_id=1, source_target_pairs={{0,2},{1,3},{2,4},{3,5},{4,6},{5,7},{6,0},{7,1},{8,10},{9,11},{10,... | collective-permute-start | bytes 589832 | tf_op jit(solution)/shard_map/ppermute | solution.py:583
  34.3 9.8 %collective-permute-start.7 = (bf16[256,384]{1,0:T(8,128)(2,1)}, bf16[256,384]{1,0:T(8,128)(2,1)S(1)}, u32[]{:S(2)}, u32[]{:S(2)}) collective-permute-start(bf16[256,384]{1,0:T(8,128)(2,1)} %get-tuple-element.58), channel_id=1, source_target_pairs={{0,6},{1,7},{2,0},{3,1},{4,2},{5,3},{6,4},{7,5},{8,14},{9,15},{10,... | collective-permute-start | bytes 589832 | tf_op jit(solution)/shard_map/ppermute | solution.py:583
  40.8 11.6 %collective-permute-start.18 = (bf16[256,256]{1,0:T(8,128)(2,1)S(1)}, bf16[256,256]{1,0:T(8,128)(2,1)S(1)}, u32[]{:S(2)}, u32[]{:S(2)}) collective-permute-start(bf16[256,256]{1,0:T(8,128)(2,1)S(1)} %collective-permute-done.14.refs_10_), channel_id=1, source_target_pairs={{0,1},{1,0},{2,3},{3,2},{4,5},{5,4},{6,7},{7,6},{8,9},{9,8},{10,11... | collective-permute-start | bytes 393224 | tf_op jit(solution)/shard_map/ppermute | solution.py:583
  44.2 8.3 %collective-permute-start.19 = (bf16[256,256]{1,0:T(8,128)(2,1)S(1)}, bf16[256,256]{1,0:T(8,128)(2,1)S(1)}, u32[]{:S(2)}, u32[]{:S(2)}) collective-permute-start(bf16[256,256]{1,0:T(8,128)(2,1)S(1)} %collective-permute-done.15.refs_11_), channel_id=1, source_target_pairs={{0,1},{1,0},{2,3},{3,2},{4,5},{5,4},{6,7},{7,6},{8,9},{9,8},{10,11... | collective-permute-start | bytes 393224 | tf_op jit(solution)/shard_map/ppermute | solution.py:583
  44.2 8.3 %collective-permute-start.9 = (bf16[256,384]{1,0:T(8,128)(2,1)S(1)}, bf16[256,384]{1,0:T(8,128)(2,1)S(1)}, u32[]{:S(2)}, u32[]{:S(2)}) collective-permute-start(bf16[256,384]{1,0:T(8,128)(2,1)S(1)} %collective-permute-done.5.refs_1_), channel_id=1, source_target_pairs={{0,1},{1,0},{2,3},{3,2},{4,5},{5,4},{6,7},{7,6},{8,9},{9,8},{10,11... | collective-permute-start | bytes 589832 | tf_op jit(solution)/shard_map/ppermute | solution.py:583
  44.7 7.8 %collective-permute-start.10 = (bf16[256,384]{1,0:T(8,128)(2,1)S(1)}, bf16[256,384]{1,0:T(8,128)(2,1)S(1)}, u32[]{:S(2)}, u32[]{:S(2)}) collective-permute-start(bf16[256,384]{1,0:T(8,128)(2,1)S(1)} %collective-permute-done.6.refs_2_), channel_id=1, source_target_pairs={{0,1},{1,0},{2,3},{3,2},{4,5},{5,4},{6,7},{7,6},{8,9},{9,8},{10,11... | collective-permute-start | bytes 589832 | tf_op jit(solution)/shard_map/ppermute | solution.py:583
  71.5 10.6 %collective-permute-start.21 = (f32[256,128]{1,0:T(8,128)}, f32[256,128]{1,0:T(8,128)S(1)}, u32[]{:S(2)}, u32[]{:S(2)}) collective-permute-start(f32[256,128]{1,0:T(8,128)} %get-tuple-element.65), channel_id=1, source_target_pairs={{0,4},{1,5},{2,6},{3,7},{4,0},{5,1},{6,2},{7,3},{8,12},{9,13},{10,... | collective-permute-start | bytes 393224 | tf_op jit(solution)/shard_map/ppermute | solution.py:583
  85.9 8.3 %collective-permute-start.23 = (bf16[256,128]{1,0:T(8,128)(2,1)}, bf16[256,128]{1,0:T(8,128)(2,1)S(1)}, u32[]{:S(2)}, u32[]{:S(2)}) collective-permute-start(bf16[256,128]{1,0:T(8,128)(2,1)} %get-tuple-element.77), channel_id=1, source_target_pairs={{0,2},{1,3},{2,4},{3,5},{4,6},{5,7},{6,0},{7,1},{8,10},{9,11},{10,... | collective-permute-start | bytes 196616 | tf_op jit(solution)/shard_map/ppermute | solution.py:583
  94.3 32.2 %collective-permute-start.35 = (bf16[256,1024]{1,0:T(8,128)(2,1)}, bf16[256,1024]{1,0:T(8,128)(2,1)S(1)}, u32[]{:S(2)}, u32[]{:S(2)}) collective-permute-start(bf16[256,1024]{1,0:T(8,128)(2,1)} %get-tuple-element.94), channel_id=1, source_target_pairs={{0,1},{1,0},{2,3},{3,2},{4,5},{5,4},{6,7},{7,6},{8,9},{9,8},{10,11... | collective-permute-start | bytes 1572872 | tf_op jit(solution)/shard_map/ppermute | solution.py:583
  120.0 8.3 %collective-permute-start.53 = (f32[16,128]{1,0:T(8,128)S(1)}, f32[16,128]{1,0:T(8,128)S(1)}, u32[]{:S(2)}, u32[]{:S(2)}) collective-permute-start(f32[16,128]{1,0:T(8,128)S(1)} %add.146), channel_id=1, source_target_pairs={{0,96},{16,112},{32,64},{48,80},{64,32},{80,48},{96,0},{112,16},{1... | collective-permute-start | bytes 24584 | tf_op jit(solution)/shard_map/ppermute | solution.py:587
  122.0 8.9 %collective-permute-start.52 = (f32[16,128]{1,0:T(8,128)S(1)}, f32[16,128]{1,0:T(8,128)S(1)}, u32[]{:S(2)}, u32[]{:S(2)}) collective-permute-start(f32[16,128]{1,0:T(8,128)S(1)} %add.146), channel_id=1, source_target_pairs={{0,80},{16,64},{32,112},{48,96},{64,16},{80,0},{96,48},{112,32},{1... | collective-permute-start | bytes 24584 | tf_op jit(solution)/shard_map/ppermute | solution.py:587
  130.9 16.0 %collective-permute-start.26 = (bf16[4,256,256]{2,1,0:T(8,128)(2,1)S(1)}, bf16[4,256,256]{2,1,0:T(8,128)(2,1)S(1)}, u32[]{:S(2)}, u32[]{:S(2)}) collective-permute-start(bf16[4,256,256]{2,1,0:T(8,128)(2,1)S(1)} %copy-done.15), channel_id=1, source_target_pairs={{0,1},{1,0},{2,3},{3,2},{4,5},{5,4},{6,7},{7,6},{8,9},{9,8},{10,11... | collective-permute-start | bytes 1572872 | tf_op jit(solution)/shard_map/ppermute | solution.py:583
  131.0 15.9 %collective-permute-start.27 = (bf16[4,256,256]{2,1,0:T(8,128)(2,1)S(1)}, bf16[4,256,256]{2,1,0:T(8,128)(2,1)S(1)}, u32[]{:S(2)}, u32[]{:S(2)}) collective-permute-start(bf16[4,256,256]{2,1,0:T(8,128)(2,1)S(1)} %copy-done.14), channel_id=1, source_target_pairs={{0,1},{1,0},{2,3},{3,2},{4,5},{5,4},{6,7},{7,6},{8,9},{9,8},{10,11... | collective-permute-start | bytes 1572872 | tf_op jit(solution)/shard_map/ppermute | solution.py:583
  141.3 11.0 %collective-permute-start.39 = (bf16[32,1024]{1,0:T(8,128)(2,1)S(1)}, bf16[32,1024]{1,0:T(8,128)(2,1)S(1)}, u32[]{:S(2)}, u32[]{:S(2)}) collective-permute-start(bf16[32,1024]{1,0:T(8,128)(2,1)S(1)} %slice.117), channel_id=1, source_target_pairs={{0,8},{1,9},{2,10},{3,11},{4,12},{5,13},{6,14},{7,15},{8,0},{9,1},... | collective-permute-start | bytes 196616 | tf_op jit(solution)/shard_map/ppermute | solution.py:583
  143.4 11.1 %collective-permute-start.58 = (f32[16,128]{1,0:T(8,128)S(1)}, f32[16,128]{1,0:T(8,128)S(1)}, u32[]{:S(2)}, u32[]{:S(2)}) collective-permute-start(f32[16,128]{1,0:T(8,128)S(1)} %add.154), channel_id=1, source_target_pairs={{0,6},{1,7},{2,0},{3,1},{4,2},{5,3},{6,4},{7,5},{8,14},{9,15},{10,... | collective-permute-start | bytes 24584 | tf_op jit(solution)/shard_map/ppermute | solution.py:583
  144.3 10.2 %collective-permute-start.57 = (f32[16,128]{1,0:T(8,128)S(1)}, f32[16,128]{1,0:T(8,128)S(1)}, u32[]{:S(2)}, u32[]{:S(2)}) collective-permute-start(f32[16,128]{1,0:T(8,128)S(1)} %add.154), channel_id=1, source_target_pairs={{0,4},{1,5},{2,6},{3,7},{4,0},{5,1},{6,2},{7,3},{8,12},{9,13},{10,... | collective-permute-start | bytes 24584 | tf_op jit(solution)/shard_map/ppermute | solution.py:583
  146.9 10.1 %collective-permute-start.56 = (f32[16,128]{1,0:T(8,128)S(1)}, f32[16,128]{1,0:T(8,128)S(1)}, u32[]{:S(2)}, u32[]{:S(2)}) collective-permute-start(f32[16,128]{1,0:T(8,128)S(1)} %add.154), channel_id=1, source_target_pairs={{0,2},{1,3},{2,4},{3,5},{4,6},{5,7},{6,0},{7,1},{8,10},{9,11},{10,... | collective-permute-start | bytes 24584 | tf_op jit(solution)/shard_map/ppermute | solution.py:583
  150.6 9.1 %collective-permute-start.31 = (bf16[256,256]{1,0:T(8,128)(2,1)}, bf16[256,256]{1,0:T(8,128)(2,1)S(1)}, u32[]{:S(2)}, u32[]{:S(2)}) collective-permute-start(bf16[256,256]{1,0:T(8,128)(2,1)} %get-tuple-element.89), channel_id=1, source_target_pairs={{0,8},{1,9},{2,10},{3,11},{4,12},{5,13},{6,14},{7,15},{8,0},{9,1},... | collective-permute-start | bytes 393224 | tf_op jit(solution)/shard_map/ppermute | solution.py:583
  152.4 9.2 %collective-permute-start.32 = (bf16[256,256]{1,0:T(8,128)(2,1)}, bf16[256,256]{1,0:T(8,128)(2,1)S(1)}, u32[]{:S(2)}, u32[]{:S(2)}) collective-permute-start(bf16[256,256]{1,0:T(8,128)(2,1)} %get-tuple-element.90), channel_id=1, source_target_pairs={{0,10},{1,11},{2,12},{3,13},{4,14},{5,15},{6,8},{7,9},{8,2},{9,3},... | collective-permute-start | bytes 393224 | tf_op jit(solution)/shard_map/ppermute | solution.py:583
  154.6 8.8 %collective-permute-start.46 = (f32[4,1024]{1,0:T(4,128)S(1)}, f32[4,1024]{1,0:T(4,128)S(1)}, u32[]{:S(2)}, u32[]{:S(2)}) collective-permute-start(f32[4,1024]{1,0:T(4,128)S(1)} %get-tuple-element.102), channel_id=1, source_target_pairs={{0,112},{16,96},{32,80},{48,64},{64,48},{80,32},{96,16},{112,0},{1... | collective-permute-start | bytes 49160 | tf_op jit(solution)/shard_map/ppermute | solution.py:587
  157.1 8.8 %collective-permute-start.45 = (f32[4,1024]{1,0:T(4,128)S(1)}, f32[4,1024]{1,0:T(4,128)S(1)}, u32[]{:S(2)}, u32[]{:S(2)}) collective-permute-start(f32[4,1024]{1,0:T(4,128)S(1)} %get-tuple-element.103), channel_id=1, source_target_pairs={{0,96},{16,112},{32,64},{48,80},{64,32},{80,48},{96,0},{112,16},{1... | collective-permute-start | bytes 49160 | tf_op jit(solution)/shard_map/ppermute | solution.py:587
  159.7 10.4 %collective-permute-start.44 = (f32[4,1024]{1,0:T(4,128)S(1)}, f32[4,1024]{1,0:T(4,128)S(1)}, u32[]{:S(2)}, u32[]{:S(2)}) collective-permute-start(f32[4,1024]{1,0:T(4,128)S(1)} %get-tuple-element.104), channel_id=1, source_target_pairs={{0,80},{16,64},{32,112},{48,96},{64,16},{80,0},{96,48},{112,32},{1... | collective-permute-start | bytes 49160 | tf_op jit(solution)/shard_map/ppermute | solution.py:587
  161.6 11.1 %collective-permute-start.43 = (f32[4,1024]{1,0:T(4,128)S(1)}, f32[4,1024]{1,0:T(4,128)S(1)}, u32[]{:S(2)}, u32[]{:S(2)}) collective-permute-start(f32[4,1024]{1,0:T(4,128)S(1)} %get-tuple-element.105), channel_id=1, source_target_pairs={{0,64},{16,80},{32,96},{48,112},{64,0},{80,16},{96,32},{112,48},{1... | collective-permute-start | bytes 49160 | tf_op jit(solution)/shard_map/ppermute | solution.py:587
  162.0 12.1 %collective-permute-start.42 = (f32[4,1024]{1,0:T(4,128)S(1)}, f32[4,1024]{1,0:T(4,128)S(1)}, u32[]{:S(2)}, u32[]{:S(2)}) collective-permute-start(f32[4,1024]{1,0:T(4,128)S(1)} %get-tuple-element.106), channel_id=1, source_target_pairs={{0,48},{16,32},{32,16},{48,0},{64,112},{80,96},{96,80},{112,64},{1... | collective-permute-start | bytes 49160 | tf_op jit(solution)/shard_map/ppermute | solution.py:587
  163.4 10.8 %collective-permute-start.41 = (f32[4,1024]{1,0:T(4,128)S(1)}, f32[4,1024]{1,0:T(4,128)S(1)}, u32[]{:S(2)}, u32[]{:S(2)}) collective-permute-start(f32[4,1024]{1,0:T(4,128)S(1)} %get-tuple-element.107), channel_id=1, source_target_pairs={{0,32},{16,48},{32,0},{48,16},{64,96},{80,112},{96,64},{112,80},{1... | collective-permute-start | bytes 49160 | tf_op jit(solution)/shard_map/ppermute | solution.py:587
  165.9 11.6 %collective-permute-start.33 = (bf16[256,256]{1,0:T(8,128)(2,1)}, bf16[256,256]{1,0:T(8,128)(2,1)S(1)}, u32[]{:S(2)}, u32[]{:S(2)}) collective-permute-start(bf16[256,256]{1,0:T(8,128)(2,1)} %get-tuple-element.91), channel_id=1, source_target_pairs={{0,12},{1,13},{2,14},{3,15},{4,8},{5,9},{6,10},{7,11},{8,4},{9,5},... | collective-permute-start | bytes 393224 | tf_op jit(solution)/shard_map/ppermute | solution.py:583
  172.7 9.2 %collective-permute-start.28 = (bf16[384,256]{1,0:T(8,128)(2,1)}, bf16[384,256]{1,0:T(8,128)(2,1)S(1)}, u32[]{:S(2)}, u32[]{:S(2)}) collective-permute-start(bf16[384,256]{1,0:T(8,128)(2,1)} %get-tuple-element.86), channel_id=1, source_target_pairs={{0,2},{1,3},{2,4},{3,5},{4,6},{5,7},{6,0},{7,1},{8,10},{9,11},{10,... | collective-permute-start | bytes 589832 | tf_op jit(solution)/shard_map/ppermute | solution.py:583
  174.1 9.3 %collective-permute-start.30 = (bf16[384,256]{1,0:T(8,128)(2,1)}, bf16[384,256]{1,0:T(8,128)(2,1)S(1)}, u32[]{:S(2)}, u32[]{:S(2)}) collective-permute-start(bf16[384,256]{1,0:T(8,128)(2,1)} %get-tuple-element.88), channel_id=1, source_target_pairs={{0,6},{1,7},{2,0},{3,1},{4,2},{5,3},{6,4},{7,5},{8,14},{9,15},{10,... | collective-permute-start | bytes 589832 | tf_op jit(solution)/shard_map/ppermute | solution.py:583
  (61 other events, 456.7 us)

commit v2 on v1

v2 whole, which is shorter than its diff:
```python
import math

import jax
import jax.numpy as jnp
from jax import lax
from jax.experimental import pallas as pl
from jax.experimental.pallas import tpu as pltpu
from jax.sharding import PartitionSpec as P

f32 = jnp.float32
bf16 = jnp.bfloat16
i32 = jnp.int32
T = 128
EPS = 1e-05
HEADS = 4
BUCKETS = 12
DEVS = 16
TILES = 32
QT = 8
SCALE = 1.0 / math.sqrt(128.0)
LIST = 160
FAR_U = 8
NEAR_U = 4
NEAR_FLAG = 32768
DUMMY = QT + 16 * TILES
VMEM = pl.BlockSpec(memory_space=pltpu.VMEM)
SMEM = pl.BlockSpec(memory_space=pltpu.SMEM)
NT_DIMS = (((1,), (1,)), ((), ()))
TN_DIMS = (((0,), (0,)), ((), ()))


def params(mib=56):
    return pltpu.CompilerParams(vmem_limit_bytes=mib * 1024 * 1024)


def cost(flops, size):
    return pl.CostEstimate(flops=int(flops), bytes_accessed=int(size), transcendentals=0)


def sds(shape, dtype):
    return jax.ShapeDtypeStruct(shape, dtype)


def norm_rows(values):
    centre = jnp.mean(values, axis=-1, keepdims=True)
    shifted = values - centre
    spread = jnp.mean(shifted * shifted, axis=-1, keepdims=True)
    inverse = lax.rsqrt(spread + EPS)
    return shifted * inverse, inverse


def norm_back(upstream, normed, inverse):
    first = jnp.mean(upstream, axis=-1, keepdims=True)
    second = jnp.mean(upstream * normed, axis=-1, keepdims=True)
    return inverse * (upstream - first - normed * second)


def project_kernel(ids, tokens, meta, w_gate, w_value, w_query, w_key, gate, slope, *rest):
    outs, normed = rest[:8], rest[8]
    step = pl.program_id(0)

    @pl.when(step == 0)
    def _():
        normed[...] = norm_rows(tokens[...].astype(f32))[0].astype(bf16)

    weights = jnp.concatenate([w_gate[...], w_value[...], w_query[...], w_key[...]], axis=1)
    pre = jnp.dot(normed[...], weights, preferred_element_type=f32)
    sig = 0.5 * jnp.tanh(0.5 * pre) + 0.5
    act = (pre * sig).astype(bf16)
    slopes = (sig * (1.0 + pre * (1.0 - sig))).astype(bf16)
    for kind in range(4):
        slope[kind, 0] = slopes[:, kind * T : (kind + 1) * T]
    gate[0] = act[:, :T]
    value, query, key = act[:, T : 2 * T], act[:, 2 * T : 3 * T], act[:, 3 * T :]
    for which in range(4):

        @pl.when(step == which)
        def _(which=which):
            for ref in (outs[which], outs[4 + which]):
                ref[0:256, 0:T] = key
                ref[0:256, T : 2 * T] = value
                ref[256:, 0:256] = meta[...]
            outs[which][0:256, 2 * T :] = query
            outs[which][256:, 2 * T :] = jnp.zeros((16, T), bf16)


def project(ids, tokens, meta, in_proj):
    def column(kind):
        return pl.BlockSpec((1024, T), lambda s, ids: (0, kind * HEADS + (ids[1] + s) % HEADS))

    whole = lambda shape: pl.BlockSpec(shape, lambda s, ids: (0,) * len(shape))
    head_of = lambda s, ids: (ids[1] + s) % HEADS
    return pl.pallas_call(
        project_kernel,
        grid_spec=pltpu.PrefetchScalarGridSpec(
            num_scalar_prefetch=1,
            grid=(4,),
            in_specs=[whole((256, 1024)), whole((16, 256))] + [column(kind) for kind in range(4)],
            out_specs=[
                pl.BlockSpec((1, 256, T), lambda s, ids: (head_of(s, ids), 0, 0)),
                pl.BlockSpec((4, 1, 256, T), lambda s, ids: (0, head_of(s, ids), 0, 0)),
            ]
            + [whole((272, 384))] * 4
            + [whole((272, 256))] * 4,
            scratch_shapes=[pltpu.VMEM((256, 1024), bf16)],
        ),
        out_shape=[sds((4, 256, T), bf16), sds((4, 4, 256, T), bf16)]
        + [sds((272, 384), bf16)] * 4
        + [sds((272, 256), bf16)] * 4,
        compiler_params=params(),
        cost_estimate=cost(2 * 256 * 1024 * 2048, 7 << 20),
        name="project",
    )(ids, tokens, meta, in_proj, in_proj, in_proj, in_proj)


def bias_far(gap, table, bottom):
    first = table[bottom]
    second = table[bottom + 1]
    third = table[bottom + 2]
    limit1 = table[16 + bottom + 1]
    limit2 = table[16 + bottom + 2]
    over1 = gap >= limit1
    over2 = gap >= limit2
    return jnp.where(over2, third, jnp.where(over1, second, first)), over1, over2


def bias_near(gap, table):
    bias = jnp.full(gap.shape, table[0], f32)
    for j in range(1, BUCKETS):
        bias = jnp.where(gap >= float(2**j - 1), table[j], bias)
    return bias


def keep_near(ids, start, jj, k):
    tile = query_tile(ids, jj)
    row = lax.broadcasted_iota(i32, (T, T), 0)
    col = lax.broadcasted_iota(i32, (T, T), 1)
    later = (col - row) <= (tile - k) * T
    return later & ((col + k * T) >= start)


STAGE = [
    pltpu.VMEM((TILES + 1, T, T), bf16),
    pltpu.VMEM((TILES + 1, T, T), bf16),
    pltpu.VMEM((QT + 1, T, T), bf16),
    pltpu.VMEM((QT + 1, T, T), f32),
    pltpu.VMEM((TILES + 1, 8, T), f32),
    pltpu.VMEM((QT + 1, T, T), i32),
]


def query_tile(ids, jj):
    dev = ids[0] * 8 + (jj // 2) * 2 + ids[2]
    return jnp.where(jj % 2 == 0, dev, 2 * DEVS - 1 - dev)


def starts_of(lengths, pos):
    end0 = lengths[0]
    end1 = lengths[0] + lengths[1]
    return jnp.where(pos >= end1, end1, jnp.where(pos >= end0, end0, 0))


def stage(ids, lengths, ins, keys, values, queries, tq, tk, start, flags=None, times=None):
    y, z, core = ids[0], ids[1], ids[2]
    for group in range(4):
        for t in range(4):
            ref = ins[group * 4 + t]
            zz = (z + 4 - t) % 4
            dev = (y if group < 2 else 1 - y) * 8 + zz * 2 + (core if group % 2 == 0 else 1 - core)
            keys[dev] = ref[0:T, 0:T]
            values[dev] = ref[0:T, T : 2 * T]
            keys[2 * DEVS - 1 - dev] = ref[T : 2 * T, 0:T]
            values[2 * DEVS - 1 - dev] = ref[T : 2 * T, T : 2 * T]
            head = ref[256:272, 0:256].astype(f32)
            moments = head[0:1] * 128.0 + head[1:2]
            tk[dev] = jnp.broadcast_to(moments[:, :T], (8, T))
            tk[2 * DEVS - 1 - dev] = jnp.broadcast_to(moments[:, T:], (8, T))
            if times is not None:
                times[pl.ds(dev, 1), :] = moments[:, :T]
                times[pl.ds(2 * DEVS - 1 - dev, 1), :] = moments[:, T:]
            if group == 0:
                queries[2 * zz] = ref[0:T, 2 * T :]
                queries[2 * zz + 1] = ref[T : 2 * T, 2 * T :]
                if flags is not None:
                    flags[pl.ds(2 * zz, 1), :] = head[2:3, :T]
                    flags[pl.ds(2 * zz + 1, 1), :] = head[2:3, T:]
    keys[TILES] = jnp.zeros((T, T), bf16)
    values[TILES] = jnp.zeros((T, T), bf16)
    queries[QT] = jnp.zeros((T, T), bf16)
    tk[TILES] = jnp.zeros((8, T), f32)
    tq[QT] = jnp.zeros((T, T), f32)
    start[QT] = jnp.zeros((T, T), i32)
    rows = lax.broadcasted_iota(i32, (T, T), 0)
    for jj in range(QT):
        tile = query_tile(ids, jj)
        tq[jj] = jnp.transpose(jnp.broadcast_to(tk[tile][0:1, :], (T, T)))
        start[jj] = starts_of(lengths, rows + tile * T)


def make_lists(ids, lengths, flags, times, q_times, codes, codes_smem, sem, far, near, counts):
    def level(gap):
        total = jnp.zeros(gap.shape, i32)
        for j in range(1, BUCKETS):
            total = total + jnp.where(gap >= float(2**j - 1), 1, 0)
        return total

    for jj in range(QT):
        q_times[jj : jj + 1, :] = times[pl.ds(query_tile(ids, jj), 1), :]
    turned = jnp.transpose(times[...])
    k_first, k_last = turned[0:1, :], turned[T - 1 :, :]
    q_first, q_last = q_times[:, 0:1], q_times[:, T - 1 :]
    jj = lax.broadcasted_iota(i32, (8, T), 0)
    kk = lax.broadcasted_iota(i32, (8, T), 1)
    tile = query_tile(ids, jj)
    low = starts_of(lengths, tile * T)
    high = starts_of(lengths, tile * T + T - 1)
    bottom = level(jnp.maximum(q_first - k_last, 0.0))
    top = level(q_last - k_first)
    allowed = (flags[...] > 0.5) & (kk <= tile) & (kk * T + T - 1 >= low)
    plain = (kk < tile) & (kk * T >= high) & (top - bottom <= 2)
    entry = jj + 16 * kk
    codes[...] = jnp.where(
        allowed, jnp.where(plain, entry + 1024 * bottom, entry + NEAR_FLAG), -1
    )
    copy = pltpu.make_async_copy(codes, codes_smem, sem)
    copy.start()
    copy.wait()

    def query_step(jj, sizes):
        tile = query_tile(ids, jj)

        def key_step(k, sizes):
            n_far, n_near = sizes
            code = codes_smem[jj, k]
            far[n_far] = code
            near[n_near] = code & (NEAR_FLAG - 1)
            is_near = code >= NEAR_FLAG
            is_far = (code >= 0) & jnp.logical_not(is_near)
            return n_far + is_far.astype(i32), n_near + is_near.astype(i32)

        return lax.fori_loop(starts_of(lengths, tile * T) // T, tile + 1, key_step, sizes)

    n_far, n_near = lax.fori_loop(0, QT, query_step, (jnp.int32(0), jnp.int32(0)))
    for pad in range(FAR_U):
        far[n_far + pad] = DUMMY
    for pad in range(NEAR_U):
        near[n_near + pad] = DUMMY
    counts[0] = (n_far + FAR_U - 1) // FAR_U
    counts[1] = (n_near + NEAR_U - 1) // NEAR_U


def unpack(ref, i, count):
    got = []
    for u in range(count):
        entry = ref[i * count + u]
        got.append((entry & 15, (entry >> 4) & 63, entry >> 10))
    return got


def forward_kernel(ids, table, lengths, *refs):
    ins, o_refs, (far, near, counts) = refs[:16], refs[16:20], refs[20:23]
    keys, values, queries, tq, tk, start, acc, flags, times, q_times, codes, codes_smem, sem = refs[23:]
    z = ids[1]
    times[...] = jnp.zeros(times.shape, f32)
    stage(ids, lengths, ins, keys, values, queries, tq, tk, start, flags, times)
    make_lists(ids, lengths, flags, times, q_times, codes, codes_smem, sem, far, near, counts)
    acc[...] = jnp.zeros(acc.shape, f32)

    def far_step(i, _):
        got = unpack(far, i, FAR_U)
        dots = [lax.dot_general(queries[j], keys[k], NT_DIMS, preferred_element_type=f32) for j, k, _ in got]
        weights = []
        for u, (jj, k, bottom) in enumerate(got):
            bias, _, _ = bias_far(tq[jj] - tk[k][0:1, :], table, bottom)
            half = dots[u] * (0.5 * SCALE) + bias
            weights.append((half * jnp.tanh(half) + half).astype(bf16))
        adds = [jnp.dot(weights[u], values[got[u][1]], preferred_element_type=f32) for u in range(len(got))]
        for u in range(len(got)):
            acc[got[u][0]] += adds[u]
        return 0

    def near_step(i, _):
        got = unpack(near, i, NEAR_U)
        dots = [lax.dot_general(queries[j], keys[k], NT_DIMS, preferred_element_type=f32) for j, k, _ in got]
        weights = []
        for u, (jj, k, _) in enumerate(got):
            half = dots[u] * (0.5 * SCALE) + bias_near(tq[jj] - tk[k][0:1, :], table)
            weight = half * jnp.tanh(half) + half
            weights.append(jnp.where(keep_near(ids, start[jj], jj, k), weight, 0.0).astype(bf16))
        adds = [jnp.dot(weights[u], values[got[u][1]], preferred_element_type=f32) for u in range(len(got))]
        for u in range(len(got)):
            acc[got[u][0]] += adds[u]
        return 0

    lax.fori_loop(0, counts[0], far_step, 0)
    lax.fori_loop(0, counts[1], near_step, 0)
    for s in range(4):
        zz = (z + s) % 4
        o_refs[s][0:T] = acc[2 * zz]
        o_refs[s][T:] = acc[2 * zz + 1]


def attend(ids, table, lengths, parts):
    return pl.pallas_call(
        forward_kernel,
        in_specs=[SMEM] * 3 + [VMEM] * 16,
        out_specs=[VMEM] * 4 + [SMEM] * 3,
        out_shape=[sds((256, T), f32)] * 4 + [sds((LIST,), i32), sds((LIST,), i32), sds((8,), i32)],
        scratch_shapes=STAGE
        + [
            pltpu.VMEM((QT + 1, T, T), f32),
            pltpu.VMEM((8, T), f32),
            pltpu.VMEM((T, T), f32),
            pltpu.VMEM((8, T), f32),
            pltpu.VMEM((8, T), i32),
            pltpu.SMEM((8, T), i32),
            pltpu.SemaphoreType.DMA,
        ],
        compiler_params=params(),
        cost_estimate=cost(1e9 * 6, 6 << 20),
        name="attend",
    )(ids, table, lengths, *parts)


def middle_kernel(ids, cot, out_proj, gate, slope, *refs):
    ins, (mixed, grad_gate), g_refs = refs[:4], refs[4:6], refs[6:10]
    att, back = refs[10], refs[11]
    z = ids[1]
    for t in range(4):
        att[(z + 4 - t) % 4] = ins[t][...]
    whole = jnp.concatenate([att[h] for h in range(4)], axis=1)
    normed, inverse = norm_rows(whole)
    gates = jnp.concatenate([gate[h] for h in range(4)], axis=1).astype(f32)
    mixed[...] = (normed * gates).astype(bf16)
    grad_mix = lax.dot_general(cot[...], out_proj[...], NT_DIMS, preferred_element_type=f32)
    gate_slope = jnp.concatenate([slope[h] for h in range(4)], axis=1).astype(f32)
    grad_gate[...] = (grad_mix * normed * gate_slope).astype(bf16)
    grad = norm_back(grad_mix * gates, normed, inverse).astype(bf16)
    for h in range(4):
        back[h] = grad[:, h * T : (h + 1) * T]
    for s in range(4):
        g_refs[s][...] = back[(z + s) % 4]


def middle(ids, cot, out_proj, gate, slope, parts):
    return pl.pallas_call(
        middle_kernel,
        grid=(1,),
        in_specs=[
            SMEM,
            pl.BlockSpec((256, 1024), lambda i: (0, 0)),
            pl.BlockSpec((512, 1024), lambda i: (0, 0)),
            pl.BlockSpec((4, 256, T), lambda i: (0, 0, 0)),
            pl.BlockSpec((None, 4, 256, T), lambda i: (0, 0, 0, 0)),
        ]
        + [pl.BlockSpec((256, T), lambda i: (0, 0))] * 4,
        out_specs=[pl.BlockSpec((256, 512), lambda i: (0, 0))] * 2
        + [pl.BlockSpec((256, T), lambda i: (0, 0))] * 4,
        out_shape=[sds((256, 512), bf16)] * 2 + [sds((256, T), bf16)] * 4,
        scratch_shapes=[pltpu.VMEM((4, 256, T), f32), pltpu.VMEM((4, 256, T), bf16)],
        compiler_params=params(),
        cost_estimate=cost(2 * 256 * 512 * 1024, 4 << 20),
        name="middle",
    )(ids, cot, out_proj, gate, slope, *parts)


def output_kernel(ids, tokens, cot, out_proj, mixed, output, mine, *theirs):
    y, z, core, low, x = ids[0], ids[1], ids[2], ids[3] // 4, ids[3] % 4
    output[...] = (
        tokens[...].astype(f32) + jnp.dot(mixed[...], out_proj[...], preferred_element_type=f32)
    ).astype(bf16)
    r = lax.broadcasted_iota(i32, (512, 512), 1)
    c = lax.broadcasted_iota(i32, (512, 512), 0)
    r_x = ((r // 128) + x) % 4
    r_core = ((r // 64) % 2) ^ core
    r_z = (((r // 16) % 4) + z) % 4
    r_y = ((r // 8) % 2) ^ y
    r_low = ((r // 4) % 2) ^ low
    source = (r_low * 4 + r_x) * 64 + r_y * 32 + r_z * 8 + r_core * 4 + r % 4
    pick = jnp.where(c == source, 1.0, 0.0).astype(bf16)
    moved = jnp.dot(mixed[...], pick, preferred_element_type=f32).astype(bf16)
    part = lax.dot_general(moved, cot[...], TN_DIMS, preferred_element_type=f32)
    mine[...] = part[:T]
    for i in range(3):
        theirs[i][...] = part[(i + 1) * T : (i + 2) * T].astype(bf16)


def finish_output(ids, tokens, cot, out_proj, mixed):
    return pl.pallas_call(
        output_kernel,
        in_specs=[SMEM] + [VMEM] * 4,
        out_specs=[VMEM] * 5,
        out_shape=[sds((256, 1024), bf16), sds((T, 1024), f32)] + [sds((T, 1024), bf16)] * 3,
        compiler_params=params(),
        cost_estimate=cost(6 * 256 * 512 * 1024, 5 << 20),
        name="finish_output",
    )(ids, tokens, cot, out_proj, mixed)


def backward_kernel(ids, table, lengths, far, near, counts, *refs):
    ins, got_grads, outs = refs[:16], refs[16:20], refs[20:26]
    mine_s, mine_o, theirs_s, theirs_o, dq_out, rab_out = outs
    keys, values, queries, tq, tk, start, grads, grads_t, queries_t, dq, dkt, dvt, rab = refs[26:]
    y, z, core = ids[0], ids[1], ids[2]
    stage(ids, lengths, ins, keys, values, queries, tq, tk, start)
    for t in range(4):
        zz = (z + 4 - t) % 4
        for half in range(2):
            block = got_grads[t][half * T : (half + 1) * T, :].astype(f32) * 0.5
            grads[2 * zz + half] = block.astype(bf16)
            grads_t[2 * zz + half] = jnp.transpose(block).astype(bf16)
    for jj in range(QT):
        queries_t[jj] = jnp.transpose(queries[jj].astype(f32)).astype(bf16)
    grads[QT] = jnp.zeros((T, T), bf16)
    grads_t[QT] = jnp.zeros((T, T), bf16)
    queries_t[QT] = jnp.zeros((T, T), bf16)
    dq[...] = jnp.zeros(dq.shape, f32)
    dkt[...] = jnp.zeros(dkt.shape, f32)
    dvt[...] = jnp.zeros(dvt.shape, f32)
    rab[...] = jnp.zeros(rab.shape, f32)

    def fold(values_):
        return jnp.sum(values_.reshape(T // 8, 8, T), axis=0)

    def front(got):
        dots = [lax.dot_general(queries[j], keys[k], NT_DIMS, preferred_element_type=f32) for j, k, _ in got]
        wides = [lax.dot_general(grads[j], values[k], NT_DIMS, preferred_element_type=f32) for j, k, _ in got]
        return dots, wides

    def score(half, wide, keep):
        t = jnp.tanh(half)
        weight = half * t + half
        d_score = wide * ((1.0 + t) * (1.0 + half * (1.0 - t)))
        if keep is not None:
            weight = jnp.where(keep, weight, 0.0)
            d_score = jnp.where(keep, d_score, 0.0)
        return weight.astype(bf16), d_score

    def back(got, weights, scores):
        a = [jnp.dot(scores[u], keys[got[u][1]], preferred_element_type=f32) for u in range(len(got))]
        b = [jnp.dot(queries_t[got[u][0]], scores[u], preferred_element_type=f32) for u in range(len(got))]
        c = [jnp.dot(grads_t[got[u][0]], weights[u], preferred_element_type=f32) for u in range(len(got))]
        for u, (jj, k, _) in enumerate(got):
            dq[jj] += a[u]
            dkt[k] += b[u]
            dvt[k] += c[u]

    def far_step(i, _):
        got = unpack(far, i, FAR_U)
        dots, wides = front(got)
        weights, scores, sums = [], [], []
        for u, (jj, k, bottom) in enumerate(got):
            bias, over1, over2 = bias_far(tq[jj] - tk[k][0:1, :], table, bottom)
            weight, d_score = score(dots[u] * (0.5 * SCALE) + bias, wides[u], None)
            weights.append(weight)
            scores.append(d_score.astype(bf16))
            sums.append((fold(d_score), fold(jnp.where(over1, d_score, 0.0)), fold(jnp.where(over2, d_score, 0.0))))
        back(got, weights, scores)
        for (jj, k, bottom), (sum0, sum1, sum2) in zip(got, sums):
            rab[bottom] += sum0 - sum1
            rab[bottom + 1] += sum1 - sum2
            rab[bottom + 2] += sum2
        return 0

    def near_step(i, _):
        got = unpack(near, i, NEAR_U)
        dots, wides = front(got)
        weights, scores = [], []
        sums = [jnp.zeros((8, T), f32)] * BUCKETS
        for u, (jj, k, _) in enumerate(got):
            gap = tq[jj] - tk[k][0:1, :]
            half = dots[u] * (0.5 * SCALE) + bias_near(gap, table)
            weight, d_score = score(half, wides[u], keep_near(ids, start[jj], jj, k))
            weights.append(weight)
            scores.append(d_score.astype(bf16))
            sums[0] = sums[0] + fold(d_score)
            for j in range(1, BUCKETS):
                sums[j] = sums[j] + fold(jnp.where(gap >= float(2**j - 1), d_score, 0.0))
        back(got, weights, scores)
        for j in range(BUCKETS - 1):
            rab[j] += sums[j] - sums[j + 1]
        rab[BUCKETS - 1] += sums[BUCKETS - 1]
        return 0

    lax.fori_loop(0, counts[0], far_step, 0)
    lax.fori_loop(0, counts[1], near_step, 0)
    for other in range(2):
        for s in range(4):
            base = (y if other == 0 else 1 - y) * 8 + ((z + s) % 4) * 2
            for side in range(2):
                dev = base + (core if side == 0 else 1 - core)
                ref = ((mine_s, theirs_s), (mine_o, theirs_o))[other][side]
                for half in range(2):
                    tile = dev if half == 0 else 2 * DEVS - 1 - dev
                    ref[s, 0:T, half * T : (half + 1) * T] = (dkt[tile] * SCALE).astype(bf16)
                    ref[s, T:, half * T : (half + 1) * T] = (dvt[tile] * 2.0).astype(bf16)
    for s in range(4):
        zz = (z + s) % 4
        for half in range(2):
            dq_out[s, :, half * T : (half + 1) * T] = (dq[2 * zz + half] * SCALE).astype(bf16)
    for b in range(16):
        if b < BUCKETS:
            rab_out[b : b + 1, :] = jnp.sum(rab[b], axis=0, keepdims=True)
        else:
            rab_out[b : b + 1, :] = jnp.zeros((1, T), f32)


def attend_back(ids, table, lengths, lists, parts, grads):
    return pl.pallas_call(
        backward_kernel,
        in_specs=[SMEM] * 6 + [VMEM] * 20,
        out_specs=[VMEM] * 6,
        out_shape=[sds((4, 256, 256), bf16)] * 4 + [sds((4, T, 256), bf16), sds((16, T), f32)],
        scratch_shapes=STAGE
        + [
            pltpu.VMEM((QT + 1, T, T), bf16),
            pltpu.VMEM((QT + 1, T, T), bf16),
            pltpu.VMEM((QT + 1, T, T), bf16),
            pltpu.VMEM((QT + 1, T, T), f32),
            pltpu.VMEM((TILES + 1, T, T), f32),
            pltpu.VMEM((TILES + 1, T, T), f32),
            pltpu.VMEM((16, 8, T), f32),
        ],
        compiler_params=params(),
        cost_estimate=cost(1e9 * 12, 8 << 20),
        name="attend_back",
    )(ids, table, lengths, *lists, *parts, *grads)


def combine_kernel(mine_s, mine_o, got_s, got_o, dq, proj_own, proj_got, *outs):
    proj = proj_own[...] + proj_got[...].astype(f32)
    for s in range(4):
        outs[s][0:256, :] = (mine_s[s].astype(f32) + got_s[s].astype(f32)).astype(bf16)
        outs[s][256:384, :] = dq[s]
        outs[4 + s][0:256, :] = (mine_o[s].astype(f32) + got_o[s].astype(f32)).astype(bf16)
        for other in range(2):
            block = proj[s * 16 + other * 8 : s * 16 + other * 8 + 8, :]
            block = jnp.concatenate([block[:, c * 256 : (c + 1) * 256] for c in range(4)], axis=0)
            outs[4 * other + s][384 - 128 * other :, :] = block.astype(bf16)


def combine(mine_s, mine_o, got_s, got_o, dq, proj_own, proj_got):
    return pl.pallas_call(
        combine_kernel,
        in_specs=[VMEM] * 7,
        out_specs=[VMEM] * 8,
        out_shape=[sds((416, 256), bf16)] * 4 + [sds((288, 256), bf16)] * 4,
        compiler_params=params(),
        cost_estimate=cost(1 << 20, 5 << 20),
        name="combine",
    )(mine_s, mine_o, got_s, got_o, dq, proj_own, proj_got)


def collect_kernel(*refs):
    ins, keep, give = refs[:8], refs[8], refs[9]
    total = ins[0][...].astype(f32)
    for ref in ins[1:]:
        total = total + ref[...].astype(f32)
    for c in range(4):
        keep[:, c * 256 : (c + 1) * 256] = total[c * 8 : c * 8 + 4, :]
        give[:, c * 256 : (c + 1) * 256] = total[c * 8 + 4 : c * 8 + 8, :]


def collect(same, other):
    return pl.pallas_call(
        collect_kernel,
        grid=(1,),
        in_specs=[pl.BlockSpec((32, 256), lambda i: (12, 0))] * 4
        + [pl.BlockSpec((32, 256), lambda i: (8, 0))] * 4,
        out_specs=[pl.BlockSpec((4, 1024), lambda i: (0, 0))] * 2,
        out_shape=[sds((4, 1024), f32)] * 2,
        cost_estimate=cost(1 << 16, 1 << 18),
        name="collect",
    )(*same, *other)


def final_kernel(ids, tokens, cot, in_proj, slope, grad_gate, *refs):
    same, other, grad_in, grad_pre, grad_normed = refs[:4], refs[4:8], refs[8], refs[9], refs[10]
    step = pl.program_id(0)
    z = ids[1]

    @pl.when(step == 0)
    def _():
        grad_pre[:, 0:512] = grad_gate[...]
        for t in range(4):
            head = (z + 4 - t) % 4
            column = lambda kind: pl.ds(pl.multiple_of(kind * 512 + head * T, T), T)
            total = same[t][0:256, :].astype(f32) + other[t][0:256, :].astype(f32)
            for half in range(2):
                rows = slice(half * T, (half + 1) * T)
                key = jnp.transpose(total[0:T, rows])
                value = jnp.transpose(total[T:, rows])
                query = same[t][256:384, rows].astype(f32)
                for kind, part in ((1, value), (2, query), (3, key)):
                    grad_pre[rows, column(kind)] = (
                        part * slope[kind, head, rows, :].astype(f32)
                    ).astype(bf16)

    grad_normed[step] = lax.dot_general(
        grad_pre[...], in_proj[...], NT_DIMS, preferred_element_type=f32
    )

    @pl.when(step == 3)
    def _():
        normed, inverse = norm_rows(tokens[...].astype(f32))
        upstream = jnp.concatenate([grad_normed[i] for i in range(4)], axis=1)
        grad_in[...] = (cot[...].astype(f32) + norm_back(upstream, normed, inverse)).astype(bf16)


def finish_grad(ids, tokens, cot, in_proj, slope, grad_gate, same, other):
    whole = lambda shape: pl.BlockSpec(shape, lambda s: (0,) * len(shape))
    return pl.pallas_call(
        final_kernel,
        grid=(4,),
        in_specs=[
            SMEM,
            whole((256, 1024)),
            whole((256, 1024)),
            pl.BlockSpec((256, 2048), lambda s: (s, 0)),
            whole((4, 4, 256, T)),
            whole((256, 512)),
        ]
        + [whole((384, 256))] * 4
        + [whole((256, 256))] * 4,
        out_specs=whole((256, 1024)),
        out_shape=sds((256, 1024), bf16),
        scratch_shapes=[pltpu.VMEM((256, 2048), bf16), pltpu.VMEM((4, 256, 256), f32)],
        compiler_params=params(),
        cost_estimate=cost(2 * 256 * 1024 * 2048, 8 << 20),
        name="finish_grad",
    )(ids, tokens, cot, in_proj, slope, grad_gate, *same, *other)


def move(y_xor, z_shift, core_xor):
    pairs = []
    for dev in range(DEVS):
        y, z, core = dev // 8, (dev // 2) % 4, dev % 2
        target = (y ^ y_xor) * 8 + ((z + z_shift) % 4) * 2 + (core ^ core_xor)
        pairs.append((dev, target))
    return pairs


def send(x, y_xor, z_shift, core_xor):
    return lax.ppermute(x, "ctx", move(y_xor, z_shift, core_xor))


def send_x(part, shift):
    return lax.ppermute(part, "dp", [(d, d // 4 * 4 + (d + shift) % 4) for d in range(8)])


def sum_rab(part):
    row = jnp.sum(part, axis=1)
    row = jnp.concatenate([row, jnp.zeros((T - 16,), f32)])
    every = lax.all_to_all(jnp.broadcast_to(row[None], (T, T)), ("dp", "ctx"), 0, 0, tiled=True)
    sums = jnp.sum(every.reshape(8, 2, 4, 2, T)[..., :BUCKETS], axis=(0, 1, 3))
    return sums.T


def on_device(tokens, cotangent, in_proj, out_proj, rab_time, seq_lengths, block_mask, time_bucket):
    ctx = lax.axis_index("ctx")
    dp = lax.axis_index("dp")
    y, z, core = ctx // 8, (ctx // 2) % 4, ctx % 2
    ids = jnp.stack([y, z, core, dp]).astype(i32)
    lengths = seq_lengths.reshape(3)
    limits = [2.0**j - 1.0 for j in range(BUCKETS)] + [1e9] * 4
    head_bias = lax.dynamic_slice_in_dim(rab_time, z, 1, 1).reshape(BUCKETS) * 0.5
    table = jnp.concatenate([head_bias, jnp.zeros((4,), f32), jnp.array(limits, f32)])
    mask = block_mask.reshape(2, 16, 2)
    mask = jnp.concatenate([mask[:, :, 0], mask[:, ::-1, 1], jnp.zeros((2, 96), i32)], axis=1)
    meta = jnp.stack([time_bucket // 128, time_bucket % 128, mask.reshape(256)])
    meta = jnp.pad(meta, ((0, 13), (0, 0))).astype(bf16)

    made = project(ids, tokens, meta, in_proj)
    gate, slope, full, pairs = made[0], made[1], made[2:6], made[6:10]
    own = [full[0]] + [send(full[s], 0, s, 0) for s in (1, 2, 3)]
    across = [send(pairs[s], 1, s, 0) for s in range(4)]
    own_twin = [send(part, 0, 0, 1) for part in own]
    across_twin = [send(part, 0, 0, 1) for part in across]
    parts = own + own_twin + across + across_twin
    done = attend(ids, table, lengths, parts)
    blocks, lists = done[:4], done[4:]

    heads = [blocks[0]] + [send(blocks[s], 0, s, 0) for s in (1, 2, 3)]
    between = middle(ids, cotangent, out_proj, gate, slope, heads)
    mixed, grad_gate, grads = between[0], between[1], between[2:]
    grads = [grads[0]] + [send(grads[s], 0, s, 0) for s in (1, 2, 3)]
    made = finish_output(ids, tokens, cotangent, out_proj, mixed)
    output, proj = made[0], made[1]
    for s in (1, 2, 3):
        proj = proj + send_x(made[1 + s], s).astype(f32)
    proj_own = proj[:64]
    proj_got = send(proj[64:].astype(bf16), 0, 0, 1)

    mine_s, mine_o, theirs_s, theirs_o, dq, rab = attend_back(ids, table, lengths, lists, parts, grads)
    got_o = send(theirs_o, 0, 0, 1)
    got_s = send(theirs_s, 0, 0, 1)
    messages = combine(mine_s, mine_o, got_s, got_o, dq, proj_own, proj_got)
    messages, rab = lax.optimization_barrier((messages, rab))
    same = [messages[0]] + [send(messages[s], 0, s, 0) for s in (1, 2, 3)]
    other = [send(messages[4 + s], 1, s, 0) for s in range(4)]
    rab_grad = sum_rab(rab)
    keep, give = collect(same, other)
    proj_grad = keep + lax.ppermute(give, "dp", [(d, d ^ 4) for d in range(8)])
    grad_in = finish_grad(ids, tokens, cotangent, in_proj, slope, grad_gate, same, other)
    return output, grad_in, proj_grad, rab_grad


def solution(mesh):
    rows = P(("dp", "ctx"), None)
    placed = (rows, rows, P(), P(), P(), P("dp", None), P("dp", "ctx", None), P(("dp", "ctx")))
    return jax.shard_map(
        on_device,
        mesh=mesh,
        in_specs=placed,
        out_specs=(rows, rows, rows, P()),
        check_vma=False,
    )
```

time: 194 us -> 145 us (0.75)
  Pallas kernels: 68.5 us -> 43.7 us
  starting transfers between devices: 78 us -> 60.8 us
  waiting for transfers between devices: 31.8 us -> 25.7 us
    pallas_call x4, Pallas kernels: 47.5 us -> 22.8 us  [the longest x1 10.6 us: attend_back(): pl.pallas_call(backward_kernel, in_specs=[SMEM] * 6 + [VMEM] * 20, out_sp...]
    ppermute x45 -> x31, starting transfers between devices: 58.2 us -> 42.6 us  [send(): return lax.ppermute(x, 'ctx', move(y_xor, z_shift, core_xor))]
    ppermute x14 -> x4, starting transfers between devices: 19.8 us -> 7.07 us  [the longest x3 6.28 us: send_x(): lax.ppermute(part, 'dp', [(d, d // 4 * 4 + (d + shift) % 4) for d in rang...]
    all_to_all x0 -> x1, starting transfers between devices: none -> 11.2 us  [sum_rab(): lax.all_to_all(jnp.broadcast_to(row[None], (T, T)), ('dp', 'ctx'), 0, 0,...]
    ppermute x45 -> x31, waiting for transfers between devices: 31.8 us -> 24.7 us  [send(): return lax.ppermute(x, 'ctx', move(y_xor, z_shift, core_xor))]
    unnamed x68 -> x71, local copies, waits for them, and re-layouts: 3.73 us -> 4.56 us
  transfers between devices with their start and end apart: 59 -> 36, of which waited for: 17 -> 12; matrix products, arithmetic and copies ran while one was open for 3% -> 3% of each run, Pallas kernels for 21% -> 15%
where the time goes in v2:
time: 145 us; the launch traced here: 143 us
  starting transfers between devices  60.8 us (42%)
  Pallas kernels  43.7 us (30%)
  waiting for transfers between devices  25.7 us (18%)
  local copies, waits for them, and re-layouts  6.93 us (5%)
  other arithmetic  4.83 us (3%)
    ppermute x31, starting transfers between devices, send(): return lax.ppermute(x, 'ctx', move(y_xor, z_shift, core_xor))  42.6 us
    ppermute x31, waiting for transfers between devices, send(): return lax.ppermute(x, 'ctx', move(y_xor, z_shift, core_xor))  24.7 us
    all_to_all x1, starting transfers between devices, sum_rab(): lax.all_to_all(jnp.broadcast_to(row[None], (T, T)), ('dp', 'ctx'), 0, 0,...  11.2 us
    pallas_call x1, Pallas kernels, attend_back(): pl.pallas_call(backward_kernel, in_specs=[SMEM] * 6 + [VMEM] * 20, out_sp...  10.6 us
    pallas_call x1, Pallas kernels, attend(): pl.pallas_call(forward_kernel, in_specs=[SMEM] * 3 + [VMEM] * 16, out_spe...  7.83 us
    pallas_call x1, Pallas kernels, project(): pl.pallas_call(project_kernel, grid_spec=pltpu.PrefetchScalarGridSpec(num...  7.26 us
    pallas_call x1, Pallas kernels, finish_grad(): pl.pallas_call(final_kernel, grid=(4,), in_specs=[SMEM, whole((256, 1024)...  7 us
    ppermute x3, starting transfers between devices, send_x(): lax.ppermute(part, 'dp', [(d, d // 4 * 4 + (d + shift) % 4) for d in rang...  6.28 us
  transfers between devices with their start and end apart: 36, of which 12 were waited for; matrix products, arithmetic and copies ran while one was open for 3% of the time, Pallas kernels for 15%

profile of v2, /device:TPU:24, one launch (start us, length us, event | category | flops | bytes accessed | tf_op | source)
XLA Modules:
  0.0 143.1 jit_solution(353215600616423652)
XLA Ops:
  3.7 7.3 %project.1 = (bf16[4,256,128]{2,1,0:T(8,128)(2,1)}, bf16[4,4,256,128]{3,2,1,0:T(8,128)(2,1)}, bf16[272,384]{1,0:T(8,128)(2,1)}, bf16[272,384]{1,0:T(8,128)(2,1)}...) custom-call(s32[4]{0:T(128)} %pad_add_fusion.ids, ...), custom_call_target="tpu_custom_call" | custom-call | flops 1073741824 | bytes 7340032 | tf_op jit(solution)/shard_map/project/pallas_call | solution.py:93
  11.0 1.3 collective-permute-start.7
  12.3 3.7 %collective-permute-start.8 = (bf16[272,256]{1,0:T(8,128)(2,1)}, bf16[272,256]{1,0:T(8,128)(2,1)S(1)}, u32[]{:S(2)}, u32[]{:S(2)}) collective-permute-start(bf16[272,256]{1,0:T(8,128)(2,1)} %get-tuple-element.64), channel_id=1, source_target_pairs={{0,10},{1,11},{2,12},{3,13},{4,14},{5,15},{6,8},{7,9},{8,2},{9,3},... | collective-permute-start | bytes 417800 | tf_op jit(solution)/shard_map/ppermute | solution.py:644
  15.9 4.3 %collective-permute-start.9 = (bf16[272,256]{1,0:T(8,128)(2,1)}, bf16[272,256]{1,0:T(8,128)(2,1)S(1)}, u32[]{:S(2)}, u32[]{:S(2)}) collective-permute-start(bf16[272,256]{1,0:T(8,128)(2,1)} %get-tuple-element.65), channel_id=1, source_target_pairs={{0,12},{1,13},{2,14},{3,15},{4,8},{5,9},{6,10},{7,11},{8,4},{9,5},... | collective-permute-start | bytes 417800 | tf_op jit(solution)/shard_map/ppermute | solution.py:644
  20.2 5.0 %collective-permute-start.10 = (bf16[272,256]{1,0:T(8,128)(2,1)}, bf16[272,256]{1,0:T(8,128)(2,1)S(1)}, u32[]{:S(2)}, u32[]{:S(2)}) collective-permute-start(bf16[272,256]{1,0:T(8,128)(2,1)} %get-tuple-element.66), channel_id=1, source_target_pairs={{0,14},{1,15},{2,8},{3,9},{4,10},{5,11},{6,12},{7,13},{8,6},{9,7},... | collective-permute-start | bytes 417800 | tf_op jit(solution)/shard_map/ppermute | solution.py:644
  26.6 1.9 %collective-permute-done.9.refs_10_ = bf16[272,256]{1,0:T(8,128)(2,1)S(1)} collective-permute-done((bf16[272,256]{1,0:T(8,128)(2,1)}, bf16[272,256]{1,0:T(8,128)(2,1)S(1)}, u32[]{:S(2)}, u32[]{:S(2)}) %collective-permute-start.9) | collective-permute-done | bytes 139296 | tf_op jit(solution)/shard_map/ppermute | solution.py:644
  29.0 7.6 %collective-permute-done.refs_1_ = bf16[272,384]{1,0:T(8,128)(2,1)S(1)} collective-permute-done((bf16[272,384]{1,0:T(8,128)(2,1)}, bf16[272,384]{1,0:T(8,128)(2,1)S(1)}, u32[]{:S(2)}, u32[]{:S(2)}) %collective-permute-start) | collective-permute-done | bytes 208928 | tf_op jit(solution)/shard_map/ppermute | solution.py:644
  37.1 1.4 collective-permute-done.2.refs_3_
  41.8 7.8 %attend.1 = (f32[256,128]{1,0:T(8,128)}, f32[256,128]{1,0:T(8,128)}, f32[256,128]{1,0:T(8,128)}, f32[256,128]{1,0:T(8,128)}, s32[160]{0:T(256)}, /*index=5*/s32[160]{0:T(256)}, s32[8]{0:T(128)}) custom-call(s32[4]{0:T(128)} %pad_add_fusion.ids, f32[32]{0:T(128)} %pad_maximum_fusion.table, s32[3]{0:T(128)} %bitcast.18, ...), custom_call_target="tpu_custom_call" | custom-call | flops 6000000000 | bytes 6291456 | tf_op jit(solution)/shard_map/attend/pallas_call | solution.py:304
  49.6 1.9 %collective-permute-start.15 = (f32[256,128]{1,0:T(8,128)}, f32[256,128]{1,0:T(8,128)S(1)}, u32[]{:S(2)}, u32[]{:S(2)}) collective-permute-start(f32[256,128]{1,0:T(8,128)} %get-tuple-element.68), channel_id=1, source_target_pairs={{0,2},{1,3},{2,4},{3,5},{4,6},{5,7},{6,0},{7,1},{8,10},{9,11},{10,... | collective-permute-start | bytes 393224 | tf_op jit(solution)/shard_map/ppermute | solution.py:644
  51.5 1.8 %collective-permute-start.16 = (f32[256,128]{1,0:T(8,128)}, f32[256,128]{1,0:T(8,128)S(1)}, u32[]{:S(2)}, u32[]{:S(2)}) collective-permute-start(f32[256,128]{1,0:T(8,128)} %get-tuple-element.69), channel_id=1, source_target_pairs={{0,4},{1,5},{2,6},{3,7},{4,0},{5,1},{6,2},{7,3},{8,12},{9,13},{10,... | collective-permute-start | bytes 393224 | tf_op jit(solution)/shard_map/ppermute | solution.py:644
  53.3 1.5 %collective-permute-start.17 = (f32[256,128]{1,0:T(8,128)}, f32[256,128]{1,0:T(8,128)S(1)}, u32[]{:S(2)}, u32[]{:S(2)}) collective-permute-start(f32[256,128]{1,0:T(8,128)} %get-tuple-element.70), channel_id=1, source_target_pairs={{0,6},{1,7},{2,0},{3,1},{4,2},{5,3},{6,4},{7,5},{8,14},{9,15},{10,... | collective-permute-start | bytes 393224 | tf_op jit(solution)/shard_map/ppermute | solution.py:644
  54.8 2.5 %collective-permute-done.15.refs_1_ = f32[256,128]{1,0:T(8,128)S(1)} collective-permute-done((f32[256,128]{1,0:T(8,128)}, f32[256,128]{1,0:T(8,128)S(1)}, u32[]{:S(2)}, u32[]{:S(2)}) %collective-permute-start.15) | collective-permute-done | bytes 131104 | tf_op jit(solution)/shard_map/ppermute | solution.py:644
  57.3 3.2 %collective-permute-done.16.refs_2_ = f32[256,128]{1,0:T(8,128)S(1)} collective-permute-done((f32[256,128]{1,0:T(8,128)}, f32[256,128]{1,0:T(8,128)S(1)}, u32[]{:S(2)}, u32[]{:S(2)}) %collective-permute-start.16) | collective-permute-done | bytes 131104 | tf_op jit(solution)/shard_map/ppermute | solution.py:644
  61.6 3.1 %middle.1 = (bf16[256,512]{1,0:T(8,128)(2,1)}, bf16[256,512]{1,0:T(8,128)(2,1)}, bf16[256,128]{1,0:T(8,128)(2,1)}, bf16[256,128]{1,0:T(8,128)(2,1)}, bf16[256,128]{1,0:T(8,128)(2,1)}, /*index=5*/bf16[256,128]{1,0:T(8,128)(2,1)}) custom-call(s32[4]{0:T(128)} %pad_add_fusion.ids, bf16[256,1024]{1,0:T(8,128)(2,1)} %cot.5, bf16[512,1024]{1,0:T(8,128)(2,1)} %out_proj.3, ...), custom_call_target="tpu_custom_call" | custom-call | flops 268435456 | bytes 4194304 | tf_op jit(solution)/shard_map/middle/pallas_call | solution.py:346
  64.7 1.7 %collective-permute-start.18 = (bf16[256,128]{1,0:T(8,128)(2,1)}, bf16[256,128]{1,0:T(8,128)(2,1)S(1)}, u32[]{:S(2)}, u32[]{:S(2)}) collective-permute-start(bf16[256,128]{1,0:T(8,128)(2,1)} %get-tuple-element.78), channel_id=1, source_target_pairs={{0,2},{1,3},{2,4},{3,5},{4,6},{5,7},{6,0},{7,1},{8,10},{9,11},{10,... | collective-permute-start | bytes 196616 | tf_op jit(solution)/shard_map/ppermute | solution.py:644
  66.5 2.4 %collective-permute-start.19 = (bf16[256,128]{1,0:T(8,128)(2,1)}, bf16[256,128]{1,0:T(8,128)(2,1)S(1)}, u32[]{:S(2)}, u32[]{:S(2)}) collective-permute-start(bf16[256,128]{1,0:T(8,128)(2,1)} %get-tuple-element.79), channel_id=1, source_target_pairs={{0,4},{1,5},{2,6},{3,7},{4,0},{5,1},{6,2},{7,3},{8,12},{9,13},{10,... | collective-permute-start | bytes 196616 | tf_op jit(solution)/shard_map/ppermute | solution.py:644
  70.0 3.6 %finish_output.1 = (bf16[256,1024]{1,0:T(8,128)(2,1)}, f32[128,1024]{1,0:T(8,128)}, bf16[128,1024]{1,0:T(8,128)(2,1)}, bf16[128,1024]{1,0:T(8,128)(2,1)}, bf16[128,1024]{1,0:T(8,128)(2,1)}) custom-call(s32[4]{0:T(128)} %pad_add_fusion.ids, bf16[256,1024]{1,0:T(8,128)(2,1)} %tokens.5, bf16[256,1024]{1,0:T(8,128)(2,1)} %cot.5, bf16[512,1024]{1,0:T(8,128)(2,1)} %out_proj.3, ...), custom_call_target="tpu_custom_call" | custom-call | flops 805306368 | bytes 5242880 | tf_op jit(solution)/shard_map/finish_output/pallas_call | solution.py:389
  74.7 3.8 %collective-permute-start.24 = (bf16[128,1024]{1,0:T(8,128)(2,1)}, bf16[128,1024]{1,0:T(8,128)(2,1)S(1)}, u32[]{:S(2)}, u32[]{:S(2)}) collective-permute-start(bf16[128,1024]{1,0:T(8,128)(2,1)} %get-tuple-element.88), channel_id=1, source_target_pairs={{0,32},{16,48},{32,0},{48,16},{64,96},{80,112},{96,64},{112,80},{1... | collective-permute-start | bytes 786440 | tf_op jit(solution)/shard_map/ppermute | solution.py:648
  78.5 1.4 collective-permute-start.25
  80.5 10.6 %attend_back.1 = (bf16[4,256,256]{2,1,0:T(8,128)(2,1)}, bf16[4,256,256]{2,1,0:T(8,128)(2,1)}, bf16[4,256,256]{2,1,0:T(8,128)(2,1)}, bf16[4,256,256]{2,1,0:T(8,12...) custom-call(s32[4]{0:T(128)} %pad_add_fusion.ids, f32[32]{0:T(128)} %pad_maximum_fusion.table, s32[3]{0:T(128)} %bitcast.19, ...), custom_call_target="tpu_custom_call" | custom-call | flops 12000000000 | bytes 8388608 | tf_op jit(solution)/shard_map/attend_back/pallas_call | solution.py:509
  95.0 2.9 %combine.1 = (bf16[416,256]{1,0:T(8,128)(2,1)}, bf16[416,256]{1,0:T(8,128)(2,1)}, bf16[416,256]{1,0:T(8,128)(2,1)}, bf16[416,256]{1,0:T(8,128)(2,1)}, bf16[288,2...) custom-call(bf16[4,256,256]{2,1,0:T(8,128)(2,1)} %get-tuple-element.81.mine_s, ...), custom_call_target="tpu_custom_call" | custom-call | flops 1048576 | bytes 5242880 | tf_op jit(solution)/shard_map/combine/pallas_call | solution.py:543
  97.9 2.5 %collective-permute-start.30 = (bf16[288,256]{1,0:T(8,128)(2,1)}, bf16[288,256]{1,0:T(8,128)(2,1)S(1)}, u32[]{:S(2)}, u32[]{:S(2)}) collective-permute-start(bf16[288,256]{1,0:T(8,128)(2,1)} %get-tuple-element.103), channel_id=1, source_target_pairs={{0,8},{1,9},{2,10},{3,11},{4,12},{5,13},{6,14},{7,15},{8,0},{9,1},... | collective-permute-start | bytes 442376 | tf_op jit(solution)/shard_map/ppermute | solution.py:644
  100.4 1.4 collective-permute-start.31
  102.2 3.4 %collective-permute-start.28 = (bf16[416,256]{1,0:T(8,128)(2,1)}, bf16[416,256]{1,0:T(8,128)(2,1)S(1)}, u32[]{:S(2)}, u32[]{:S(2)}) collective-permute-start(bf16[416,256]{1,0:T(8,128)(2,1)} %get-tuple-element.101), channel_id=1, source_target_pairs={{0,4},{1,5},{2,6},{3,7},{4,0},{5,1},{6,2},{7,3},{8,12},{9,13},{10,... | collective-permute-start | bytes 638984 | tf_op jit(solution)/shard_map/ppermute | solution.py:644
  106.4 11.2 %all-to-all-start = ((f32[128,1,128]{2,1,0:T(1,128)}), f32[128,1,128]{2,1,0:T(1,128)S(1)}, u32[]{:S(2)}, u32[]{:S(2)}) async-start(f32[128,1,128]{2,1,0:T(1,128)} %broadcast_in_dim.5), calls=%async_computation | async-start | bytes 131072 | tf_op jit(solution)/shard_map/all_to_all | solution.py:654
  117.6 4.3 %collective-permute-start.32 = (bf16[288,256]{1,0:T(8,128)(2,1)}, bf16[288,256]{1,0:T(8,128)(2,1)S(1)}, u32[]{:S(2)}, u32[]{:S(2)}) collective-permute-start(bf16[288,256]{1,0:T(8,128)(2,1)} %get-tuple-element.105), channel_id=1, source_target_pairs={{0,12},{1,13},{2,14},{3,15},{4,8},{5,9},{6,10},{7,11},{8,4},{9,5},... | collective-permute-start | bytes 442376 | tf_op jit(solution)/shard_map/ppermute | solution.py:644
  122.0 2.5 %collective-permute-start.33 = (bf16[288,256]{1,0:T(8,128)(2,1)}, bf16[288,256]{1,0:T(8,128)(2,1)S(1)}, u32[]{:S(2)}, u32[]{:S(2)}) collective-permute-start(bf16[288,256]{1,0:T(8,128)(2,1)} %get-tuple-element.106), channel_id=1, source_target_pairs={{0,14},{1,15},{2,8},{3,9},{4,10},{5,11},{6,12},{7,13},{8,6},{9,7},... | collective-permute-start | bytes 442376 | tf_op jit(solution)/shard_map/ppermute | solution.py:644
  126.1 2.0 %collective-permute-done.32.refs_6_ = bf16[288,256]{1,0:T(8,128)(2,1)S(1)} collective-permute-done((bf16[288,256]{1,0:T(8,128)(2,1)}, bf16[288,256]{1,0:T(8,128)(2,1)S(1)}, u32[]{:S(2)}, u32[]{:S(2)}) %collective-permute-start.32) | collective-permute-done | bytes 147488 | tf_op jit(solution)/shard_map/ppermute | solution.py:644
  128.1 3.6 %collective-permute-done.33.refs_7_ = bf16[288,256]{1,0:T(8,128)(2,1)S(1)} collective-permute-done((bf16[288,256]{1,0:T(8,128)(2,1)}, bf16[288,256]{1,0:T(8,128)(2,1)S(1)}, u32[]{:S(2)}, u32[]{:S(2)}) %collective-permute-start.33) | collective-permute-done | bytes 147488 | tf_op jit(solution)/shard_map/ppermute | solution.py:644
  133.2 1.5 %collect.1 = (f32[4,1024]{1,0:T(4,128)}, f32[4,1024]{1,0:T(4,128)}) custom-call(bf16[416,256]{1,0:T(8,128)(2,1)} %get-tuple-element.99.refs_0_, bf16[416,256]{1,0:T(8,128)(2,1)} %copy-done, bf16[416,256]{1,0:T(8,128)(2,1)} %copy-done.1, bf16[416,256]{1,0:T(8,128)(2,1)} %copy-done.2, bf16[288,256]{1,0:T(8,128)(2,1)} %copy-done.3, bf16[288,256]{1,0:T(8,128)(2,1)} %copy-done.4, ...), custom_call_target="tpu_custom_call" | custom-call | flops 65536 | bytes 262144 | tf_op jit(solution)/shard_map/collect/pallas_call | solution.py:565
  135.5 7.0 %finish_grad.1 = bf16[256,1024]{1,0:T(8,128)(2,1)} custom-call(s32[4]{0:T(128)} %pad_add_fusion.ids, bf16[256,1024]{1,0:T(8,128)(2,1)} %tokens.5, bf16[256,1024]{1,0:T(8,128)(2,1)} %cot.5, bf16[1024,2048]{1,0:T(8,128)(2,1)} %in_proj.1, bf16[4,4,256,128]{3,2,1,0:T(8,128)(2,1)} %get-tuple-element.58.slope, bf16[256,512]{1,0:T(8,128)(2,1)} %get-tuple-element.73.grad_gate, ...), custom_call_target="tpu_custom_call" | custom-call | flops 1073741824 | bytes 8388608 | tf_op jit(solution)/shard_map/finish_grad/pallas_call | solution.py:612
  (142 shorter events, 22.1 us)
Async XLA Ops:
  11.0 14.2 %collective-permute-start.7 = (bf16[272,256]{1,0:T(8,128)(2,1)}, bf16[272,256]{1,0:T(8,128)(2,1)S(1)}, u32[]{:S(2)}, u32[]{:S(2)}) collective-permute-start(bf16[272,256]{1,0:T(8,128)(2,1)} %get-tuple-element.63), channel_id=1, source_target_pairs={{0,8},{1,9},{2,10},{3,11},{4,12},{5,13},{6,14},{7,15},{8,0},{9,1},... | collective-permute-start | bytes 417800 | tf_op jit(solution)/shard_map/ppermute | solution.py:644
  12.3 13.7 %collective-permute-start.8 = (bf16[272,256]{1,0:T(8,128)(2,1)}, bf16[272,256]{1,0:T(8,128)(2,1)S(1)}, u32[]{:S(2)}, u32[]{:S(2)}) collective-permute-start(bf16[272,256]{1,0:T(8,128)(2,1)} %get-tuple-element.64), channel_id=1, source_target_pairs={{0,10},{1,11},{2,12},{3,13},{4,14},{5,15},{6,8},{7,9},{8,2},{9,3},... | collective-permute-start | bytes 417800 | tf_op jit(solution)/shard_map/ppermute | solution.py:644
  15.9 12.6 %collective-permute-start.9 = (bf16[272,256]{1,0:T(8,128)(2,1)}, bf16[272,256]{1,0:T(8,128)(2,1)S(1)}, u32[]{:S(2)}, u32[]{:S(2)}) collective-permute-start(bf16[272,256]{1,0:T(8,128)(2,1)} %get-tuple-element.65), channel_id=1, source_target_pairs={{0,12},{1,13},{2,14},{3,15},{4,8},{5,9},{6,10},{7,11},{8,4},{9,5},... | collective-permute-start | bytes 417800 | tf_op jit(solution)/shard_map/ppermute | solution.py:644
  20.2 16.4 %collective-permute-start = (bf16[272,384]{1,0:T(8,128)(2,1)}, bf16[272,384]{1,0:T(8,128)(2,1)S(1)}, u32[]{:S(2)}, u32[]{:S(2)}) collective-permute-start(bf16[272,384]{1,0:T(8,128)(2,1)} %get-tuple-element.60), channel_id=1, source_target_pairs={{0,2},{1,3},{2,4},{3,5},{4,6},{5,7},{6,0},{7,1},{8,10},{9,11},{10,... | collective-permute-start | bytes 626696 | tf_op jit(solution)/shard_map/ppermute | solution.py:644
  20.2 8.4 %collective-permute-start.10 = (bf16[272,256]{1,0:T(8,128)(2,1)}, bf16[272,256]{1,0:T(8,128)(2,1)S(1)}, u32[]{:S(2)}, u32[]{:S(2)}) collective-permute-start(bf16[272,256]{1,0:T(8,128)(2,1)} %get-tuple-element.66), channel_id=1, source_target_pairs={{0,14},{1,15},{2,8},{3,9},{4,10},{5,11},{6,12},{7,13},{8,6},{9,7},... | collective-permute-start | bytes 417800 | tf_op jit(solution)/shard_map/ppermute | solution.py:644
  25.2 11.4 %collective-permute-start.1 = (bf16[272,384]{1,0:T(8,128)(2,1)}, bf16[272,384]{1,0:T(8,128)(2,1)S(1)}, u32[]{:S(2)}, u32[]{:S(2)}) collective-permute-start(bf16[272,384]{1,0:T(8,128)(2,1)} %get-tuple-element.61), channel_id=1, source_target_pairs={{0,4},{1,5},{2,6},{3,7},{4,0},{5,1},{6,2},{7,3},{8,12},{9,13},{10,... | collective-permute-start | bytes 626696 | tf_op jit(solution)/shard_map/ppermute | solution.py:644
  26.0 12.5 %collective-permute-start.2 = (bf16[272,384]{1,0:T(8,128)(2,1)}, bf16[272,384]{1,0:T(8,128)(2,1)S(1)}, u32[]{:S(2)}, u32[]{:S(2)}) collective-permute-start(bf16[272,384]{1,0:T(8,128)(2,1)} %get-tuple-element.62), channel_id=1, source_target_pairs={{0,6},{1,7},{2,0},{3,1},{4,2},{5,3},{6,4},{7,5},{8,14},{9,15},{10,... | collective-permute-start | bytes 626696 | tf_op jit(solution)/shard_map/ppermute | solution.py:644
  28.5 10.0 %collective-permute-start.3 = (bf16[272,384]{1,0:T(8,128)(2,1)}, bf16[272,384]{1,0:T(8,128)(2,1)S(1)}, u32[]{:S(2)}, u32[]{:S(2)}) collective-permute-start(bf16[272,384]{1,0:T(8,128)(2,1)} %get-tuple-element.59.refs_0_), channel_id=1, source_target_pairs={{0,1},{1,0},{2,3},{3,2},{4,5},{5,4},{6,7},{7,6},{8,9},{9,8},{10,11... | collective-permute-start | bytes 626696 | tf_op jit(solution)/shard_map/ppermute | solution.py:644
  28.6 10.4 %collective-permute-start.11 = (bf16[272,256]{1,0:T(8,128)(2,1)S(1)}, bf16[272,256]{1,0:T(8,128)(2,1)S(1)}, u32[]{:S(2)}, u32[]{:S(2)}) collective-permute-start(bf16[272,256]{1,0:T(8,128)(2,1)S(1)} %collective-permute-done.7.refs_8_), channel_id=1, source_target_pairs={{0,1},{1,0},{2,3},{3,2},{4,5},{5,4},{6,7},{7,6},{8,9},{9,8},{10,11... | collective-permute-start | bytes 417800 | tf_op jit(solution)/shard_map/ppermute | solution.py:644
  36.6 2.5 %collective-permute-start.12 = (bf16[272,256]{1,0:T(8,128)(2,1)S(1)}, bf16[272,256]{1,0:T(8,128)(2,1)S(1)}, u32[]{:S(2)}, u32[]{:S(2)}) collective-permute-start(bf16[272,256]{1,0:T(8,128)(2,1)S(1)} %collective-permute-done.8.refs_9_), channel_id=1, source_target_pairs={{0,1},{1,0},{2,3},{3,2},{4,5},{5,4},{6,7},{7,6},{8,9},{9,8},{10,11... | collective-permute-start | bytes 417800 | tf_op jit(solution)/shard_map/ppermute | solution.py:644
  36.6 4.2 %collective-permute-start.13 = (bf16[272,256]{1,0:T(8,128)(2,1)S(1)}, bf16[272,256]{1,0:T(8,128)(2,1)S(1)}, u32[]{:S(2)}, u32[]{:S(2)}) collective-permute-start(bf16[272,256]{1,0:T(8,128)(2,1)S(1)} %collective-permute-done.9.refs_10_), channel_id=1, source_target_pairs={{0,1},{1,0},{2,3},{3,2},{4,5},{5,4},{6,7},{7,6},{8,9},{9,8},{10,11... | collective-permute-start | bytes 417800 | tf_op jit(solution)/shard_map/ppermute | solution.py:644
  38.5 2.3 %collective-permute-start.14 = (bf16[272,256]{1,0:T(8,128)(2,1)S(1)}, bf16[272,256]{1,0:T(8,128)(2,1)S(1)}, u32[]{:S(2)}, u32[]{:S(2)}) collective-permute-start(bf16[272,256]{1,0:T(8,128)(2,1)S(1)} %collective-permute-done.10.refs_11_), channel_id=1, source_target_pairs={{0,1},{1,0},{2,3},{3,2},{4,5},{5,4},{6,7},{7,6},{8,9},{9,8},{10,11... | collective-permute-start | bytes 417800 | tf_op jit(solution)/shard_map/ppermute | solution.py:644
  49.6 7.7 %collective-permute-start.15 = (f32[256,128]{1,0:T(8,128)}, f32[256,128]{1,0:T(8,128)S(1)}, u32[]{:S(2)}, u32[]{:S(2)}) collective-permute-start(f32[256,128]{1,0:T(8,128)} %get-tuple-element.68), channel_id=1, source_target_pairs={{0,2},{1,3},{2,4},{3,5},{4,6},{5,7},{6,0},{7,1},{8,10},{9,11},{10,... | collective-permute-start | bytes 393224 | tf_op jit(solution)/shard_map/ppermute | solution.py:644
  51.5 9.0 %collective-permute-start.16 = (f32[256,128]{1,0:T(8,128)}, f32[256,128]{1,0:T(8,128)S(1)}, u32[]{:S(2)}, u32[]{:S(2)}) collective-permute-start(f32[256,128]{1,0:T(8,128)} %get-tuple-element.69), channel_id=1, source_target_pairs={{0,4},{1,5},{2,6},{3,7},{4,0},{5,1},{6,2},{7,3},{8,12},{9,13},{10,... | collective-permute-start | bytes 393224 | tf_op jit(solution)/shard_map/ppermute | solution.py:644
  53.3 7.7 %collective-permute-start.17 = (f32[256,128]{1,0:T(8,128)}, f32[256,128]{1,0:T(8,128)S(1)}, u32[]{:S(2)}, u32[]{:S(2)}) collective-permute-start(f32[256,128]{1,0:T(8,128)} %get-tuple-element.70), channel_id=1, source_target_pairs={{0,6},{1,7},{2,0},{3,1},{4,2},{5,3},{6,4},{7,5},{8,14},{9,15},{10,... | collective-permute-start | bytes 393224 | tf_op jit(solution)/shard_map/ppermute | solution.py:644
  64.7 13.7 %collective-permute-start.18 = (bf16[256,128]{1,0:T(8,128)(2,1)}, bf16[256,128]{1,0:T(8,128)(2,1)S(1)}, u32[]{:S(2)}, u32[]{:S(2)}) collective-permute-start(bf16[256,128]{1,0:T(8,128)(2,1)} %get-tuple-element.78), channel_id=1, source_target_pairs={{0,2},{1,3},{2,4},{3,5},{4,6},{5,7},{6,0},{7,1},{8,10},{9,11},{10,... | collective-permute-start | bytes 196616 | tf_op jit(solution)/shard_map/ppermute | solution.py:644
  66.5 13.4 %collective-permute-start.19 = (bf16[256,128]{1,0:T(8,128)(2,1)}, bf16[256,128]{1,0:T(8,128)(2,1)S(1)}, u32[]{:S(2)}, u32[]{:S(2)}) collective-permute-start(bf16[256,128]{1,0:T(8,128)(2,1)} %get-tuple-element.79), channel_id=1, source_target_pairs={{0,4},{1,5},{2,6},{3,7},{4,0},{5,1},{6,2},{7,3},{8,12},{9,13},{10,... | collective-permute-start | bytes 196616 | tf_op jit(solution)/shard_map/ppermute | solution.py:644
  68.9 11.0 %collective-permute-start.20 = (bf16[256,128]{1,0:T(8,128)(2,1)}, bf16[256,128]{1,0:T(8,128)(2,1)S(1)}, u32[]{:S(2)}, u32[]{:S(2)}) collective-permute-start(bf16[256,128]{1,0:T(8,128)(2,1)} %get-tuple-element.80), channel_id=1, source_target_pairs={{0,6},{1,7},{2,0},{3,1},{4,2},{5,3},{6,4},{7,5},{8,14},{9,15},{10,... | collective-permute-start | bytes 196616 | tf_op jit(solution)/shard_map/ppermute | solution.py:644
  73.6 18.1 %collective-permute-start.23 = (bf16[128,1024]{1,0:T(8,128)(2,1)}, bf16[128,1024]{1,0:T(8,128)(2,1)S(1)}, u32[]{:S(2)}, u32[]{:S(2)}) collective-permute-start(bf16[128,1024]{1,0:T(8,128)(2,1)} %get-tuple-element.87), channel_id=1, source_target_pairs={{0,16},{16,32},{32,48},{48,0},{64,80},{80,96},{96,112},{112,64},{1... | collective-permute-start | bytes 786440 | tf_op jit(solution)/shard_map/ppermute | solution.py:648
  74.7 17.0 %collective-permute-start.24 = (bf16[128,1024]{1,0:T(8,128)(2,1)}, bf16[128,1024]{1,0:T(8,128)(2,1)S(1)}, u32[]{:S(2)}, u32[]{:S(2)}) collective-permute-start(bf16[128,1024]{1,0:T(8,128)(2,1)} %get-tuple-element.88), channel_id=1, source_target_pairs={{0,32},{16,48},{32,0},{48,16},{64,96},{80,112},{96,64},{112,80},{1... | collective-permute-start | bytes 786440 | tf_op jit(solution)/shard_map/ppermute | solution.py:648
  78.5 13.2 %collective-permute-start.25 = (bf16[128,1024]{1,0:T(8,128)(2,1)}, bf16[128,1024]{1,0:T(8,128)(2,1)S(1)}, u32[]{:S(2)}, u32[]{:S(2)}) collective-permute-start(bf16[128,1024]{1,0:T(8,128)(2,1)} %get-tuple-element.89), channel_id=1, source_target_pairs={{0,48},{16,0},{32,16},{48,32},{64,112},{80,64},{96,80},{112,96},{1... | collective-permute-start | bytes 786440 | tf_op jit(solution)/shard_map/ppermute | solution.py:648
  91.1 2.9 %collective-permute-start.21 = (bf16[4,256,256]{2,1,0:T(8,128)(2,1)}, bf16[4,256,256]{2,1,0:T(8,128)(2,1)S(1)}, u32[]{:S(2)}, u32[]{:S(2)}) collective-permute-start(bf16[4,256,256]{2,1,0:T(8,128)(2,1)} %get-tuple-element.83), channel_id=1, source_target_pairs={{0,1},{1,0},{2,3},{3,2},{4,5},{5,4},{6,7},{7,6},{8,9},{9,8},{10,11... | collective-permute-start | bytes 1572872 | tf_op jit(solution)/shard_map/ppermute | solution.py:644
  91.2 2.9 %collective-permute-start.22 = (bf16[4,256,256]{2,1,0:T(8,128)(2,1)}, bf16[4,256,256]{2,1,0:T(8,128)(2,1)S(1)}, u32[]{:S(2)}, u32[]{:S(2)}) collective-permute-start(bf16[4,256,256]{2,1,0:T(8,128)(2,1)} %get-tuple-element.84), channel_id=1, source_target_pairs={{0,1},{1,0},{2,3},{3,2},{4,5},{5,4},{6,7},{7,6},{8,9},{9,8},{10,11... | collective-permute-start | bytes 1572872 | tf_op jit(solution)/shard_map/ppermute | solution.py:644
  97.9 19.7 %collective-permute-start.30 = (bf16[288,256]{1,0:T(8,128)(2,1)}, bf16[288,256]{1,0:T(8,128)(2,1)S(1)}, u32[]{:S(2)}, u32[]{:S(2)}) collective-permute-start(bf16[288,256]{1,0:T(8,128)(2,1)} %get-tuple-element.103), channel_id=1, source_target_pairs={{0,8},{1,9},{2,10},{3,11},{4,12},{5,13},{6,14},{7,15},{8,0},{9,1},... | collective-permute-start | bytes 442376 | tf_op jit(solution)/shard_map/ppermute | solution.py:644
  100.4 21.6 %collective-permute-start.31 = (bf16[288,256]{1,0:T(8,128)(2,1)}, bf16[288,256]{1,0:T(8,128)(2,1)S(1)}, u32[]{:S(2)}, u32[]{:S(2)}) collective-permute-start(bf16[288,256]{1,0:T(8,128)(2,1)} %get-tuple-element.104), channel_id=1, source_target_pairs={{0,10},{1,11},{2,12},{3,13},{4,14},{5,15},{6,8},{7,9},{8,2},{9,3},... | collective-permute-start | bytes 442376 | tf_op jit(solution)/shard_map/ppermute | solution.py:644
  101.8 29.9 %collective-permute-start.27 = (bf16[416,256]{1,0:T(8,128)(2,1)}, bf16[416,256]{1,0:T(8,128)(2,1)S(1)}, u32[]{:S(2)}, u32[]{:S(2)}) collective-permute-start(bf16[416,256]{1,0:T(8,128)(2,1)} %get-tuple-element.100), channel_id=1, source_target_pairs={{0,2},{1,3},{2,4},{3,5},{4,6},{5,7},{6,0},{7,1},{8,10},{9,11},{10,... | collective-permute-start | bytes 638984 | tf_op jit(solution)/shard_map/ppermute | solution.py:644
  102.2 29.5 %collective-permute-start.28 = (bf16[416,256]{1,0:T(8,128)(2,1)}, bf16[416,256]{1,0:T(8,128)(2,1)S(1)}, u32[]{:S(2)}, u32[]{:S(2)}) collective-permute-start(bf16[416,256]{1,0:T(8,128)(2,1)} %get-tuple-element.101), channel_id=1, source_target_pairs={{0,4},{1,5},{2,6},{3,7},{4,0},{5,1},{6,2},{7,3},{8,12},{9,13},{10,... | collective-permute-start | bytes 638984 | tf_op jit(solution)/shard_map/ppermute | solution.py:644
  105.6 26.1 %collective-permute-start.29 = (bf16[416,256]{1,0:T(8,128)(2,1)}, bf16[416,256]{1,0:T(8,128)(2,1)S(1)}, u32[]{:S(2)}, u32[]{:S(2)}) collective-permute-start(bf16[416,256]{1,0:T(8,128)(2,1)} %get-tuple-element.102), channel_id=1, source_target_pairs={{0,6},{1,7},{2,0},{3,1},{4,2},{5,3},{6,4},{7,5},{8,14},{9,15},{10,... | collective-permute-start | bytes 638984 | tf_op jit(solution)/shard_map/ppermute | solution.py:644
  106.4 19.1 %all-to-all-start = ((f32[128,1,128]{2,1,0:T(1,128)}), f32[128,1,128]{2,1,0:T(1,128)S(1)}, u32[]{:S(2)}, u32[]{:S(2)}) async-start(f32[128,1,128]{2,1,0:T(1,128)} %broadcast_in_dim.5), calls=%async_computation | async-start | bytes 131072 | tf_op jit(solution)/shard_map/all_to_all | solution.py:654
  117.6 10.5 %collective-permute-start.32 = (bf16[288,256]{1,0:T(8,128)(2,1)}, bf16[288,256]{1,0:T(8,128)(2,1)S(1)}, u32[]{:S(2)}, u32[]{:S(2)}) collective-permute-start(bf16[288,256]{1,0:T(8,128)(2,1)} %get-tuple-element.105), channel_id=1, source_target_pairs={{0,12},{1,13},{2,14},{3,15},{4,8},{5,9},{6,10},{7,11},{8,4},{9,5},... | collective-permute-start | bytes 442376 | tf_op jit(solution)/shard_map/ppermute | solution.py:644
  122.0 9.7 %collective-permute-start.33 = (bf16[288,256]{1,0:T(8,128)(2,1)}, bf16[288,256]{1,0:T(8,128)(2,1)S(1)}, u32[]{:S(2)}, u32[]{:S(2)}) collective-permute-start(bf16[288,256]{1,0:T(8,128)(2,1)} %get-tuple-element.106), channel_id=1, source_target_pairs={{0,14},{1,15},{2,8},{3,9},{4,10},{5,11},{6,12},{7,13},{8,6},{9,7},... | collective-permute-start | bytes 442376 | tf_op jit(solution)/shard_map/ppermute | solution.py:644
  134.7 7.8 %collective-permute-start.34 = (f32[4,1024]{1,0:T(4,128)}, f32[4,1024]{1,0:T(4,128)S(1)}, u32[]{:S(2)}, u32[]{:S(2)}) collective-permute-start(f32[4,1024]{1,0:T(4,128)} %get-tuple-element.108), channel_id=1, source_target_pairs={{0,64},{16,80},{32,96},{48,112},{64,0},{80,16},{96,32},{112,48},{1... | collective-permute-start | bytes 49160 | tf_op jit(solution)/shard_map/ppermute | solution.py:703
  (39 other events, 194.8 us)

commit v3 on v2

v3 whole, which is shorter than its diff:
```python
import functools
import math

import jax
import jax.numpy as jnp
from jax import lax
from jax.experimental import pallas as pl
from jax.experimental.pallas import tpu as pltpu
from jax.sharding import PartitionSpec as P

f32 = jnp.float32
bf16 = jnp.bfloat16
i32 = jnp.int32
T = 128
EPS = 1e-05
HEADS = 4
BUCKETS = 12
DEVS = 16
TILES = 32
QT = 8
SCALE = 1.0 / math.sqrt(128.0)
LIST = 160
FAR_U = 8
NEAR_U = 4
NEAR_FLAG = 32768
DUMMY = QT + 16 * TILES
VM_ATTEND = 20
VM_BACK = 24
VMEM = pl.BlockSpec(memory_space=pltpu.VMEM)
SMEM = pl.BlockSpec(memory_space=pltpu.SMEM)
NT_DIMS = (((1,), (1,)), ((), ()))
TN_DIMS = (((0,), (0,)), ((), ()))


def params(mib=24):
    return pltpu.CompilerParams(vmem_limit_bytes=mib * 1024 * 1024)


def cost(flops, size):
    return pl.CostEstimate(flops=int(flops), bytes_accessed=int(size), transcendentals=0)


def sds(shape, dtype):
    return jax.ShapeDtypeStruct(shape, dtype)


def norm_rows(values):
    centre = jnp.mean(values, axis=-1, keepdims=True)
    shifted = values - centre
    spread = jnp.mean(shifted * shifted, axis=-1, keepdims=True)
    inverse = lax.rsqrt(spread + EPS)
    return shifted * inverse, inverse


def norm_back(upstream, normed, inverse):
    first = jnp.mean(upstream, axis=-1, keepdims=True)
    second = jnp.mean(upstream * normed, axis=-1, keepdims=True)
    return inverse * (upstream - first - normed * second)


def in_hbm(part):
    return pltpu.with_memory_space_constraint(part, pltpu.HBM)


def project_kernel(own, tokens, *refs):
    weights, outs, normed = refs[own : 2 * own + 2], refs[2 * own + 2 : -1], refs[-1]
    head = pl.program_id(0)
    shift = (head + 4 - (lax.axis_index("ctx") // 2) % 4) % 4

    @pl.when(head == 0)
    def _():
        normed[...] = norm_rows(tokens[0:256, :].astype(f32))[0].astype(bf16)

    wide = jnp.concatenate([w[...] for w in weights], axis=1)
    half = 0.5 * jnp.dot(normed[...], wide, preferred_element_type=f32)
    act = (half * jnp.tanh(half) + half).astype(bf16)
    meta = tokens[256:, 0:256]
    if own:
        mask, blank = refs[0], jnp.zeros((1, T - TILES), f32)
        row = [mask[0, 0:1].astype(f32), blank, mask[0, 1:2].astype(f32), blank]
        rows = [meta[0:2].astype(f32), jnp.concatenate(row, axis=1), jnp.zeros((13, 256), f32)]
        meta = jnp.concatenate(rows, axis=0).astype(bf16)
    for which in range(4):

        @pl.when(shift == which)
        def _(which=which):
            outs[which][0:256, :] = act
            outs[which][256:, 0:256] = meta
            if own:
                outs[which][256:, 256:] = jnp.zeros((16, T), bf16)


def project(tokens, in_proj, mask=None):
    own = mask is not None
    width = 384 if own else 256

    def column(kind):
        return pl.BlockSpec((1024, T), lambda h: (0, kind * HEADS + h))

    whole = lambda shape: pl.BlockSpec(shape, lambda h: (0,) * len(shape))
    kinds = (3, 1, 2) if own else (3, 1)
    return pl.pallas_call(
        functools.partial(project_kernel, int(own)),
        grid=(HEADS,),
        in_specs=[whole((272, 1024))] + [whole((1, 2, TILES))] * own + [column(kind) for kind in kinds],
        out_specs=[whole((272, width))] * 4,
        out_shape=[sds((272, width), bf16)] * 4,
        scratch_shapes=[pltpu.VMEM((256, 1024), bf16)],
        compiler_params=params(12),
        cost_estimate=cost(2 * 256 * 1024 * 4 * width, 5 << 20),
        name="project_own" if own else "project_other",
    )(tokens, *([in_hbm(mask)] if own else []), *[in_hbm(in_proj)] * len(kinds))


def gates_kernel(tokens, in_proj, cot, out_proj, gate, slope, grad_mix, normed):
    kind = pl.program_id(0)

    @pl.when(kind == 0)
    def _():
        normed[...] = norm_rows(tokens[...].astype(f32))[0].astype(bf16)
        grad_mix[...] = lax.dot_general(cot[...], out_proj[...], NT_DIMS, preferred_element_type=f32)

    pre = jnp.dot(normed[...], in_proj[...], preferred_element_type=f32)
    sig = 0.5 * jnp.tanh(0.5 * pre) + 0.5
    slope[...] = (sig * (1.0 + pre * (1.0 - sig))).astype(bf16)

    @pl.when(kind == 0)
    def _():
        gate[...] = (pre * sig).astype(bf16)


def make_gates(tokens, in_proj, cot, out_proj):
    whole = lambda shape: pl.BlockSpec(shape, lambda s: (0,) * len(shape))
    return pl.pallas_call(
        gates_kernel,
        grid=(4,),
        in_specs=[
            whole((256, 1024)),
            pl.BlockSpec((1024, 512), lambda s: (0, s)),
            whole((256, 1024)),
            whole((512, 1024)),
        ],
        out_specs=[whole((256, 512)), pl.BlockSpec((256, 512), lambda s: (0, s)), whole((256, 512))],
        out_shape=[sds((256, 512), bf16), sds((256, 2048), bf16), sds((256, 512), f32)],
        scratch_shapes=[pltpu.VMEM((256, 1024), bf16)],
        compiler_params=params(16),
        cost_estimate=cost(2 * 256 * 1024 * 2048, 7 << 20),
        name="gates",
    )(in_hbm(tokens), in_hbm(in_proj), in_hbm(cot), in_hbm(out_proj))


def bias_far(gap, table, bottom):
    first = table[bottom]
    second = table[bottom + 1]
    third = table[bottom + 2]
    limit1 = table[16 + bottom + 1]
    limit2 = table[16 + bottom + 2]
    over1 = gap >= limit1
    over2 = gap >= limit2
    return jnp.where(over2, third, jnp.where(over1, second, first)), over1, over2


def bias_near(gap, table):
    bias = jnp.full(gap.shape, table[0], f32)
    for j in range(1, BUCKETS):
        bias = jnp.where(gap >= float(2**j - 1), table[j], bias)
    return bias


def keep_near(ids, start, jj, k):
    tile = query_tile(ids, jj)
    row = lax.broadcasted_iota(i32, (T, T), 0)
    col = lax.broadcasted_iota(i32, (T, T), 1)
    later = (col - row) <= (tile - k) * T
    return later & ((col + k * T) >= start)


STAGE = [pltpu.VMEM((QT + 1, T, T), f32), pltpu.VMEM((QT + 1, T, T), i32)]


def query_tile(ids, jj):
    dev = ids[0] * 8 + (jj // 2) * 2 + ids[2]
    return jnp.where(jj % 2 == 0, dev, 2 * DEVS - 1 - dev)


def starts_of(lengths, pos):
    end0 = lengths[0]
    end1 = lengths[0] + lengths[1]
    return jnp.where(pos >= end1, end1, jnp.where(pos >= end0, end0, 0))


def stage(ids, ins, keys, values, queries, tk, flags, times):
    y, z, core = ids[0], ids[1], ids[2]
    for group in range(4):
        for t in range(4):
            ref = ins[group * 4 + t]
            zz = (z + 4 - t) % 4
            dev = (y if group < 2 else 1 - y) * 8 + zz * 2 + (core if group % 2 == 0 else 1 - core)
            keys[dev] = ref[0:T, 0:T]
            values[dev] = ref[0:T, T : 2 * T]
            keys[2 * DEVS - 1 - dev] = ref[T : 2 * T, 0:T]
            values[2 * DEVS - 1 - dev] = ref[T : 2 * T, T : 2 * T]
            head = ref[256:272, 0:256].astype(f32)
            moments = head[0:1] * 128.0 + head[1:2]
            tk[dev] = jnp.broadcast_to(moments[:, :T], (8, T))
            tk[2 * DEVS - 1 - dev] = jnp.broadcast_to(moments[:, T:], (8, T))
            times[pl.ds(dev, 1), :] = moments[:, :T]
            times[pl.ds(2 * DEVS - 1 - dev, 1), :] = moments[:, T:]
            if group == 0:
                queries[2 * zz] = ref[0:T, 2 * T :]
                queries[2 * zz + 1] = ref[T : 2 * T, 2 * T :]
                flags[pl.ds(2 * zz, 1), :] = head[2:3, :T]
                flags[pl.ds(2 * zz + 1, 1), :] = head[2:3, T:]
    keys[TILES] = jnp.zeros((T, T), bf16)
    values[TILES] = jnp.zeros((T, T), bf16)
    queries[QT] = jnp.zeros((T, T), bf16)
    tk[TILES] = jnp.zeros((8, T), f32)


def stage_times(ids, lengths, tq, tk, start):
    tq[QT] = jnp.zeros((T, T), f32)
    start[QT] = jnp.zeros((T, T), i32)
    rows = lax.broadcasted_iota(i32, (T, T), 0)
    for jj in range(QT):
        tile = query_tile(ids, jj)
        tq[jj] = jnp.transpose(jnp.broadcast_to(tk[tile][0:1, :], (T, T)))
        start[jj] = starts_of(lengths, rows + tile * T)


def make_lists(ids, lengths, flags, times, q_times, codes, codes_smem, sem, far, near, counts):
    def level(gap):
        total = jnp.zeros(gap.shape, i32)
        for j in range(1, BUCKETS):
            total = total + jnp.where(gap >= float(2**j - 1), 1, 0)
        return total

    for jj in range(QT):
        q_times[jj : jj + 1, :] = times[pl.ds(query_tile(ids, jj), 1), :]
    turned = jnp.transpose(times[...])
    k_first, k_last = turned[0:1, :], turned[T - 1 :, :]
    q_first, q_last = q_times[:, 0:1], q_times[:, T - 1 :]
    jj = lax.broadcasted_iota(i32, (8, T), 0)
    kk = lax.broadcasted_iota(i32, (8, T), 1)
    tile = query_tile(ids, jj)
    low = starts_of(lengths, tile * T)
    high = starts_of(lengths, tile * T + T - 1)
    bottom = level(jnp.maximum(q_first - k_last, 0.0))
    top = level(q_last - k_first)
    row = lax.broadcasted_iota(i32, (T, T), 0)
    col = lax.broadcasted_iota(i32, (T, T), 1)
    turn = jnp.where(row == jnp.where(col < DEVS, 2 * col, 4 * DEVS - 1 - 2 * col), 1.0, 0.0).astype(bf16)
    ordered = jnp.dot(flags[...].astype(bf16), turn, preferred_element_type=f32)
    allowed = (ordered > 0.5) & (kk <= tile) & (kk * T + T - 1 >= low)
    plain = (kk < tile) & (kk * T >= high) & (top - bottom <= 2)
    entry = jj + 16 * kk
    codes[...] = jnp.where(
        allowed, jnp.where(plain, entry + 1024 * bottom, entry + NEAR_FLAG), -1
    )
    copy = pltpu.make_async_copy(codes, codes_smem, sem)
    copy.start()
    copy.wait()

    def query_step(jj, sizes):
        tile = query_tile(ids, jj)

        def key_step(k, sizes):
            n_far, n_near = sizes
            code = codes_smem[jj, k]
            far[n_far] = code
            near[n_near] = code & (NEAR_FLAG - 1)
            is_near = code >= NEAR_FLAG
            is_far = (code >= 0) & jnp.logical_not(is_near)
            return n_far + is_far.astype(i32), n_near + is_near.astype(i32)

        return lax.fori_loop(starts_of(lengths, tile * T) // T, tile + 1, key_step, sizes)

    n_far, n_near = lax.fori_loop(0, QT, query_step, (jnp.int32(0), jnp.int32(0)))
    for pad in range(FAR_U):
        far[n_far + pad] = DUMMY
    for pad in range(NEAR_U):
        near[n_near + pad] = DUMMY
    counts[0] = (n_far + FAR_U - 1) // FAR_U
    counts[1] = (n_near + NEAR_U - 1) // NEAR_U


def unpack(ref, i, count):
    got = []
    for u in range(count):
        entry = ref[i * count + u]
        got.append((entry & 15, (entry >> 4) & 63, entry >> 10))
    return got


def forward_kernel(ids, table, lengths, *refs):
    ins, (out, far, near, counts, keys, values, queries, tk) = refs[:16], refs[16:24]
    tq, start, acc, flags, times, q_times, codes, codes_smem, sem = refs[24:]
    times[...] = jnp.zeros(times.shape, f32)
    stage(ids, ins, keys, values, queries, tk, flags, times)
    stage_times(ids, lengths, tq, tk, start)
    make_lists(ids, lengths, flags, times, q_times, codes, codes_smem, sem, far, near, counts)
    acc[...] = jnp.zeros(acc.shape, f32)

    def far_step(i, _):
        got = unpack(far, i, FAR_U)
        dots = [lax.dot_general(queries[j], keys[k], NT_DIMS, preferred_element_type=f32) for j, k, _ in got]
        weights = []
        for u, (jj, k, bottom) in enumerate(got):
            bias, _, _ = bias_far(tq[jj] - tk[k][0:1, :], table, bottom)
            half = dots[u] * (0.5 * SCALE) + bias
            weights.append((half * jnp.tanh(half) + half).astype(bf16))
        adds = [jnp.dot(weights[u], values[got[u][1]], preferred_element_type=f32) for u in range(len(got))]
        for u in range(len(got)):
            acc[got[u][0]] += adds[u]
        return 0

    def near_step(i, _):
        got = unpack(near, i, NEAR_U)
        dots = [lax.dot_general(queries[j], keys[k], NT_DIMS, preferred_element_type=f32) for j, k, _ in got]
        weights = []
        for u, (jj, k, _) in enumerate(got):
            half = dots[u] * (0.5 * SCALE) + bias_near(tq[jj] - tk[k][0:1, :], table)
            weight = half * jnp.tanh(half) + half
            weights.append(jnp.where(keep_near(ids, start[jj], jj, k), weight, 0.0).astype(bf16))
        adds = [jnp.dot(weights[u], values[got[u][1]], preferred_element_type=f32) for u in range(len(got))]
        for u in range(len(got)):
            acc[got[u][0]] += adds[u]
        return 0

    lax.fori_loop(0, counts[0], far_step, 0)
    lax.fori_loop(0, counts[1], near_step, 0)
    for zz in range(4):
        out[zz, 0:T] = acc[2 * zz]
        out[zz, T:] = acc[2 * zz + 1]


def attend(ids, table, lengths, parts):
    return pl.pallas_call(
        forward_kernel,
        in_specs=[SMEM] * 3 + [VMEM] * 16,
        out_specs=[VMEM] + [SMEM] * 3 + [VMEM] * 4,
        out_shape=[sds((4, 256, T), f32), sds((LIST,), i32), sds((LIST,), i32), sds((8,), i32)]
        + [sds((TILES + 1, T, T), bf16)] * 2
        + [sds((QT + 1, T, T), bf16), sds((TILES + 1, 8, T), f32)],
        scratch_shapes=STAGE
        + [
            pltpu.VMEM((QT + 1, T, T), f32),
            pltpu.VMEM((8, T), f32),
            pltpu.VMEM((T, T), f32),
            pltpu.VMEM((8, T), f32),
            pltpu.VMEM((8, T), i32),
            pltpu.SMEM((8, T), i32),
            pltpu.SemaphoreType.DMA,
        ],
        compiler_params=params(VM_ATTEND),
        cost_estimate=cost(1e9 * 6, 6 << 20),
        name="attend",
    )(ids, table, lengths, *parts)


def middle_kernel(heads, gate, slope, grad_mix, mixed, grad_gate, grads):
    whole = jnp.concatenate([heads[h] for h in range(4)], axis=1)
    normed, inverse = norm_rows(whole)
    gates = gate[...].astype(f32)
    mixed[...] = (normed * gates).astype(bf16)
    back = grad_mix[...]
    grad_gate[...] = (back * normed * slope[...].astype(f32)).astype(bf16)
    grad = norm_back(back * gates, normed, inverse).astype(bf16)
    for h in range(4):
        grads[h] = grad[:, h * T : (h + 1) * T]


def middle(heads, gate, slope, grad_mix):
    whole = lambda shape: pl.BlockSpec(shape, lambda i: (0,) * len(shape))
    return pl.pallas_call(
        middle_kernel,
        grid=(1,),
        in_specs=[whole((4, 256, T)), whole((256, 512)), whole((256, 512)), whole((256, 512))],
        out_specs=[whole((256, 512)), whole((256, 512)), whole((4, 256, T))],
        out_shape=[sds((256, 512), bf16), sds((256, 512), bf16), sds((4, 256, T), bf16)],
        compiler_params=params(12),
        cost_estimate=cost(1 << 24, 3 << 20),
        name="middle",
    )(heads, gate, slope, grad_mix)


def output_kernel(ids, tokens, cot, out_proj, mixed, output, mine, *theirs):
    y, z, core, low, x = ids[0], ids[1], ids[2], ids[3] // 4, ids[3] % 4
    output[...] = (
        tokens[...].astype(f32) + jnp.dot(mixed[...], out_proj[...], preferred_element_type=f32)
    ).astype(bf16)
    r = lax.broadcasted_iota(i32, (512, 512), 1)
    c = lax.broadcasted_iota(i32, (512, 512), 0)
    r_x = ((r // 128) + x) % 4
    r_core = ((r // 64) % 2) ^ core
    r_z = (((r // 16) % 4) + z) % 4
    r_y = ((r // 8) % 2) ^ y
    source = (((r // 4) % 2) * 4 + r_x) * 64 + r_y * 32 + r_z * 8 + r_core * 4 + r % 4
    pick = jnp.where(c == source, 1.0, 0.0).astype(bf16)
    moved = jnp.dot(mixed[...], pick, preferred_element_type=f32).astype(bf16)
    part = lax.dot_general(moved, cot[...], TN_DIMS, preferred_element_type=f32)
    mine[...] = part[:T]
    for i in range(3):
        theirs[i][...] = part[(i + 1) * T : (i + 2) * T].astype(bf16)


def finish_output(ids, tokens, cot, out_proj, mixed):
    return pl.pallas_call(
        output_kernel,
        in_specs=[SMEM] + [VMEM] * 4,
        out_specs=[VMEM] * 5,
        out_shape=[sds((256, 1024), bf16), sds((T, 1024), f32)] + [sds((T, 1024), bf16)] * 3,
        compiler_params=params(24),
        cost_estimate=cost(6 * 256 * 512 * 1024, 5 << 20),
        name="finish_output",
    )(ids, in_hbm(tokens), in_hbm(cot), in_hbm(out_proj), mixed)


def backward_kernel(ids, table, lengths, far, near, counts, *refs):
    (keys, values, queries, tk), got_grads, outs = refs[:4], refs[4], refs[5:11]
    mine_s, mine_o, theirs_s, theirs_o, dq_out, rab_out = outs
    tq, start, grads, grads_t, queries_t, dq, dkt, dvt, rab = refs[11:]
    y, z, core = ids[0], ids[1], ids[2]
    stage_times(ids, lengths, tq, tk, start)
    for zz in range(4):
        for half in range(2):
            block = got_grads[zz, half * T : (half + 1) * T, :].astype(f32) * 0.5
            grads[2 * zz + half] = block.astype(bf16)
            grads_t[2 * zz + half] = jnp.transpose(block).astype(bf16)
    for jj in range(QT):
        queries_t[jj] = jnp.transpose(queries[jj].astype(f32)).astype(bf16)
    grads[QT] = jnp.zeros((T, T), bf16)
    grads_t[QT] = jnp.zeros((T, T), bf16)
    queries_t[QT] = jnp.zeros((T, T), bf16)
    dq[...] = jnp.zeros(dq.shape, f32)
    dkt[...] = jnp.zeros(dkt.shape, f32)
    dvt[...] = jnp.zeros(dvt.shape, f32)
    rab[...] = jnp.zeros(rab.shape, f32)

    def fold(values_):
        return jnp.sum(values_.reshape(T // 8, 8, T), axis=0)

    def front(got):
        dots = [lax.dot_general(queries[j], keys[k], NT_DIMS, preferred_element_type=f32) for j, k, _ in got]
        wides = [lax.dot_general(grads[j], values[k], NT_DIMS, preferred_element_type=f32) for j, k, _ in got]
        return dots, wides

    def score(half, wide, keep):
        t = jnp.tanh(half)
        weight = half * t + half
        d_score = wide * ((1.0 + t) * (1.0 + half * (1.0 - t)))
        if keep is not None:
            weight = jnp.where(keep, weight, 0.0)
            d_score = jnp.where(keep, d_score, 0.0)
        return weight.astype(bf16), d_score

    def back(got, weights, scores):
        a = [jnp.dot(scores[u], keys[got[u][1]], preferred_element_type=f32) for u in range(len(got))]
        b = [jnp.dot(queries_t[got[u][0]], scores[u], preferred_element_type=f32) for u in range(len(got))]
        c = [jnp.dot(grads_t[got[u][0]], weights[u], preferred_element_type=f32) for u in range(len(got))]
        for u, (jj, k, _) in enumerate(got):
            dq[jj] += a[u]
            dkt[k] += b[u]
            dvt[k] += c[u]

    def far_step(i, _):
        got = unpack(far, i, FAR_U)
        dots, wides = front(got)
        weights, scores, sums = [], [], []
        for u, (jj, k, bottom) in enumerate(got):
            bias, over1, over2 = bias_far(tq[jj] - tk[k][0:1, :], table, bottom)
            weight, d_score = score(dots[u] * (0.5 * SCALE) + bias, wides[u], None)
            weights.append(weight)
            scores.append(d_score.astype(bf16))
            sums.append((fold(d_score), fold(jnp.where(over1, d_score, 0.0)), fold(jnp.where(over2, d_score, 0.0))))
        back(got, weights, scores)
        for (jj, k, bottom), (sum0, sum1, sum2) in zip(got, sums):
            rab[bottom] += sum0 - sum1
            rab[bottom + 1] += sum1 - sum2
            rab[bottom + 2] += sum2
        return 0

    def near_step(i, _):
        got = unpack(near, i, NEAR_U)
        dots, wides = front(got)
        weights, scores = [], []
        sums = [jnp.zeros((8, T), f32)] * BUCKETS
        for u, (jj, k, _) in enumerate(got):
            gap = tq[jj] - tk[k][0:1, :]
            half = dots[u] * (0.5 * SCALE) + bias_near(gap, table)
            weight, d_score = score(half, wides[u], keep_near(ids, start[jj], jj, k))
            weights.append(weight)
            scores.append(d_score.astype(bf16))
            sums[0] = sums[0] + fold(d_score)
            for j in range(1, BUCKETS):
                sums[j] = sums[j] + fold(jnp.where(gap >= float(2**j - 1), d_score, 0.0))
        back(got, weights, scores)
        for j in range(BUCKETS - 1):
            rab[j] += sums[j] - sums[j + 1]
        rab[BUCKETS - 1] += sums[BUCKETS - 1]
        return 0

    lax.fori_loop(0, counts[0], far_step, 0)
    lax.fori_loop(0, counts[1], near_step, 0)
    for other in range(2):
        for s in range(4):
            base = (y if other == 0 else 1 - y) * 8 + ((z + s) % 4) * 2
            for side in range(2):
                dev = base + (core if side == 0 else 1 - core)
                ref = ((mine_s, theirs_s), (mine_o, theirs_o))[other][side]
                for half in range(2):
                    tile = dev if half == 0 else 2 * DEVS - 1 - dev
                    ref[s, 0:T, half * T : (half + 1) * T] = (dkt[tile] * SCALE).astype(bf16)
                    ref[s, T:, half * T : (half + 1) * T] = (dvt[tile] * 2.0).astype(bf16)
    for s in range(4):
        zz = (z + s) % 4
        for half in range(2):
            dq_out[s, :, half * T : (half + 1) * T] = (dq[2 * zz + half] * SCALE).astype(bf16)
    for b in range(16):
        if b < BUCKETS:
            rab_out[b : b + 1, :] = jnp.sum(rab[b], axis=0, keepdims=True)
        else:
            rab_out[b : b + 1, :] = jnp.zeros((1, T), f32)


def attend_back(ids, table, lengths, saved, grads):
    return pl.pallas_call(
        backward_kernel,
        in_specs=[SMEM] * 6 + [VMEM] * 5,
        out_specs=[VMEM] * 6,
        out_shape=[sds((4, 256, 256), bf16)] * 4 + [sds((4, T, 256), bf16), sds((16, T), f32)],
        scratch_shapes=STAGE
        + [
            pltpu.VMEM((QT + 1, T, T), bf16),
            pltpu.VMEM((QT + 1, T, T), bf16),
            pltpu.VMEM((QT + 1, T, T), bf16),
            pltpu.VMEM((QT + 1, T, T), f32),
            pltpu.VMEM((TILES + 1, T, T), f32),
            pltpu.VMEM((TILES + 1, T, T), f32),
            pltpu.VMEM((16, 8, T), f32),
        ],
        compiler_params=params(VM_BACK),
        cost_estimate=cost(1e9 * 12, 8 << 20),
        name="attend_back",
    )(ids, table, lengths, *saved[:3], *[in_hbm(part) for part in saved[3:]], grads)


def combine_kernel(mine_s, mine_o, got_s, got_o, dq, proj_own, proj_got, rab, rab_got, *outs):
    proj = proj_own[...] + proj_got[...].astype(f32)
    both = rab[...] + rab_got[...]
    high = both.astype(bf16)
    low = (both - high.astype(f32)).astype(bf16)
    for s in range(4):
        outs[s][0:256, :] = (mine_s[s].astype(f32) + got_s[s].astype(f32)).astype(bf16)
        outs[s][256:384, :] = dq[s]
        outs[4 + s][0:256, :] = (mine_o[s].astype(f32) + got_o[s].astype(f32)).astype(bf16)
        for other in range(2):
            block = proj[s * 16 + other * 8 : s * 16 + other * 8 + 8, :]
            block = jnp.concatenate([block[:, c * 256 : (c + 1) * 256] for c in range(4)], axis=0)
            base = 384 - 128 * other
            outs[4 * other + s][base : base + 32, :] = block.astype(bf16)
            outs[4 * other + s][base + 32 :, 0:T] = high
            outs[4 * other + s][base + 32 :, T:] = low


def combine(*parts):
    return pl.pallas_call(
        combine_kernel,
        in_specs=[VMEM] * 9,
        out_specs=[VMEM] * 8,
        out_shape=[sds((432, 256), bf16)] * 4 + [sds((304, 256), bf16)] * 4,
        compiler_params=params(24),
        cost_estimate=cost(1 << 20, 5 << 20),
        name="combine",
    )(*parts)


def collect_kernel(ids, *refs):
    ins, rabs, out = refs[:8], refs[8:16], refs[16]
    total = ins[0][...].astype(f32)
    for ref in ins[1:]:
        total = total + ref[...].astype(f32)
    for d in range(8):
        for c in range(4):
            rows = total[c * 8 + (d // 4) * 4 : c * 8 + (d // 4) * 4 + 4, :]
            out[d, 0:4, c * 256 : (c + 1) * 256] = jnp.where(ids[3] % 4 == d % 4, rows, 0.0)
    lane = lax.broadcasted_iota(i32, (16, T), 1)
    table = jnp.zeros((16, T), f32)
    for t in range(4):
        near, far = rabs[t][...].astype(f32), rabs[4 + t][...].astype(f32)
        near, far = near[:, :T] + near[:, T:], far[:, :T] + far[:, T:]
        first, second = jnp.where(ids[0] == 0, near, far), jnp.where(ids[0] == 0, far, near)
        head = (ids[1] + 4 - t) % 4
        table = jnp.where(lane == head, jnp.sum(first + second, axis=1, keepdims=True), table)
    turned = jnp.transpose(jnp.concatenate([table, jnp.zeros((T - 16, T), f32)], axis=0))
    for d in range(8):
        out[d, 4:, :T] = turned[0:4]
        out[d, 4:, T:] = jnp.zeros((4, 1024 - T), f32)


def collect(ids, same, other):
    return pl.pallas_call(
        collect_kernel,
        grid=(1,),
        in_specs=[SMEM]
        + [pl.BlockSpec((32, 256), lambda i: (12, 0))] * 4
        + [pl.BlockSpec((32, 256), lambda i: (8, 0))] * 4
        + [pl.BlockSpec((16, 256), lambda i: (26, 0))] * 4
        + [pl.BlockSpec((16, 256), lambda i: (18, 0))] * 4,
        out_specs=pl.BlockSpec((8, 8, 1024), lambda i: (0, 0, 0)),
        out_shape=sds((8, 8, 1024), f32),
        compiler_params=params(8),
        cost_estimate=cost(1 << 16, 1 << 18),
        name="collect",
    )(ids, *same, *other, *same, *other)


def final_kernel(ids, grad_gate, in_proj_hbm, tokens_hbm, cot_hbm, slope_hbm, *refs):
    same, other, grad_in = refs[:4], refs[4:8], refs[8]
    grad_pre, in_proj, tokens, cot, slope, sems = refs[9:]
    z = ids[1]
    first = pltpu.make_async_copy(slope_hbm, slope, sems.at[4])
    weights = [
        pltpu.make_async_copy(in_proj_hbm.at[pl.ds(i * 256, 256)], in_proj.at[i], sems.at[i])
        for i in range(4)
    ]
    lasts = [
        pltpu.make_async_copy(tokens_hbm, tokens, sems.at[5]),
        pltpu.make_async_copy(cot_hbm, cot, sems.at[6]),
    ]
    for copy in [first] + weights + lasts:
        copy.start()
    grad_pre[:, 0:512] = grad_gate[...]
    first.wait()
    for t in range(4):
        head = (z + 4 - t) % 4
        column = lambda kind: pl.ds(pl.multiple_of(kind * 512 + head * T, T), T)
        total = same[t][0:256, :].astype(f32) + other[t][0:256, :].astype(f32)
        for half in range(2):
            rows = slice(half * T, (half + 1) * T)
            key = jnp.transpose(total[0:T, rows])
            value = jnp.transpose(total[T:, rows])
            query = same[t][256:384, rows].astype(f32)
            for kind, part in ((1, value), (2, query), (3, key)):
                grad_pre[rows, column(kind)] = (
                    part * slope[rows, column(kind)].astype(f32)
                ).astype(bf16)
    parts = []
    for i in range(4):
        weights[i].wait()
        parts.append(
            lax.dot_general(grad_pre[...], in_proj[i], NT_DIMS, preferred_element_type=f32)
        )
    for copy in lasts:
        copy.wait()
    normed, inverse = norm_rows(tokens[...].astype(f32))
    upstream = jnp.concatenate(parts, axis=1)
    grad_in[...] = (cot[...].astype(f32) + norm_back(upstream, normed, inverse)).astype(bf16)


def finish_grad(ids, tokens, cot, in_proj, slope, grad_gate, same, other):
    whole = lambda shape: pl.BlockSpec(shape, lambda s: (0,) * len(shape))
    hbm = pl.BlockSpec(memory_space=pltpu.HBM)
    return pl.pallas_call(
        final_kernel,
        grid=(1,),
        in_specs=[SMEM, whole((256, 512)), hbm, hbm, hbm, hbm]
        + [whole((384, 256))] * 4
        + [whole((256, 256))] * 4,
        out_specs=whole((256, 1024)),
        out_shape=sds((256, 1024), bf16),
        scratch_shapes=[
            pltpu.VMEM((256, 2048), bf16),
            pltpu.VMEM((4, 256, 2048), bf16),
            pltpu.VMEM((256, 1024), bf16),
            pltpu.VMEM((256, 1024), bf16),
            pltpu.VMEM((256, 2048), bf16),
            pltpu.SemaphoreType.DMA((7,)),
        ],
        compiler_params=params(56),
        cost_estimate=cost(2 * 256 * 1024 * 2048, 8 << 20),
        name="finish_grad",
    )(ids, grad_gate, in_proj, tokens, cot, slope, *same, *other)


def move(y_xor, z_shift, core_xor):
    pairs = []
    for dev in range(DEVS):
        y, z, core = dev // 8, (dev // 2) % 4, dev % 2
        target = (y ^ y_xor) * 8 + ((z + z_shift) % 4) * 2 + (core ^ core_xor)
        pairs.append((dev, target))
    return pairs


def send(x, y_xor, z_shift, core_xor):
    return lax.ppermute(x, "ctx", move(y_xor, z_shift, core_xor))


OVER_Z = [[y * 8 + z * 2 + c for z in range(4)] for y in range(2) for c in range(2)]
OVER_X = [[low * 4 + x for x in range(4)] for low in range(2)]


def send_x(part, shift):
    return lax.ppermute(part, "dp", [(d, d // 4 * 4 + (d + shift) % 4) for d in range(8)])


def swap_z(part):
    return lax.all_to_all(part, "ctx", 0, 0, axis_index_groups=OVER_Z, tiled=True)


def on_device(tokens, cotangent, in_proj, out_proj, rab_time, seq_lengths, block_mask, time_bucket):
    ctx = lax.axis_index("ctx")
    y, z, core = ctx // 8, (ctx // 2) % 4, ctx % 2
    times = jnp.stack([time_bucket // T, time_bucket % T]).astype(bf16)
    near_tokens = jnp.concatenate([tokens, jnp.pad(times, ((0, 14), (0, 768)))], axis=0)
    far_tokens = send(near_tokens, 1, 0, 0)
    full = project(near_tokens, in_proj, block_mask)
    own = [full[0]] + [send(full[s], 0, s, 0) for s in (1, 2, 3)]
    pairs = project(far_tokens, in_proj)
    own, pairs = lax.optimization_barrier((own, pairs))
    across = [pairs[0]] + [send(pairs[s], 0, s, 0) for s in (1, 2, 3)]
    gate, slope, grad_mix = make_gates(tokens, in_proj, cotangent, out_proj)
    own_twin = [send(part, 0, 0, 1) for part in own]
    across_twin = [send(part, 0, 0, 1) for part in across]
    parts = own + own_twin + across + across_twin

    ids = jnp.stack([y, z, core, lax.axis_index("dp")]).astype(i32)
    lengths = seq_lengths.reshape(3)
    limits = [2.0**j - 1.0 for j in range(BUCKETS)] + [1e9] * 4
    head_bias = lax.dynamic_slice_in_dim(rab_time, z, 1, 1).reshape(BUCKETS) * 0.5
    table = jnp.concatenate([head_bias, jnp.zeros((4,), f32), jnp.array(limits, f32)])
    heads, *saved = attend(ids, table, lengths, parts)

    mixed, grad_gate, grads = middle(swap_z(heads), gate, slope, grad_mix)
    grads = swap_z(grads)
    output, proj, *proj_x = finish_output(ids, tokens, cotangent, out_proj, mixed)
    grads, proj_x = lax.optimization_barrier((grads, proj_x))
    proj_x = [send_x(proj_x[s - 1], s) for s in (1, 2, 3)]

    mine_s, mine_o, theirs_s, theirs_o, dq, rab = attend_back(ids, table, lengths, saved, grads)
    got_o = send(theirs_o, 0, 0, 1)
    got_s = send(theirs_s, 0, 0, 1)
    rab_got = send(rab, 0, 0, 1)
    for part in proj_x:
        proj = proj + part.astype(f32)
    proj_own, proj_got = proj[:64], send(proj[64:].astype(bf16), 0, 0, 1)
    messages = combine(mine_s, mine_o, got_s, got_o, dq, proj_own, proj_got, rab, rab_got)
    same = [messages[0]] + [send(messages[s], 0, s, 0) for s in (1, 2, 3)]
    other = [send(messages[4 + s], 1, s, 0) for s in range(4)]
    lines = lax.all_to_all(collect(ids, same, other), "dp", 0, 0, tiled=True)
    sums = jnp.sum(lines, axis=0)
    grad_in = finish_grad(ids, tokens, cotangent, in_proj, slope, grad_gate, same, other)
    return output, grad_in, sums[:4], sums[4:, :BUCKETS].T


def solution(mesh):
    rows = P(("dp", "ctx"), None)
    placed = (rows, rows, P(), P(), P(), P("dp", None), P("dp", "ctx", None), P(("dp", "ctx")))
    return jax.shard_map(
        on_device,
        mesh=mesh,
        in_specs=placed,
        out_specs=(rows, rows, rows, P()),
        check_vma=False,
    )
```

time: 145 us -> 134 us (0.924)
  starting transfers between devices: 60.8 us -> 43.6 us
  waiting for transfers between devices: 25.7 us -> 32 us
  Pallas kernels: 43.7 us -> 47.1 us
  other arithmetic: 4.83 us -> 2.79 us
  local copies, waits for them, and re-layouts: 6.93 us -> 5.38 us
    ppermute x31 -> x26, starting transfers between devices: 42.6 us -> 28.9 us  [send(): return lax.ppermute(x, 'ctx', move(y_xor, z_shift, core_xor))]
    all_to_all x1 -> x3, waiting for transfers between devices: 0.99 us -> 8.92 us  [the longest x2 8.91 us: swap_z(): lax.all_to_all(part, 'ctx', 0, 0, axis_index_groups=OVER_Z, tiled=True)]
    pallas_call x6 -> x8, Pallas kernels: 32.3 us -> 35.4 us  [the longest x1 11.9 us: attend_back(): pl.pallas_call(backward_kernel, in_specs=[SMEM] * 6 + [VMEM] * 5, out_spe...]
    ppermute x3, starting transfers between devices: 6.28 us -> 3.7 us  [send_x(): lax.ppermute(part, 'dp', [(d, d // 4 * 4 + (d + shift) % 4) for d in rang...]
    ppermute x31 -> x26, waiting for transfers between devices: 24.7 us -> 23 us  [send(): return lax.ppermute(x, 'ctx', move(y_xor, z_shift, core_xor))]
    unnamed x71 -> x34, local copies, waits for them, and re-layouts: 4.56 us -> 4.14 us
    all_to_all x1 -> x3, starting transfers between devices: 11.2 us -> 11 us  [the longest x2 7.62 us: swap_z(): lax.all_to_all(part, 'ctx', 0, 0, axis_index_groups=OVER_Z, tiled=True)]
  transfers between devices with their start and end apart: 36 -> 32, of which waited for: 12 -> 18; matrix products, arithmetic and copies ran while one was open for 3% -> 1% of each run, Pallas kernels for 15% -> 27%
where the time goes in v3:
time: 134 us; the launch traced here: 132 us
  Pallas kernels  47.1 us (35%)
  starting transfers between devices  43.6 us (33%)
  waiting for transfers between devices  32 us (24%)
  local copies, waits for them, and re-layouts  5.38 us (4%)
  other arithmetic  2.79 us (2%)
    ppermute x26, starting transfers between devices, send(): return lax.ppermute(x, 'ctx', move(y_xor, z_shift, core_xor))  28.9 us
    ppermute x26, waiting for transfers between devices, send(): return lax.ppermute(x, 'ctx', move(y_xor, z_shift, core_xor))  23 us
    pallas_call x1, Pallas kernels, attend_back(): pl.pallas_call(backward_kernel, in_specs=[SMEM] * 6 + [VMEM] * 5, out_spe...  11.9 us
    all_to_all x2, waiting for transfers between devices, swap_z(): lax.all_to_all(part, 'ctx', 0, 0, axis_index_groups=OVER_Z, tiled=True)  8.91 us
    pallas_call x1, Pallas kernels, attend(): pl.pallas_call(forward_kernel, in_specs=[SMEM] * 3 + [VMEM] * 16, out_spe...  8.81 us
    pallas_call x2, Pallas kernels, project(): pl.pallas_call(functools.partial(project_kernel, int(own)), grid=(HEADS,)...  7.7 us
    all_to_all x2, starting transfers between devices, swap_z(): lax.all_to_all(part, 'ctx', 0, 0, axis_index_groups=OVER_Z, tiled=True)  7.62 us
    pallas_call x1, Pallas kernels, finish_grad(): pl.pallas_call(final_kernel, grid=(1,), in_specs=[SMEM, whole((256, 512))...  7.54 us
  transfers between devices with their start and end apart: 32, of which 18 were waited for; matrix products, arithmetic and copies ran while one was open for 1% of the time, Pallas kernels for 27%

profile of v3, /device:TPU:24, one launch (start us, length us, event | category | flops | bytes accessed | tf_op | source)
XLA Modules:
  0.0 131.6 jit_solution(4994986888150890664)
XLA Ops:
  1.4 1.1 pad_maximum_fusion.tokens
  2.4 1.3 collective-permute-start.3
  3.8 4.2 %project_own.1 = (bf16[272,384]{1,0:T(8,128)(2,1)S(1)}, bf16[272,384]{1,0:T(8,128)(2,1)S(1)}, bf16[272,384]{1,0:T(8,128)(2,1)S(1)}, bf16[272,384]{1,0:T(8,128)(2,1)S(1)}) custom-call(bf16[272,1024]{1,0:T(8,128)(2,1)S(1)} %pad_maximum_fusion.tokens, s32[1,2,32]{2,1,0:T(2,128)} %refs_0_.2, bf16[1024,2048]{1,0:T(8,128)(2,1)} %in_proj_hbm.1, ...), custom_call_target="tpu_custom_call" | custom-call | flops 805306368 | bytes 5242880 | tf_op jit(solution)/shard_map/project_own/pallas_call | solution.py:102
  7.9 2.0 %collective-permute-start = (bf16[272,384]{1,0:T(8,128)(2,1)S(1)}, bf16[272,384]{1,0:T(8,128)(2,1)S(1)}, u32[]{:S(2)}, u32[]{:S(2)}) collective-permute-start(bf16[272,384]{1,0:T(8,128)(2,1)S(1)} %get-tuple-element.58), channel_id=1, source_target_pairs={{0,2},{1,3},{2,4},{3,5},{4,6},{5,7},{6,0},{7,1},{8,10},{9,11},{10,... | collective-permute-start | bytes 626696 | tf_op jit(solution)/shard_map/ppermute | solution.py:695
  9.9 3.6 %collective-permute-start.1 = (bf16[272,384]{1,0:T(8,128)(2,1)S(1)}, bf16[272,384]{1,0:T(8,128)(2,1)S(1)}, u32[]{:S(2)}, u32[]{:S(2)}) collective-permute-start(bf16[272,384]{1,0:T(8,128)(2,1)S(1)} %get-tuple-element.59), channel_id=1, source_target_pairs={{0,4},{1,5},{2,6},{3,7},{4,0},{5,1},{6,2},{7,3},{8,12},{9,13},{10,... | collective-permute-start | bytes 626696 | tf_op jit(solution)/shard_map/ppermute | solution.py:695
  14.5 3.9 %collective-permute-done.3.tokens = bf16[272,1024]{1,0:T(8,128)(2,1)S(1)} collective-permute-done((bf16[272,1024]{1,0:T(8,128)(2,1)S(1)}, bf16[272,1024]{1,0:T(8,128)(2,1)S(1)}, u32[]{:S(2)}, u32[]{:S(2)}) %collective-permute-start.3) | collective-permute-done | bytes 557088 | tf_op jit(solution)/shard_map/ppermute | solution.py:695
  18.4 3.5 %project_other.1 = (bf16[272,256]{1,0:T(8,128)(2,1)S(1)}, bf16[272,256]{1,0:T(8,128)(2,1)S(1)}, bf16[272,256]{1,0:T(8,128)(2,1)S(1)}, bf16[272,256]{1,0:T(8,128)(2,1)S(1)}) custom-call(bf16[272,1024]{1,0:T(8,128)(2,1)S(1)} %collective-permute-done.3.tokens, bf16[1024,2048]{1,0:T(8,128)(2,1)} %in_proj_hbm.1, bf16[1024,2048]{1,0:T(8,128)(2,1)} %in_proj_hbm.1), custom_call_target="tpu_custom_call" | custom-call | flops 536870912 | bytes 5242880 | tf_op jit(solution)/shard_map/project_other/pallas_call | solution.py:102
  22.6 1.4 %collective-permute-start.8 = (bf16[272,256]{1,0:T(8,128)(2,1)S(1)}, bf16[272,256]{1,0:T(8,128)(2,1)S(1)}, u32[]{:S(2)}, u32[]{:S(2)}) collective-permute-start(bf16[272,256]{1,0:T(8,128)(2,1)S(1)} %get-tuple-element.70), channel_id=1, source_target_pairs={{0,2},{1,3},{2,4},{3,5},{4,6},{5,7},{6,0},{7,1},{8,10},{9,11},{10,... | collective-permute-start | bytes 417800 | tf_op jit(solution)/shard_map/ppermute | solution.py:695
  24.5 3.6 %collective-permute-start.9 = (bf16[272,256]{1,0:T(8,128)(2,1)S(1)}, bf16[272,256]{1,0:T(8,128)(2,1)S(1)}, u32[]{:S(2)}, u32[]{:S(2)}) collective-permute-start(bf16[272,256]{1,0:T(8,128)(2,1)S(1)} %get-tuple-element.71), channel_id=1, source_target_pairs={{0,4},{1,5},{2,6},{3,7},{4,0},{5,1},{6,2},{7,3},{8,12},{9,13},{10,... | collective-permute-start | bytes 417800 | tf_op jit(solution)/shard_map/ppermute | solution.py:695
  30.2 3.2 %collective-permute-done.9.refs_10_ = bf16[272,256]{1,0:T(8,128)(2,1)S(1)} collective-permute-done((bf16[272,256]{1,0:T(8,128)(2,1)S(1)}, bf16[272,256]{1,0:T(8,128)(2,1)S(1)}, u32[]{:S(2)}, u32[]{:S(2)}) %collective-permute-start.9) | collective-permute-done | bytes 139296 | tf_op jit(solution)/shard_map/ppermute | solution.py:695
  36.2 8.8 %attend.1 = (f32[4,256,128]{2,1,0:T(8,128)}, s32[160]{0:T(256)S(1)}, s32[160]{0:T(256)S(1)}, s32[8]{0:T(128)S(1)}, bf16[33,128,128]{2,1,0:T(8,128)(2,1)S(1)}, /*...) custom-call(s32[4]{0:T(128)S(1)} %pad_add_fusion.ids, ...), custom_call_target="tpu_custom_call" | custom-call | flops 6000000000 | bytes 6291456 | tf_op jit(solution)/shard_map/attend/pallas_call | solution.py:337
  48.5 4.2 %all-to-all-start = ((f32[4,256,128]{2,1,0:T(8,128)}), f32[4,256,128]{2,1,0:T(8,128)S(1)}, u32[]{:S(2)}, u32[]{:S(2)}) async-start(f32[4,256,128]{2,1,0:T(8,128)} %get-tuple-element.73), calls=%async_computation | async-start | bytes 1048576 | tf_op jit(solution)/shard_map/all_to_all | solution.py:707
  52.7 5.5 %gates.1 = (bf16[256,512]{1,0:T(8,128)(2,1)S(1)}, bf16[256,2048]{1,0:T(8,128)(2,1)S(1)}, f32[256,512]{1,0:T(8,128)S(1)}) custom-call(bf16[256,1024]{1,0:T(8,128)(2,1)} %tokens_hbm.1, bf16[1024,2048]{1,0:T(8,128)(2,1)} %in_proj_hbm.1, bf16[256,1024]{1,0:T(8,128)(2,1)} %cot_hbm.1, bf16[512,1024]{1,0:T(8,128)(2,1)} %out_proj.3), custom_call_target="tpu_custom_call" | custom-call | flops 1073741824 | bytes 7340032 | tf_op jit(solution)/shard_map/gates/pallas_call | solution.py:134
  58.2 4.9 %all-to-all-done.heads = f32[4,256,128]{2,1,0:T(8,128)S(1)} async-done(((f32[4,256,128]{2,1,0:T(8,128)}), f32[4,256,128]{2,1,0:T(8,128)S(1)}, u32[]{:S(2)}, u32[]{:S(2)}) %all-to-all-start) | async-done | bytes 524320 | tf_op jit(solution)/shard_map/all_to_all | solution.py:707
  63.1 1.2 middle.1
  65.0 3.4 %all-to-all-start.1 = ((bf16[4,256,128]{2,1,0:T(8,128)(2,1)}), bf16[4,256,128]{2,1,0:T(8,128)(2,1)S(1)}, u32[]{:S(2)}, u32[]{:S(2)}) async-start(bf16[4,256,128]{2,1,0:T(8,128)(2,1)} %get-tuple-element.87), calls=%async_computation.1 | async-start | bytes 524288 | tf_op jit(solution)/shard_map/all_to_all | solution.py:707
  68.4 2.8 %finish_output.1 = (bf16[256,1024]{1,0:T(8,128)(2,1)}, f32[128,1024]{1,0:T(8,128)S(1)}, bf16[128,1024]{1,0:T(8,128)(2,1)S(1)}, bf16[128,1024]{1,0:T(8,128)(2,1)S(1)}, bf16[128,1024]{1,0:T(8,128)(2,1)S(1)}) custom-call(s32[4]{0:T(128)S(1)} %pad_add_fusion.ids, bf16[256,1024]{1,0:T(8,128)(2,1)} %tokens_hbm.1, bf16[256,1024]{1,0:T(8,128)(2,1)} %cot_hbm.1, ...), custom_call_target="tpu_custom_call" | custom-call | flops 805306368 | bytes 5242880 | tf_op jit(solution)/shard_map/finish_output/pallas_call | solution.py:407
  71.2 4.0 %all-to-all-done.1.refs_4_ = bf16[4,256,128]{2,1,0:T(8,128)(2,1)S(1)} async-done(((bf16[4,256,128]{2,1,0:T(8,128)(2,1)}), bf16[4,256,128]{2,1,0:T(8,128)(2,1)S(1)}, u32[]{:S(2)}, u32[]{:S(2)}) %all-to-all-start.1) | async-done | bytes 262176 | tf_op jit(solution)/shard_map/all_to_all | solution.py:707
  75.2 2.0 %collective-permute-start.18 = (bf16[128,1024]{1,0:T(8,128)(2,1)S(1)}, bf16[128,1024]{1,0:T(8,128)(2,1)S(1)}, u32[]{:S(2)}, u32[]{:S(2)}) collective-permute-start(bf16[128,1024]{1,0:T(8,128)(2,1)S(1)} %get-tuple-element.99), channel_id=1, source_target_pairs={{0,32},{16,48},{32,0},{48,16},{64,96},{80,112},{96,64},{112,80},{1... | collective-permute-start | bytes 786440 | tf_op jit(solution)/shard_map/ppermute | solution.py:703
  77.3 1.6 %collective-permute-start.19 = (bf16[128,1024]{1,0:T(8,128)(2,1)S(1)}, bf16[128,1024]{1,0:T(8,128)(2,1)S(1)}, u32[]{:S(2)}, u32[]{:S(2)}) collective-permute-start(bf16[128,1024]{1,0:T(8,128)(2,1)S(1)} %get-tuple-element.100), channel_id=1, source_target_pairs={{0,48},{16,0},{32,16},{48,32},{64,112},{80,64},{96,80},{112,96},{1... | collective-permute-start | bytes 786440 | tf_op jit(solution)/shard_map/ppermute | solution.py:703
  78.9 11.9 %attend_back.1 = (bf16[4,256,256]{2,1,0:T(8,128)(2,1)S(1)}, bf16[4,256,256]{2,1,0:T(8,128)(2,1)S(1)}, bf16[4,256,256]{2,1,0:T(8,128)(2,1)S(1)}, bf16[4,256,256]{...) custom-call(s32[4]{0:T(128)S(1)} %pad_add_fusion.ids, f32[32]{0:T(128)S(1)} %pad_maximum_fusion.1.table, ...), custom_call_target="tpu_custom_call" | custom-call | flops 12000000000 | bytes 8388608 | tf_op jit(solution)/shard_map/attend_back/pallas_call | solution.py:526
  92.2 1.5 %collective-permute-done.21.rab_got = f32[16,128]{1,0:T(8,128)S(1)} collective-permute-done((f32[16,128]{1,0:T(8,128)S(1)}, f32[16,128]{1,0:T(8,128)S(1)}, u32[]{:S(2)}, u32[]{:S(2)}) %collective-permute-start.21) | collective-permute-done | bytes 8224 | tf_op jit(solution)/shard_map/ppermute | solution.py:695
  94.1 3.5 %collective-permute-start.26 = (bf16[304,256]{1,0:T(8,128)(2,1)S(1)}, bf16[304,256]{1,0:T(8,128)(2,1)S(1)}, u32[]{:S(2)}, u32[]{:S(2)}) collective-permute-start(bf16[304,256]{1,0:T(8,128)(2,1)S(1)} %get-tuple-element.107), channel_id=1, source_target_pairs={{0,10},{1,11},{2,12},{3,13},{4,14},{5,15},{6,8},{7,9},{8,2},{9,3},... | collective-permute-start | bytes 466952 | tf_op jit(solution)/shard_map/ppermute | solution.py:695
  97.7 4.1 %collective-permute-start.23 = (bf16[432,256]{1,0:T(8,128)(2,1)S(1)}, bf16[432,256]{1,0:T(8,128)(2,1)S(1)}, u32[]{:S(2)}, u32[]{:S(2)}) collective-permute-start(bf16[432,256]{1,0:T(8,128)(2,1)S(1)} %get-tuple-element.104), channel_id=1, source_target_pairs={{0,4},{1,5},{2,6},{3,7},{4,0},{5,1},{6,2},{7,3},{8,12},{9,13},{10,... | collective-permute-start | bytes 663560 | tf_op jit(solution)/shard_map/ppermute | solution.py:695
  103.3 2.4 %collective-permute-done.26.refs_5_.refs_13_ = bf16[304,256]{1,0:T(8,128)(2,1)S(1)} collective-permute-done((bf16[304,256]{1,0:T(8,128)(2,1)S(1)}, bf16[304,256]{1,0:T(8,128)(2,1)S(1)}, u32[]{:S(2)}, u32[]{:S(2)}) %collective-permute-start.26) | collective-permute-done | bytes 155680 | tf_op jit(solution)/shard_map/ppermute | solution.py:695
  105.7 3.2 %collective-permute-start.28 = (bf16[304,256]{1,0:T(8,128)(2,1)S(1)}, bf16[304,256]{1,0:T(8,128)(2,1)S(1)}, u32[]{:S(2)}, u32[]{:S(2)}) collective-permute-start(bf16[304,256]{1,0:T(8,128)(2,1)S(1)} %get-tuple-element.109), channel_id=1, source_target_pairs={{0,14},{1,15},{2,8},{3,9},{4,10},{5,11},{6,12},{7,13},{8,6},{9,7},... | collective-permute-start | bytes 466952 | tf_op jit(solution)/shard_map/ppermute | solution.py:695
  108.9 3.5 %collective-permute-done.27.refs_6_.refs_14_ = bf16[304,256]{1,0:T(8,128)(2,1)S(1)} collective-permute-done((bf16[304,256]{1,0:T(8,128)(2,1)S(1)}, bf16[304,256]{1,0:T(8,128)(2,1)S(1)}, u32[]{:S(2)}, u32[]{:S(2)}) %collective-permute-start.27) | collective-permute-done | bytes 155680 | tf_op jit(solution)/shard_map/ppermute | solution.py:695
  112.5 1.3 %collective-permute-done.28.refs_7_.refs_15_ = bf16[304,256]{1,0:T(8,128)(2,1)S(1)} collective-permute-done((bf16[304,256]{1,0:T(8,128)(2,1)S(1)}, bf16[304,256]{1,0:T(8,128)(2,1)S(1)}, u32[]{:S(2)}, u32[]{:S(2)}) %collective-permute-start.28) | collective-permute-done | bytes 155680 | tf_op jit(solution)/shard_map/ppermute | solution.py:695
  113.8 3.8 %collective-permute-done.23.refs_2_.refs_10_ = bf16[432,256]{1,0:T(8,128)(2,1)S(1)} collective-permute-done((bf16[432,256]{1,0:T(8,128)(2,1)S(1)}, bf16[432,256]{1,0:T(8,128)(2,1)S(1)}, u32[]{:S(2)}, u32[]{:S(2)}) %collective-permute-start.23) | collective-permute-done | bytes 221216 | tf_op jit(solution)/shard_map/ppermute | solution.py:695
  118.0 1.4 %collect.1 = f32[8,8,1024]{2,1,0:T(8,128)} custom-call(s32[4]{0:T(128)S(1)} %pad_add_fusion.ids, bf16[432,256]{1,0:T(8,128)(2,1)S(1)} %get-tuple-element.102.refs_0_.refs_8_, bf16[432,256]{1,0:T(8,128)(2,1)S(1)} %collective-permute-done.22.refs_1_.refs_9_, bf16[432,256]{1,0:T(8,128)(2,1)S(1)} %collective-permute-done.23.refs_2_.refs_10_, ...), custom_call_target="tpu_custom_call" | custom-call | flops 65536 | bytes 262144 | tf_op jit(solution)/shard_map/collect/pallas_call | solution.py:601
  119.5 3.4 %all-to-all-start.2 = ((f32[8,8,1024]{2,1,0:T(8,128)}), f32[8,8,1024]{2,1,0:T(8,128)S(1)}, u32[]{:S(2)}, u32[]{:S(2)}) async-start(f32[8,8,1024]{2,1,0:T(8,128)} %collect.1), calls=%async_computation.2 | async-start | bytes 524288 | tf_op jit(solution)/shard_map/all_to_all | solution.py:749
  122.9 7.5 %finish_grad.1 = bf16[256,1024]{1,0:T(8,128)(2,1)} custom-call(s32[4]{0:T(128)} %copy-done.10, bf16[256,512]{1,0:T(8,128)(2,1)} %copy-done.9, bf16[1024,2048]{1,0:T(8,128)(2,1)} %in_proj_hbm.1, bf16[256,1024]{1,0:T(8,128)(2,1)} %tokens_hbm.1, bf16[256,1024]{1,0:T(8,128)(2,1)} %cot_hbm.1, bf16[256,2048]{1,0:T(8,128)(2,1)} %copy-done, ...), custom_call_target="tpu_custom_call" | custom-call | flops 1073741824 | bytes 8388608 | tf_op jit(solution)/shard_map/finish_grad/pallas_call | solution.py:663
  (91 shorter events, 17.0 us)
Async XLA Ops:
  2.4 15.9 %collective-permute-start.3 = (bf16[272,1024]{1,0:T(8,128)(2,1)S(1)}, bf16[272,1024]{1,0:T(8,128)(2,1)S(1)}, u32[]{:S(2)}, u32[]{:S(2)}) collective-permute-start(bf16[272,1024]{1,0:T(8,128)(2,1)S(1)} %pad_maximum_fusion.tokens), channel_id=1, source_target_pairs={{0,8},{1,9},{2,10},{3,11},{4,12},{5,13},{6,14},{7,15},{8,0},{9,1},... | collective-permute-start | bytes 1671176 | tf_op jit(solution)/shard_map/ppermute | solution.py:695
  7.9 14.0 %collective-permute-start = (bf16[272,384]{1,0:T(8,128)(2,1)S(1)}, bf16[272,384]{1,0:T(8,128)(2,1)S(1)}, u32[]{:S(2)}, u32[]{:S(2)}) collective-permute-start(bf16[272,384]{1,0:T(8,128)(2,1)S(1)} %get-tuple-element.58), channel_id=1, source_target_pairs={{0,2},{1,3},{2,4},{3,5},{4,6},{5,7},{6,0},{7,1},{8,10},{9,11},{10,... | collective-permute-start | bytes 626696 | tf_op jit(solution)/shard_map/ppermute | solution.py:695
  9.9 12.7 %collective-permute-start.1 = (bf16[272,384]{1,0:T(8,128)(2,1)S(1)}, bf16[272,384]{1,0:T(8,128)(2,1)S(1)}, u32[]{:S(2)}, u32[]{:S(2)}) collective-permute-start(bf16[272,384]{1,0:T(8,128)(2,1)S(1)} %get-tuple-element.59), channel_id=1, source_target_pairs={{0,4},{1,5},{2,6},{3,7},{4,0},{5,1},{6,2},{7,3},{8,12},{9,13},{10,... | collective-permute-start | bytes 626696 | tf_op jit(solution)/shard_map/ppermute | solution.py:695
  13.5 9.1 %collective-permute-start.2 = (bf16[272,384]{1,0:T(8,128)(2,1)S(1)}, bf16[272,384]{1,0:T(8,128)(2,1)S(1)}, u32[]{:S(2)}, u32[]{:S(2)}) collective-permute-start(bf16[272,384]{1,0:T(8,128)(2,1)S(1)} %get-tuple-element.60), channel_id=1, source_target_pairs={{0,6},{1,7},{2,0},{3,1},{4,2},{5,3},{6,4},{7,5},{8,14},{9,15},{10,... | collective-permute-start | bytes 626696 | tf_op jit(solution)/shard_map/ppermute | solution.py:695
  22.6 6.9 %collective-permute-start.8 = (bf16[272,256]{1,0:T(8,128)(2,1)S(1)}, bf16[272,256]{1,0:T(8,128)(2,1)S(1)}, u32[]{:S(2)}, u32[]{:S(2)}) collective-permute-start(bf16[272,256]{1,0:T(8,128)(2,1)S(1)} %get-tuple-element.70), channel_id=1, source_target_pairs={{0,2},{1,3},{2,4},{3,5},{4,6},{5,7},{6,0},{7,1},{8,10},{9,11},{10,... | collective-permute-start | bytes 417800 | tf_op jit(solution)/shard_map/ppermute | solution.py:695
  23.9 10.7 %collective-permute-start.4 = (bf16[272,384]{1,0:T(8,128)(2,1)S(1)}, bf16[272,384]{1,0:T(8,128)(2,1)S(1)}, u32[]{:S(2)}, u32[]{:S(2)}) collective-permute-start(bf16[272,384]{1,0:T(8,128)(2,1)S(1)} %get-tuple-element.65.refs_0_), channel_id=1, source_target_pairs={{0,1},{1,0},{2,3},{3,2},{4,5},{5,4},{6,7},{7,6},{8,9},{9,8},{10,11... | collective-permute-start | bytes 626696 | tf_op jit(solution)/shard_map/ppermute | solution.py:695
  23.9 10.8 %collective-permute-start.5 = (bf16[272,384]{1,0:T(8,128)(2,1)S(1)}, bf16[272,384]{1,0:T(8,128)(2,1)S(1)}, u32[]{:S(2)}, u32[]{:S(2)}) collective-permute-start(bf16[272,384]{1,0:T(8,128)(2,1)S(1)} %collective-permute-done.refs_1_), channel_id=1, source_target_pairs={{0,1},{1,0},{2,3},{3,2},{4,5},{5,4},{6,7},{7,6},{8,9},{9,8},{10,11... | collective-permute-start | bytes 626696 | tf_op jit(solution)/shard_map/ppermute | solution.py:695
  24.5 8.9 %collective-permute-start.9 = (bf16[272,256]{1,0:T(8,128)(2,1)S(1)}, bf16[272,256]{1,0:T(8,128)(2,1)S(1)}, u32[]{:S(2)}, u32[]{:S(2)}) collective-permute-start(bf16[272,256]{1,0:T(8,128)(2,1)S(1)} %get-tuple-element.71), channel_id=1, source_target_pairs={{0,4},{1,5},{2,6},{3,7},{4,0},{5,1},{6,2},{7,3},{8,12},{9,13},{10,... | collective-permute-start | bytes 417800 | tf_op jit(solution)/shard_map/ppermute | solution.py:695
  28.0 6.1 %collective-permute-start.10 = (bf16[272,256]{1,0:T(8,128)(2,1)S(1)}, bf16[272,256]{1,0:T(8,128)(2,1)S(1)}, u32[]{:S(2)}, u32[]{:S(2)}) collective-permute-start(bf16[272,256]{1,0:T(8,128)(2,1)S(1)} %get-tuple-element.72), channel_id=1, source_target_pairs={{0,6},{1,7},{2,0},{3,1},{4,2},{5,3},{6,4},{7,5},{8,14},{9,15},{10,... | collective-permute-start | bytes 417800 | tf_op jit(solution)/shard_map/ppermute | solution.py:695
  29.5 4.7 %collective-permute-start.11 = (bf16[272,256]{1,0:T(8,128)(2,1)S(1)}, bf16[272,256]{1,0:T(8,128)(2,1)S(1)}, u32[]{:S(2)}, u32[]{:S(2)}) collective-permute-start(bf16[272,256]{1,0:T(8,128)(2,1)S(1)} %get-tuple-element.69.refs_8_), channel_id=1, source_target_pairs={{0,1},{1,0},{2,3},{3,2},{4,5},{5,4},{6,7},{7,6},{8,9},{9,8},{10,11... | collective-permute-start | bytes 417800 | tf_op jit(solution)/shard_map/ppermute | solution.py:695
  33.4 2.0 %collective-permute-start.6 = (bf16[272,384]{1,0:T(8,128)(2,1)S(1)}, bf16[272,384]{1,0:T(8,128)(2,1)S(1)}, u32[]{:S(2)}, u32[]{:S(2)}) collective-permute-start(bf16[272,384]{1,0:T(8,128)(2,1)S(1)} %collective-permute-done.1.refs_2_), channel_id=1, source_target_pairs={{0,1},{1,0},{2,3},{3,2},{4,5},{5,4},{6,7},{7,6},{8,9},{9,8},{10,11... | collective-permute-start | bytes 626696 | tf_op jit(solution)/shard_map/ppermute | solution.py:695
  34.2 1.5 %collective-permute-start.7 = (bf16[272,384]{1,0:T(8,128)(2,1)S(1)}, bf16[272,384]{1,0:T(8,128)(2,1)S(1)}, u32[]{:S(2)}, u32[]{:S(2)}) collective-permute-start(bf16[272,384]{1,0:T(8,128)(2,1)S(1)} %collective-permute-done.2.refs_3_), channel_id=1, source_target_pairs={{0,1},{1,0},{2,3},{3,2},{4,5},{5,4},{6,7},{7,6},{8,9},{9,8},{10,11... | collective-permute-start | bytes 626696 | tf_op jit(solution)/shard_map/ppermute | solution.py:695
  34.2 1.7 %collective-permute-start.12 = (bf16[272,256]{1,0:T(8,128)(2,1)S(1)}, bf16[272,256]{1,0:T(8,128)(2,1)S(1)}, u32[]{:S(2)}, u32[]{:S(2)}) collective-permute-start(bf16[272,256]{1,0:T(8,128)(2,1)S(1)} %collective-permute-done.8.refs_9_), channel_id=1, source_target_pairs={{0,1},{1,0},{2,3},{3,2},{4,5},{5,4},{6,7},{7,6},{8,9},{9,8},{10,11... | collective-permute-start | bytes 417800 | tf_op jit(solution)/shard_map/ppermute | solution.py:695
  34.7 1.4 %collective-permute-start.13 = (bf16[272,256]{1,0:T(8,128)(2,1)S(1)}, bf16[272,256]{1,0:T(8,128)(2,1)S(1)}, u32[]{:S(2)}, u32[]{:S(2)}) collective-permute-start(bf16[272,256]{1,0:T(8,128)(2,1)S(1)} %collective-permute-done.9.refs_10_), channel_id=1, source_target_pairs={{0,1},{1,0},{2,3},{3,2},{4,5},{5,4},{6,7},{7,6},{8,9},{9,8},{10,11... | collective-permute-start | bytes 417800 | tf_op jit(solution)/shard_map/ppermute | solution.py:695
  34.8 1.5 %collective-permute-start.14 = (bf16[272,256]{1,0:T(8,128)(2,1)S(1)}, bf16[272,256]{1,0:T(8,128)(2,1)S(1)}, u32[]{:S(2)}, u32[]{:S(2)}) collective-permute-start(bf16[272,256]{1,0:T(8,128)(2,1)S(1)} %collective-permute-done.10.refs_11_), channel_id=1, source_target_pairs={{0,1},{1,0},{2,3},{3,2},{4,5},{5,4},{6,7},{7,6},{8,9},{9,8},{10,11... | collective-permute-start | bytes 417800 | tf_op jit(solution)/shard_map/ppermute | solution.py:695
  48.5 14.7 %all-to-all-start = ((f32[4,256,128]{2,1,0:T(8,128)}), f32[4,256,128]{2,1,0:T(8,128)S(1)}, u32[]{:S(2)}, u32[]{:S(2)}) async-start(f32[4,256,128]{2,1,0:T(8,128)} %get-tuple-element.73), calls=%async_computation | async-start | bytes 1048576 | tf_op jit(solution)/shard_map/all_to_all | solution.py:707
  65.0 10.3 %all-to-all-start.1 = ((bf16[4,256,128]{2,1,0:T(8,128)(2,1)}), bf16[4,256,128]{2,1,0:T(8,128)(2,1)S(1)}, u32[]{:S(2)}, u32[]{:S(2)}) async-start(bf16[4,256,128]{2,1,0:T(8,128)(2,1)} %get-tuple-element.87), calls=%async_computation.1 | async-start | bytes 524288 | tf_op jit(solution)/shard_map/all_to_all | solution.py:707
  75.2 16.2 %collective-permute-start.17 = (bf16[128,1024]{1,0:T(8,128)(2,1)S(1)}, bf16[128,1024]{1,0:T(8,128)(2,1)S(1)}, u32[]{:S(2)}, u32[]{:S(2)}) collective-permute-start(bf16[128,1024]{1,0:T(8,128)(2,1)S(1)} %get-tuple-element.98), channel_id=1, source_target_pairs={{0,16},{16,32},{32,48},{48,0},{64,80},{80,96},{96,112},{112,64},{1... | collective-permute-start | bytes 786440 | tf_op jit(solution)/shard_map/ppermute | solution.py:703
  75.2 16.2 %collective-permute-start.18 = (bf16[128,1024]{1,0:T(8,128)(2,1)S(1)}, bf16[128,1024]{1,0:T(8,128)(2,1)S(1)}, u32[]{:S(2)}, u32[]{:S(2)}) collective-permute-start(bf16[128,1024]{1,0:T(8,128)(2,1)S(1)} %get-tuple-element.99), channel_id=1, source_target_pairs={{0,32},{16,48},{32,0},{48,16},{64,96},{80,112},{96,64},{112,80},{1... | collective-permute-start | bytes 786440 | tf_op jit(solution)/shard_map/ppermute | solution.py:703
  77.3 14.1 %collective-permute-start.19 = (bf16[128,1024]{1,0:T(8,128)(2,1)S(1)}, bf16[128,1024]{1,0:T(8,128)(2,1)S(1)}, u32[]{:S(2)}, u32[]{:S(2)}) collective-permute-start(bf16[128,1024]{1,0:T(8,128)(2,1)S(1)} %get-tuple-element.100), channel_id=1, source_target_pairs={{0,48},{16,0},{32,16},{48,32},{64,112},{80,64},{96,80},{112,96},{1... | collective-permute-start | bytes 786440 | tf_op jit(solution)/shard_map/ppermute | solution.py:703
  90.8 2.9 %collective-permute-start.15 = (bf16[4,256,256]{2,1,0:T(8,128)(2,1)S(1)}, bf16[4,256,256]{2,1,0:T(8,128)(2,1)S(1)}, u32[]{:S(2)}, u32[]{:S(2)}) collective-permute-start(bf16[4,256,256]{2,1,0:T(8,128)(2,1)S(1)} %get-tuple-element.94), channel_id=1, source_target_pairs={{0,1},{1,0},{2,3},{3,2},{4,5},{5,4},{6,7},{7,6},{8,9},{9,8},{10,11... | collective-permute-start | bytes 1572872 | tf_op jit(solution)/shard_map/ppermute | solution.py:695
  90.9 2.9 %collective-permute-start.16 = (bf16[4,256,256]{2,1,0:T(8,128)(2,1)S(1)}, bf16[4,256,256]{2,1,0:T(8,128)(2,1)S(1)}, u32[]{:S(2)}, u32[]{:S(2)}) collective-permute-start(bf16[4,256,256]{2,1,0:T(8,128)(2,1)S(1)} %get-tuple-element.95), channel_id=1, source_target_pairs={{0,1},{1,0},{2,3},{3,2},{4,5},{5,4},{6,7},{7,6},{8,9},{9,8},{10,11... | collective-permute-start | bytes 1572872 | tf_op jit(solution)/shard_map/ppermute | solution.py:695
  91.6 2.2 %collective-permute-start.20 = (bf16[64,1024]{1,0:T(8,128)(2,1)S(1)}, bf16[64,1024]{1,0:T(8,128)(2,1)S(1)}, u32[]{:S(2)}, u32[]{:S(2)}) collective-permute-start(bf16[64,1024]{1,0:T(8,128)(2,1)S(1)} %slice.23), channel_id=1, source_target_pairs={{0,1},{1,0},{2,3},{3,2},{4,5},{5,4},{6,7},{7,6},{8,9},{9,8},{10,11... | collective-permute-start | bytes 393224 | tf_op jit(solution)/shard_map/ppermute | solution.py:695
  91.8 2.0 %collective-permute-start.21 = (f32[16,128]{1,0:T(8,128)S(1)}, f32[16,128]{1,0:T(8,128)S(1)}, u32[]{:S(2)}, u32[]{:S(2)}) collective-permute-start(f32[16,128]{1,0:T(8,128)S(1)} %get-tuple-element.101.rab), channel_id=1, source_target_pairs={{0,1},{1,0},{2,3},{3,2},{4,5},{5,4},{6,7},{7,6},{8,9},{9,8},{10,11... | collective-permute-start | bytes 24584 | tf_op jit(solution)/shard_map/ppermute | solution.py:695
  94.0 8.4 %collective-permute-start.25 = (bf16[304,256]{1,0:T(8,128)(2,1)S(1)}, bf16[304,256]{1,0:T(8,128)(2,1)S(1)}, u32[]{:S(2)}, u32[]{:S(2)}) collective-permute-start(bf16[304,256]{1,0:T(8,128)(2,1)S(1)} %get-tuple-element.106), channel_id=1, source_target_pairs={{0,8},{1,9},{2,10},{3,11},{4,12},{5,13},{6,14},{7,15},{8,0},{9,1},... | collective-permute-start | bytes 466952 | tf_op jit(solution)/shard_map/ppermute | solution.py:695
  94.1 11.6 %collective-permute-start.26 = (bf16[304,256]{1,0:T(8,128)(2,1)S(1)}, bf16[304,256]{1,0:T(8,128)(2,1)S(1)}, u32[]{:S(2)}, u32[]{:S(2)}) collective-permute-start(bf16[304,256]{1,0:T(8,128)(2,1)S(1)} %get-tuple-element.107), channel_id=1, source_target_pairs={{0,10},{1,11},{2,12},{3,13},{4,14},{5,15},{6,8},{7,9},{8,2},{9,3},... | collective-permute-start | bytes 466952 | tf_op jit(solution)/shard_map/ppermute | solution.py:695
  97.7 16.1 %collective-permute-start.22 = (bf16[432,256]{1,0:T(8,128)(2,1)S(1)}, bf16[432,256]{1,0:T(8,128)(2,1)S(1)}, u32[]{:S(2)}, u32[]{:S(2)}) collective-permute-start(bf16[432,256]{1,0:T(8,128)(2,1)S(1)} %get-tuple-element.103), channel_id=1, source_target_pairs={{0,2},{1,3},{2,4},{3,5},{4,6},{5,7},{6,0},{7,1},{8,10},{9,11},{10,... | collective-permute-start | bytes 663560 | tf_op jit(solution)/shard_map/ppermute | solution.py:695
  97.7 19.9 %collective-permute-start.23 = (bf16[432,256]{1,0:T(8,128)(2,1)S(1)}, bf16[432,256]{1,0:T(8,128)(2,1)S(1)}, u32[]{:S(2)}, u32[]{:S(2)}) collective-permute-start(bf16[432,256]{1,0:T(8,128)(2,1)S(1)} %get-tuple-element.104), channel_id=1, source_target_pairs={{0,4},{1,5},{2,6},{3,7},{4,0},{5,1},{6,2},{7,3},{8,12},{9,13},{10,... | collective-permute-start | bytes 663560 | tf_op jit(solution)/shard_map/ppermute | solution.py:695
  101.8 16.2 %collective-permute-start.24 = (bf16[432,256]{1,0:T(8,128)(2,1)S(1)}, bf16[432,256]{1,0:T(8,128)(2,1)S(1)}, u32[]{:S(2)}, u32[]{:S(2)}) collective-permute-start(bf16[432,256]{1,0:T(8,128)(2,1)S(1)} %get-tuple-element.105), channel_id=1, source_target_pairs={{0,6},{1,7},{2,0},{3,1},{4,2},{5,3},{6,4},{7,5},{8,14},{9,15},{10,... | collective-permute-start | bytes 663560 | tf_op jit(solution)/shard_map/ppermute | solution.py:695
  102.5 10.0 %collective-permute-start.27 = (bf16[304,256]{1,0:T(8,128)(2,1)S(1)}, bf16[304,256]{1,0:T(8,128)(2,1)S(1)}, u32[]{:S(2)}, u32[]{:S(2)}) collective-permute-start(bf16[304,256]{1,0:T(8,128)(2,1)S(1)} %get-tuple-element.108), channel_id=1, source_target_pairs={{0,12},{1,13},{2,14},{3,15},{4,8},{5,9},{6,10},{7,11},{8,4},{9,5},... | collective-permute-start | bytes 466952 | tf_op jit(solution)/shard_map/ppermute | solution.py:695
  105.7 8.1 %collective-permute-start.28 = (bf16[304,256]{1,0:T(8,128)(2,1)S(1)}, bf16[304,256]{1,0:T(8,128)(2,1)S(1)}, u32[]{:S(2)}, u32[]{:S(2)}) collective-permute-start(bf16[304,256]{1,0:T(8,128)(2,1)S(1)} %get-tuple-element.109), channel_id=1, source_target_pairs={{0,14},{1,15},{2,8},{3,9},{4,10},{5,11},{6,12},{7,13},{8,6},{9,7},... | collective-permute-start | bytes 466952 | tf_op jit(solution)/shard_map/ppermute | solution.py:695
  119.5 10.9 %all-to-all-start.2 = ((f32[8,8,1024]{2,1,0:T(8,128)}), f32[8,8,1024]{2,1,0:T(8,128)S(1)}, u32[]{:S(2)}, u32[]{:S(2)}) async-start(f32[8,8,1024]{2,1,0:T(8,128)} %collect.1), calls=%async_computation.2 | async-start | bytes 524288 | tf_op jit(solution)/shard_map/all_to_all | solution.py:749
  (17 other events, 215.0 us)

commit v4 on v3

--- a/solution.py
+++ b/solution.py
@@ -141,7 +141,11 @@
             whole((512, 1024)),
         ],
         out_specs=[whole((256, 512)), pl.BlockSpec((256, 512), lambda s: (0, s)), whole((256, 512))],
-        out_shape=[sds((256, 512), bf16), sds((256, 2048), bf16), sds((256, 512), f32)],
+        out_shape=[
+            pltpu.VMEM((256, 512), bf16),
+            pltpu.VMEM((256, 2048), bf16),
+            pltpu.VMEM((256, 512), f32),
+        ],
         scratch_shapes=[pltpu.VMEM((256, 1024), bf16)],
         compiler_params=params(16),
         cost_estimate=cost(2 * 256 * 1024 * 2048, 7 << 20),
@@ -339,8 +343,8 @@
         in_specs=[SMEM] * 3 + [VMEM] * 16,
         out_specs=[VMEM] + [SMEM] * 3 + [VMEM] * 4,
         out_shape=[sds((4, 256, T), f32), sds((LIST,), i32), sds((LIST,), i32), sds((8,), i32)]
-        + [sds((TILES + 1, T, T), bf16)] * 2
-        + [sds((QT + 1, T, T), bf16), sds((TILES + 1, 8, T), f32)],
+        + [pltpu.HBM((TILES + 1, T, T), bf16)] * 2
+        + [pltpu.HBM((QT + 1, T, T), bf16), pltpu.HBM((TILES + 1, 8, T), f32)],
         scratch_shapes=STAGE
         + [
             pltpu.VMEM((QT + 1, T, T), f32),
@@ -376,7 +380,11 @@
         grid=(1,),
         in_specs=[whole((4, 256, T)), whole((256, 512)), whole((256, 512)), whole((256, 512))],
         out_specs=[whole((256, 512)), whole((256, 512)), whole((4, 256, T))],
-        out_shape=[sds((256, 512), bf16), sds((256, 512), bf16), sds((4, 256, T), bf16)],
+        out_shape=[
+            pltpu.HBM((256, 512), bf16),
+            pltpu.HBM((256, 512), bf16),
+            sds((4, 256, T), bf16),
+        ],
         compiler_params=params(12),
         cost_estimate=cost(1 << 24, 3 << 20),
         name="middle",
@@ -412,7 +420,7 @@
         compiler_params=params(24),
         cost_estimate=cost(6 * 256 * 512 * 1024, 5 << 20),
         name="finish_output",
-    )(ids, in_hbm(tokens), in_hbm(cot), in_hbm(out_proj), mixed)
+    )(ids, in_hbm(tokens), in_hbm(cot), in_hbm(out_proj), in_hbm(mixed))
 
 
 def backward_kernel(ids, table, lengths, far, near, counts, *refs):
@@ -614,23 +622,63 @@
     )(ids, *same, *other, *same, *other)
 
 
-def final_kernel(ids, grad_gate, in_proj_hbm, tokens_hbm, cot_hbm, slope_hbm, *refs):
-    same, other, grad_in = refs[:4], refs[4:8], refs[8]
-    grad_pre, in_proj, tokens, cot, slope, sems = refs[9:]
+def lines_kernel(lines, proj_grad, rab_grad):
+    total = lines[0]
+    for d in range(1, 8):
+        total = total + lines[d]
+    proj_grad[...] = total[0:4]
+    rab_grad[...] = total[4:, 0:BUCKETS]
+
+
+def add_lines(lines):
+    return pl.pallas_call(
+        lines_kernel,
+        in_specs=[VMEM],
+        out_specs=[VMEM] * 2,
+        out_shape=[sds((4, 1024), f32), sds((HEADS, BUCKETS), f32)],
+        compiler_params=params(8),
+        cost_estimate=cost(1 << 16, 1 << 18),
+        name="add_lines",
+    )(lines)
+
+
+def ready_kernel(tokens, cot, in_proj, normed, inverse, cot_out, in_proj_out, sems):
+    copies = [
+        pltpu.make_async_copy(in_proj, in_proj_out, sems.at[0]),
+        pltpu.make_async_copy(cot, cot_out, sems.at[1]),
+    ]
+    for copy in copies:
+        copy.start()
+    shaped, scale = norm_rows(tokens[...].astype(f32))
+    normed[...] = shaped
+    inverse[...] = jnp.broadcast_to(scale, (256, T))
+    for copy in copies:
+        copy.wait()
+
+
+def make_ready(tokens, cot, in_proj):
+    hbm = pl.BlockSpec(memory_space=pltpu.HBM)
+    return pl.pallas_call(
+        ready_kernel,
+        in_specs=[VMEM, hbm, hbm],
+        out_specs=[VMEM] * 4,
+        out_shape=[
+            pltpu.VMEM((256, 1024), f32),
+            pltpu.VMEM((256, T), f32),
+            pltpu.VMEM((256, 1024), bf16),
+            pltpu.VMEM((1024, 2048), bf16),
+        ],
+        scratch_shapes=[pltpu.SemaphoreType.DMA((2,))],
+        compiler_params=params(16),
+        cost_estimate=cost(1 << 22, 6 << 20),
+        name="ready",
+    )(in_hbm(tokens), in_hbm(cot), in_hbm(in_proj))
+
+
+def final_kernel(ids, grad_gate, slope, normed, inverse, cot, in_proj, *refs):
+    same, other, grad_in, grad_pre = refs[:4], refs[4:8], refs[8], refs[9]
     z = ids[1]
-    first = pltpu.make_async_copy(slope_hbm, slope, sems.at[4])
-    weights = [
-        pltpu.make_async_copy(in_proj_hbm.at[pl.ds(i * 256, 256)], in_proj.at[i], sems.at[i])
-        for i in range(4)
-    ]
-    lasts = [
-        pltpu.make_async_copy(tokens_hbm, tokens, sems.at[5]),
-        pltpu.make_async_copy(cot_hbm, cot, sems.at[6]),
-    ]
-    for copy in [first] + weights + lasts:
-        copy.start()
     grad_pre[:, 0:512] = grad_gate[...]
-    first.wait()
     for t in range(4):
         head = (z + 4 - t) % 4
         column = lambda kind: pl.ds(pl.multiple_of(kind * 512 + head * T, T), T)
@@ -644,42 +692,22 @@
                 grad_pre[rows, column(kind)] = (
                     part * slope[rows, column(kind)].astype(f32)
                 ).astype(bf16)
-    parts = []
-    for i in range(4):
-        weights[i].wait()
-        parts.append(
-            lax.dot_general(grad_pre[...], in_proj[i], NT_DIMS, preferred_element_type=f32)
-        )
-    for copy in lasts:
-        copy.wait()
-    normed, inverse = norm_rows(tokens[...].astype(f32))
-    upstream = jnp.concatenate(parts, axis=1)
-    grad_in[...] = (cot[...].astype(f32) + norm_back(upstream, normed, inverse)).astype(bf16)
-
-
-def finish_grad(ids, tokens, cot, in_proj, slope, grad_gate, same, other):
-    whole = lambda shape: pl.BlockSpec(shape, lambda s: (0,) * len(shape))
-    hbm = pl.BlockSpec(memory_space=pltpu.HBM)
+    upstream = lax.dot_general(grad_pre[...], in_proj[...], NT_DIMS, preferred_element_type=f32)
+    back = norm_back(upstream, normed[...], inverse[:, 0:1])
+    grad_in[...] = (cot[...].astype(f32) + back).astype(bf16)
+
+
+def finish_grad(ids, ready, slope, grad_gate, same, other):
     return pl.pallas_call(
         final_kernel,
-        grid=(1,),
-        in_specs=[SMEM, whole((256, 512)), hbm, hbm, hbm, hbm]
-        + [whole((384, 256))] * 4
-        + [whole((256, 256))] * 4,
-        out_specs=whole((256, 1024)),
+        in_specs=[SMEM] + [VMEM] * 14,
+        out_specs=VMEM,
         out_shape=sds((256, 1024), bf16),
-        scratch_shapes=[
-            pltpu.VMEM((256, 2048), bf16),
-            pltpu.VMEM((4, 256, 2048), bf16),
-            pltpu.VMEM((256, 1024), bf16),
-            pltpu.VMEM((256, 1024), bf16),
-            pltpu.VMEM((256, 2048), bf16),
-            pltpu.SemaphoreType.DMA((7,)),
-        ],
-        compiler_params=params(56),
+        scratch_shapes=[pltpu.VMEM((256, 2048), bf16)],
+        compiler_params=params(24),
         cost_estimate=cost(2 * 256 * 1024 * 2048, 8 << 20),
         name="finish_grad",
-    )(ids, grad_gate, in_proj, tokens, cot, slope, *same, *other)
+    )(ids, grad_gate, slope, *ready, *same, *other)
 
 
 def move(y_xor, z_shift, core_xor):
@@ -716,8 +744,8 @@
     full = project(near_tokens, in_proj, block_mask)
     own = [full[0]] + [send(full[s], 0, s, 0) for s in (1, 2, 3)]
     pairs = project(far_tokens, in_proj)
-    own, pairs = lax.optimization_barrier((own, pairs))
     across = [pairs[0]] + [send(pairs[s], 0, s, 0) for s in (1, 2, 3)]
+    own, across[1] = lax.optimization_barrier((own, across[1]))
     gate, slope, grad_mix = make_gates(tokens, in_proj, cotangent, out_proj)
     own_twin = [send(part, 0, 0, 1) for part in own]
     across_twin = [send(part, 0, 0, 1) for part in across]
@@ -744,12 +772,14 @@
         proj = proj + part.astype(f32)
     proj_own, proj_got = proj[:64], send(proj[64:].astype(bf16), 0, 0, 1)
     messages = combine(mine_s, mine_o, got_s, got_o, dq, proj_own, proj_got, rab, rab_got)
+    messages, late_cot = lax.optimization_barrier((messages, cotangent))
+    ready = make_ready(tokens, late_cot, in_proj)
     same = [messages[0]] + [send(messages[s], 0, s, 0) for s in (1, 2, 3)]
     other = [send(messages[4 + s], 1, s, 0) for s in range(4)]
     lines = lax.all_to_all(collect(ids, same, other), "dp", 0, 0, tiled=True)
-    sums = jnp.sum(lines, axis=0)
-    grad_in = finish_grad(ids, tokens, cotangent, in_proj, slope, grad_gate, same, other)
-    return output, grad_in, sums[:4], sums[4:, :BUCKETS].T
+    proj_grad, rab_grad = add_lines(lines)
+    grad_in = finish_grad(ids, ready, slope, grad_gate, same, other)
+    return output, grad_in, proj_grad, rab_grad.T
 
 
 def solution(mesh):

time: 134 us -> 129 us (0.963); the launches traced: 132 us -> 129 us
  local copies, waits for them, and re-layouts: 5.38 us -> 0.06 us
  starting transfers between devices: 43.6 us -> 47.7 us
    unnamed x34 -> x6, local copies, waits for them, and re-layouts: 4.14 us -> 0.01 us
    all_to_all x1, starting transfers between devices: 3.37 us -> 5.66 us  [on_device(): lines = lax.all_to_all(collect(ids, same, other), 'dp', 0, 0, tiled=True)]
    ppermute x3, starting transfers between devices: 3.7 us -> 5.85 us  [send_x(): lax.ppermute(part, 'dp', [(d, d // 4 * 4 + (d + shift) % 4) for d in rang...]
    ppermute x3, waiting for transfers between devices: 0.01 us -> 1.52 us  [send_x(): lax.ppermute(part, 'dp', [(d, d // 4 * 4 + (d + shift) % 4) for d in rang...]
    pallas_call x1 -> x3, Pallas kernels: 7.54 us -> 7.4 us  [the longest x1 3.4 us: make_ready(): pl.pallas_call(ready_kernel, in_specs=[VMEM, hbm, hbm], out_specs=[VMEM]...]
  transfers between devices with their start and end apart: 32 -> 32, of which waited for: 18 -> 13; matrix products, arithmetic and copies ran while one was open for 1% -> 1% of each run, Pallas kernels for 27% -> 26%
where the time goes in v4:
time: 129 us
  starting transfers between devices  47.7 us (37%)
  Pallas kernels  46.3 us (36%)
  waiting for transfers between devices  31.5 us (24%)
  other arithmetic  2.77 us (2%)
    ppermute x26, starting transfers between devices, send(): return lax.ppermute(x, 'ctx', move(y_xor, z_shift, core_xor))  29.3 us
    ppermute x26, waiting for transfers between devices, send(): return lax.ppermute(x, 'ctx', move(y_xor, z_shift, core_xor))  22.1 us
    pallas_call x1, Pallas kernels, attend_back(): pl.pallas_call(backward_kernel, in_specs=[SMEM] * 6 + [VMEM] * 5, out_spe...  10.8 us
    pallas_call x1, Pallas kernels, attend(): pl.pallas_call(forward_kernel, in_specs=[SMEM] * 3 + [VMEM] * 16, out_spe...  9.08 us
    all_to_all x2, waiting for transfers between devices, swap_z(): lax.all_to_all(part, 'ctx', 0, 0, axis_index_groups=OVER_Z, tiled=True)  7.9 us
    pallas_call x2, Pallas kernels, project(): pl.pallas_call(functools.partial(project_kernel, int(own)), grid=(HEADS,)...  7.7 us
    all_to_all x2, starting transfers between devices, swap_z(): lax.all_to_all(part, 'ctx', 0, 0, axis_index_groups=OVER_Z, tiled=True)  6.89 us
    ppermute x3, starting transfers between devices, send_x(): lax.ppermute(part, 'dp', [(d, d // 4 * 4 + (d + shift) % 4) for d in rang...  5.85 us
  transfers between devices with their start and end apart: 32, of which 13 were waited for; matrix products, arithmetic and copies ran while one was open for 1% of the time, Pallas kernels for 26%

profile of v4, /device:TPU:24, one launch (start us, length us, event | category | flops | bytes accessed | tf_op | source)
XLA Modules:
  0.0 129.1 jit_solution(75314505647384525)
XLA Ops:
  2.4 1.3 %collective-permute-start.3 = (bf16[272,1024]{1,0:T(8,128)(2,1)S(1)}, bf16[272,1024]{1,0:T(8,128)(2,1)S(1)}, u32[]{:S(2)}, u32[]{:S(2)}) collective-permute-start(bf16[272,1024]{1,0:T(8,128)(2,1)S(1)} %pad_maximum_fusion.tokens), channel_id=1, source_target_pairs={{0,8},{1,9},{2,10},{3,11},{4,12},{5,13},{6,14},{7,15},{8,0},{9,1},... | collective-permute-start | bytes 1671176 | tf_op jit(solution)/shard_map/ppermute | solution.py:723
  3.8 4.2 %project_own.1 = (bf16[272,384]{1,0:T(8,128)(2,1)S(1)}, bf16[272,384]{1,0:T(8,128)(2,1)S(1)}, bf16[272,384]{1,0:T(8,128)(2,1)S(1)}, bf16[272,384]{1,0:T(8,128)(2,1)S(1)}) custom-call(bf16[272,1024]{1,0:T(8,128)(2,1)S(1)} %pad_maximum_fusion.tokens, s32[1,2,32]{2,1,0:T(2,128)} %refs_0_.2, bf16[1024,2048]{1,0:T(8,128)(2,1)} %in_proj.3, ...), custom_call_target="tpu_custom_call" | custom-call | flops 805306368 | bytes 5242880 | tf_op jit(solution)/shard_map/project_own/pallas_call | solution.py:102
  7.9 2.0 %collective-permute-start = (bf16[272,384]{1,0:T(8,128)(2,1)S(1)}, bf16[272,384]{1,0:T(8,128)(2,1)S(1)}, u32[]{:S(2)}, u32[]{:S(2)}) collective-permute-start(bf16[272,384]{1,0:T(8,128)(2,1)S(1)} %get-tuple-element.70), channel_id=1, source_target_pairs={{0,2},{1,3},{2,4},{3,5},{4,6},{5,7},{6,0},{7,1},{8,10},{9,11},{10,... | collective-permute-start | bytes 626696 | tf_op jit(solution)/shard_map/ppermute | solution.py:723
  9.9 3.6 %collective-permute-start.1 = (bf16[272,384]{1,0:T(8,128)(2,1)S(1)}, bf16[272,384]{1,0:T(8,128)(2,1)S(1)}, u32[]{:S(2)}, u32[]{:S(2)}) collective-permute-start(bf16[272,384]{1,0:T(8,128)(2,1)S(1)} %get-tuple-element.71), channel_id=1, source_target_pairs={{0,4},{1,5},{2,6},{3,7},{4,0},{5,1},{6,2},{7,3},{8,12},{9,13},{10,... | collective-permute-start | bytes 626696 | tf_op jit(solution)/shard_map/ppermute | solution.py:723
  14.5 3.9 %collective-permute-done.3.tokens = bf16[272,1024]{1,0:T(8,128)(2,1)S(1)} collective-permute-done((bf16[272,1024]{1,0:T(8,128)(2,1)S(1)}, bf16[272,1024]{1,0:T(8,128)(2,1)S(1)}, u32[]{:S(2)}, u32[]{:S(2)}) %collective-permute-start.3) | collective-permute-done | bytes 557088 | tf_op jit(solution)/shard_map/ppermute | solution.py:723
  18.4 3.5 %project_other.1 = (bf16[272,256]{1,0:T(8,128)(2,1)S(1)}, bf16[272,256]{1,0:T(8,128)(2,1)S(1)}, bf16[272,256]{1,0:T(8,128)(2,1)S(1)}, bf16[272,256]{1,0:T(8,128)(2,1)S(1)}) custom-call(bf16[272,1024]{1,0:T(8,128)(2,1)S(1)} %collective-permute-done.3.tokens, bf16[1024,2048]{1,0:T(8,128)(2,1)} %in_proj.3, bf16[1024,2048]{1,0:T(8,128)(2,1)} %in_proj.3), custom_call_target="tpu_custom_call" | custom-call | flops 536870912 | bytes 5242880 | tf_op jit(solution)/shard_map/project_other/pallas_call | solution.py:102
  21.9 2.0 %collective-permute-start.4 = (bf16[272,256]{1,0:T(8,128)(2,1)S(1)}, bf16[272,256]{1,0:T(8,128)(2,1)S(1)}, u32[]{:S(2)}, u32[]{:S(2)}) collective-permute-start(bf16[272,256]{1,0:T(8,128)(2,1)S(1)} %get-tuple-element.73), channel_id=1, source_target_pairs={{0,2},{1,3},{2,4},{3,5},{4,6},{5,7},{6,0},{7,1},{8,10},{9,11},{10,... | collective-permute-start | bytes 417800 | tf_op jit(solution)/shard_map/ppermute | solution.py:723
  23.9 3.6 %collective-permute-start.9 = (bf16[272,256]{1,0:T(8,128)(2,1)S(1)}, bf16[272,256]{1,0:T(8,128)(2,1)S(1)}, u32[]{:S(2)}, u32[]{:S(2)}) collective-permute-start(bf16[272,256]{1,0:T(8,128)(2,1)S(1)} %get-tuple-element.80), channel_id=1, source_target_pairs={{0,4},{1,5},{2,6},{3,7},{4,0},{5,1},{6,2},{7,3},{8,12},{9,13},{10,... | collective-permute-start | bytes 417800 | tf_op jit(solution)/shard_map/ppermute | solution.py:723
  28.5 1.7 %collective-permute-done.4.refs_9_ = bf16[272,256]{1,0:T(8,128)(2,1)S(1)} collective-permute-done((bf16[272,256]{1,0:T(8,128)(2,1)S(1)}, bf16[272,256]{1,0:T(8,128)(2,1)S(1)}, u32[]{:S(2)}, u32[]{:S(2)}) %collective-permute-start.4) | collective-permute-done | bytes 139296 | tf_op jit(solution)/shard_map/ppermute | solution.py:723
  30.2 2.8 %collective-permute-done.9.refs_10_ = bf16[272,256]{1,0:T(8,128)(2,1)S(1)} collective-permute-done((bf16[272,256]{1,0:T(8,128)(2,1)S(1)}, bf16[272,256]{1,0:T(8,128)(2,1)S(1)}, u32[]{:S(2)}, u32[]{:S(2)}) %collective-permute-start.9) | collective-permute-done | bytes 139296 | tf_op jit(solution)/shard_map/ppermute | solution.py:723
  36.5 9.1 %attend.1 = (f32[4,256,128]{2,1,0:T(8,128)}, s32[160]{0:T(256)S(1)}, s32[160]{0:T(256)S(1)}, s32[8]{0:T(128)S(1)}, bf16[33,128,128]{2,1,0:T(8,128)(2,1)}, /*inde...) custom-call(s32[4]{0:T(128)S(1)} %pad_add_fusion.ids, ...), custom_call_target="tpu_custom_call" | custom-call | flops 6000000000 | bytes 6291456 | tf_op jit(solution)/shard_map/attend/pallas_call | solution.py:341
  45.6 3.5 %all-to-all-start = ((f32[4,256,128]{2,1,0:T(8,128)}), f32[4,256,128]{2,1,0:T(8,128)S(1)}, u32[]{:S(2)}, u32[]{:S(2)}) async-start(f32[4,256,128]{2,1,0:T(8,128)} %get-tuple-element.82), calls=%async_computation | async-start | bytes 1048576 | tf_op jit(solution)/shard_map/all_to_all | solution.py:735
  49.1 5.5 %gates.1 = (bf16[256,512]{1,0:T(8,128)(2,1)S(1)}, bf16[256,2048]{1,0:T(8,128)(2,1)S(1)}, f32[256,512]{1,0:T(8,128)S(1)}) custom-call(bf16[256,1024]{1,0:T(8,128)(2,1)} %tokens.5, bf16[1024,2048]{1,0:T(8,128)(2,1)} %in_proj.3, bf16[256,1024]{1,0:T(8,128)(2,1)} %cot.4, bf16[512,1024]{1,0:T(8,128)(2,1)} %out_proj.3), custom_call_target="tpu_custom_call" | custom-call | flops 1073741824 | bytes 7340032 | tf_op jit(solution)/shard_map/gates/pallas_call | solution.py:134
  54.6 4.1 %all-to-all-done.heads = f32[4,256,128]{2,1,0:T(8,128)S(1)} async-done(((f32[4,256,128]{2,1,0:T(8,128)}), f32[4,256,128]{2,1,0:T(8,128)S(1)}, u32[]{:S(2)}, u32[]{:S(2)}) %all-to-all-start) | async-done | bytes 524320 | tf_op jit(solution)/shard_map/all_to_all | solution.py:735
  58.7 1.2 middle.1
  60.0 3.4 %all-to-all-start.1 = ((bf16[4,256,128]{2,1,0:T(8,128)(2,1)}), bf16[4,256,128]{2,1,0:T(8,128)(2,1)S(1)}, u32[]{:S(2)}, u32[]{:S(2)}) async-start(bf16[4,256,128]{2,1,0:T(8,128)(2,1)} %get-tuple-element.96), calls=%async_computation.1 | async-start | bytes 524288 | tf_op jit(solution)/shard_map/all_to_all | solution.py:735
  63.4 2.9 %finish_output.1 = (bf16[256,1024]{1,0:T(8,128)(2,1)}, f32[128,1024]{1,0:T(8,128)S(1)}, bf16[128,1024]{1,0:T(8,128)(2,1)S(1)}, bf16[128,1024]{1,0:T(8,128)(2,1)S(1)}, bf16[128,1024]{1,0:T(8,128)(2,1)S(1)}) custom-call(s32[4]{0:T(128)S(1)} %pad_add_fusion.ids, bf16[256,1024]{1,0:T(8,128)(2,1)} %tokens.5, bf16[256,1024]{1,0:T(8,128)(2,1)} %cot.4, ...), custom_call_target="tpu_custom_call" | custom-call | flops 805306368 | bytes 5242880 | tf_op jit(solution)/shard_map/finish_output/pallas_call | solution.py:415
  66.2 3.8 %all-to-all-done.1.refs_4_ = bf16[4,256,128]{2,1,0:T(8,128)(2,1)S(1)} async-done(((bf16[4,256,128]{2,1,0:T(8,128)(2,1)}), bf16[4,256,128]{2,1,0:T(8,128)(2,1)S(1)}, u32[]{:S(2)}, u32[]{:S(2)}) %all-to-all-start.1) | async-done | bytes 262176 | tf_op jit(solution)/shard_map/all_to_all | solution.py:735
  70.0 5.0 %collective-permute-start.19 = (bf16[128,1024]{1,0:T(8,128)(2,1)S(1)}, bf16[128,1024]{1,0:T(8,128)(2,1)S(1)}, u32[]{:S(2)}, u32[]{:S(2)}) collective-permute-start(bf16[128,1024]{1,0:T(8,128)(2,1)S(1)} %get-tuple-element.109), channel_id=1, source_target_pairs={{0,48},{16,0},{32,16},{48,32},{64,112},{80,64},{96,80},{112,96},{1... | collective-permute-start | bytes 786440 | tf_op jit(solution)/shard_map/ppermute | solution.py:731
  75.9 10.8 %attend_back.1 = (bf16[4,256,256]{2,1,0:T(8,128)(2,1)S(1)}, bf16[4,256,256]{2,1,0:T(8,128)(2,1)S(1)}, bf16[4,256,256]{2,1,0:T(8,128)(2,1)S(1)}, bf16[4,256,256]{...) custom-call(s32[4]{0:T(128)S(1)} %pad_add_fusion.ids, f32[32]{0:T(128)S(1)} %pad_maximum_fusion.1.table, ...), custom_call_target="tpu_custom_call" | custom-call | flops 12000000000 | bytes 8388608 | tf_op jit(solution)/shard_map/attend_back/pallas_call | solution.py:534
  87.2 1.5 %collective-permute-done.17 = bf16[128,1024]{1,0:T(8,128)(2,1)S(1)} collective-permute-done((bf16[128,1024]{1,0:T(8,128)(2,1)S(1)}, bf16[128,1024]{1,0:T(8,128)(2,1)S(1)}, u32[]{:S(2)}, u32[]{:S(2)}) %collective-permute-start.17) | collective-permute-done | bytes 262176 | tf_op jit(solution)/shard_map/ppermute | solution.py:731
  90.8 3.5 %collective-permute-start.26 = (bf16[304,256]{1,0:T(8,128)(2,1)S(1)}, bf16[304,256]{1,0:T(8,128)(2,1)S(1)}, u32[]{:S(2)}, u32[]{:S(2)}) collective-permute-start(bf16[304,256]{1,0:T(8,128)(2,1)S(1)} %get-tuple-element.129), channel_id=1, source_target_pairs={{0,10},{1,11},{2,12},{3,13},{4,14},{5,15},{6,8},{7,9},{8,2},{9,3},... | collective-permute-start | bytes 466952 | tf_op jit(solution)/shard_map/ppermute | solution.py:723
  94.6 3.8 %collective-permute-start.23 = (bf16[432,256]{1,0:T(8,128)(2,1)S(1)}, bf16[432,256]{1,0:T(8,128)(2,1)S(1)}, u32[]{:S(2)}, u32[]{:S(2)}) collective-permute-start(bf16[432,256]{1,0:T(8,128)(2,1)S(1)} %get-tuple-element.126), channel_id=1, source_target_pairs={{0,4},{1,5},{2,6},{3,7},{4,0},{5,1},{6,2},{7,3},{8,12},{9,13},{10,... | collective-permute-start | bytes 663560 | tf_op jit(solution)/shard_map/ppermute | solution.py:723
  100.0 2.6 %collective-permute-done.26.refs_5_.refs_13_ = bf16[304,256]{1,0:T(8,128)(2,1)S(1)} collective-permute-done((bf16[304,256]{1,0:T(8,128)(2,1)S(1)}, bf16[304,256]{1,0:T(8,128)(2,1)S(1)}, u32[]{:S(2)}, u32[]{:S(2)}) %collective-permute-start.26) | collective-permute-done | bytes 155680 | tf_op jit(solution)/shard_map/ppermute | solution.py:723
  102.5 3.0 %collective-permute-start.28 = (bf16[304,256]{1,0:T(8,128)(2,1)S(1)}, bf16[304,256]{1,0:T(8,128)(2,1)S(1)}, u32[]{:S(2)}, u32[]{:S(2)}) collective-permute-start(bf16[304,256]{1,0:T(8,128)(2,1)S(1)} %get-tuple-element.131), channel_id=1, source_target_pairs={{0,14},{1,15},{2,8},{3,9},{4,10},{5,11},{6,12},{7,13},{8,6},{9,7},... | collective-permute-start | bytes 466952 | tf_op jit(solution)/shard_map/ppermute | solution.py:723
  105.5 3.0 %collective-permute-done.27.refs_6_.refs_14_ = bf16[304,256]{1,0:T(8,128)(2,1)S(1)} collective-permute-done((bf16[304,256]{1,0:T(8,128)(2,1)S(1)}, bf16[304,256]{1,0:T(8,128)(2,1)S(1)}, u32[]{:S(2)}, u32[]{:S(2)}) %collective-permute-start.27) | collective-permute-done | bytes 155680 | tf_op jit(solution)/shard_map/ppermute | solution.py:723
  108.6 1.7 %collective-permute-done.28.refs_7_.refs_15_ = bf16[304,256]{1,0:T(8,128)(2,1)S(1)} collective-permute-done((bf16[304,256]{1,0:T(8,128)(2,1)S(1)}, bf16[304,256]{1,0:T(8,128)(2,1)S(1)}, u32[]{:S(2)}, u32[]{:S(2)}) %collective-permute-start.28) | collective-permute-done | bytes 155680 | tf_op jit(solution)/shard_map/ppermute | solution.py:723
  110.3 4.4 %collective-permute-done.23.refs_2_.refs_10_ = bf16[432,256]{1,0:T(8,128)(2,1)S(1)} collective-permute-done((bf16[432,256]{1,0:T(8,128)(2,1)S(1)}, bf16[432,256]{1,0:T(8,128)(2,1)S(1)}, u32[]{:S(2)}, u32[]{:S(2)}) %collective-permute-start.23) | collective-permute-done | bytes 221216 | tf_op jit(solution)/shard_map/ppermute | solution.py:723
  114.6 1.4 %collect.1 = f32[8,8,1024]{2,1,0:T(8,128)} custom-call(s32[4]{0:T(128)S(1)} %pad_add_fusion.ids, bf16[432,256]{1,0:T(8,128)(2,1)S(1)} %get-tuple-element.124.refs_0_.refs_8_, bf16[432,256]{1,0:T(8,128)(2,1)S(1)} %collective-permute-done.22.refs_1_.refs_9_, bf16[432,256]{1,0:T(8,128)(2,1)S(1)} %collective-permute-done.23.refs_2_.refs_10_, ...), custom_call_target="tpu_custom_call" | custom-call | flops 65536 | bytes 262144 | tf_op jit(solution)/shard_map/collect/pallas_call | solution.py:609
  116.1 5.7 %all-to-all-start.2 = ((f32[8,8,1024]{2,1,0:T(8,128)}), f32[8,8,1024]{2,1,0:T(8,128)S(1)}, u32[]{:S(2)}, u32[]{:S(2)}) async-start(f32[8,8,1024]{2,1,0:T(8,128)} %collect.1), calls=%async_computation.2 | async-start | bytes 524288 | tf_op jit(solution)/shard_map/all_to_all | solution.py:779
  121.7 3.4 %ready.1 = (f32[256,1024]{1,0:T(8,128)S(1)}, f32[256,128]{1,0:T(8,128)S(1)}, bf16[256,1024]{1,0:T(8,128)(2,1)S(1)}, bf16[1024,2048]{1,0:T(8,128)(2,1)S(1)}) custom-call(bf16[256,1024]{1,0:T(8,128)(2,1)} %tokens.5, bf16[256,1024]{1,0:T(8,128)(2,1)} %cot.4, bf16[1024,2048]{1,0:T(8,128)(2,1)} %in_proj.3), custom_call_target="tpu_custom_call" | custom-call | flops 4194304 | bytes 6291456 | tf_op jit(solution)/shard_map/ready/pallas_call | solution.py:661
  125.1 3.4 %finish_grad.1 = bf16[256,1024]{1,0:T(8,128)(2,1)} custom-call(s32[4]{0:T(128)S(1)} %pad_add_fusion.ids, bf16[256,512]{1,0:T(8,128)(2,1)S(1)} %copy-done, bf16[256,2048]{1,0:T(8,128)(2,1)S(1)} %get-tuple-element.84.slope, f32[256,1024]{1,0:T(8,128)S(1)} %get-tuple-element.120.normed, f32[256,128]{1,0:T(8,128)S(1)} %get-tuple-element.121.inverse, ...), custom_call_target="tpu_custom_call" | custom-call | flops 1073741824 | bytes 8388608 | tf_op jit(solution)/shard_map/finish_grad/pallas_call | solution.py:701
  (62 shorter events, 13.2 us)
Async XLA Ops:
  2.4 15.9 %collective-permute-start.3 = (bf16[272,1024]{1,0:T(8,128)(2,1)S(1)}, bf16[272,1024]{1,0:T(8,128)(2,1)S(1)}, u32[]{:S(2)}, u32[]{:S(2)}) collective-permute-start(bf16[272,1024]{1,0:T(8,128)(2,1)S(1)} %pad_maximum_fusion.tokens), channel_id=1, source_target_pairs={{0,8},{1,9},{2,10},{3,11},{4,12},{5,13},{6,14},{7,15},{8,0},{9,1},... | collective-permute-start | bytes 1671176 | tf_op jit(solution)/shard_map/ppermute | solution.py:723
  7.9 19.6 %collective-permute-start = (bf16[272,384]{1,0:T(8,128)(2,1)S(1)}, bf16[272,384]{1,0:T(8,128)(2,1)S(1)}, u32[]{:S(2)}, u32[]{:S(2)}) collective-permute-start(bf16[272,384]{1,0:T(8,128)(2,1)S(1)} %get-tuple-element.70), channel_id=1, source_target_pairs={{0,2},{1,3},{2,4},{3,5},{4,6},{5,7},{6,0},{7,1},{8,10},{9,11},{10,... | collective-permute-start | bytes 626696 | tf_op jit(solution)/shard_map/ppermute | solution.py:723
  9.9 18.6 %collective-permute-start.1 = (bf16[272,384]{1,0:T(8,128)(2,1)S(1)}, bf16[272,384]{1,0:T(8,128)(2,1)S(1)}, u32[]{:S(2)}, u32[]{:S(2)}) collective-permute-start(bf16[272,384]{1,0:T(8,128)(2,1)S(1)} %get-tuple-element.71), channel_id=1, source_target_pairs={{0,4},{1,5},{2,6},{3,7},{4,0},{5,1},{6,2},{7,3},{8,12},{9,13},{10,... | collective-permute-start | bytes 626696 | tf_op jit(solution)/shard_map/ppermute | solution.py:723
  13.5 15.0 %collective-permute-start.2 = (bf16[272,384]{1,0:T(8,128)(2,1)S(1)}, bf16[272,384]{1,0:T(8,128)(2,1)S(1)}, u32[]{:S(2)}, u32[]{:S(2)}) collective-permute-start(bf16[272,384]{1,0:T(8,128)(2,1)S(1)} %get-tuple-element.72), channel_id=1, source_target_pairs={{0,6},{1,7},{2,0},{3,1},{4,2},{5,3},{6,4},{7,5},{8,14},{9,15},{10,... | collective-permute-start | bytes 626696 | tf_op jit(solution)/shard_map/ppermute | solution.py:723
  21.9 8.3 %collective-permute-start.4 = (bf16[272,256]{1,0:T(8,128)(2,1)S(1)}, bf16[272,256]{1,0:T(8,128)(2,1)S(1)}, u32[]{:S(2)}, u32[]{:S(2)}) collective-permute-start(bf16[272,256]{1,0:T(8,128)(2,1)S(1)} %get-tuple-element.73), channel_id=1, source_target_pairs={{0,2},{1,3},{2,4},{3,5},{4,6},{5,7},{6,0},{7,1},{8,10},{9,11},{10,... | collective-permute-start | bytes 417800 | tf_op jit(solution)/shard_map/ppermute | solution.py:723
  23.9 9.1 %collective-permute-start.9 = (bf16[272,256]{1,0:T(8,128)(2,1)S(1)}, bf16[272,256]{1,0:T(8,128)(2,1)S(1)}, u32[]{:S(2)}, u32[]{:S(2)}) collective-permute-start(bf16[272,256]{1,0:T(8,128)(2,1)S(1)} %get-tuple-element.80), channel_id=1, source_target_pairs={{0,4},{1,5},{2,6},{3,7},{4,0},{5,1},{6,2},{7,3},{8,12},{9,13},{10,... | collective-permute-start | bytes 417800 | tf_op jit(solution)/shard_map/ppermute | solution.py:723
  27.5 6.7 %collective-permute-start.10 = (bf16[272,256]{1,0:T(8,128)(2,1)S(1)}, bf16[272,256]{1,0:T(8,128)(2,1)S(1)}, u32[]{:S(2)}, u32[]{:S(2)}) collective-permute-start(bf16[272,256]{1,0:T(8,128)(2,1)S(1)} %get-tuple-element.81), channel_id=1, source_target_pairs={{0,6},{1,7},{2,0},{3,1},{4,2},{5,3},{6,4},{7,5},{8,14},{9,15},{10,... | collective-permute-start | bytes 417800 | tf_op jit(solution)/shard_map/ppermute | solution.py:723
  28.5 5.8 %collective-permute-start.11 = (bf16[272,256]{1,0:T(8,128)(2,1)S(1)}, bf16[272,256]{1,0:T(8,128)(2,1)S(1)}, u32[]{:S(2)}, u32[]{:S(2)}) collective-permute-start(bf16[272,256]{1,0:T(8,128)(2,1)S(1)} %get-tuple-element.78.refs_8_), channel_id=1, source_target_pairs={{0,1},{1,0},{2,3},{3,2},{4,5},{5,4},{6,7},{7,6},{8,9},{9,8},{10,11... | collective-permute-start | bytes 417800 | tf_op jit(solution)/shard_map/ppermute | solution.py:723
  30.2 4.5 %collective-permute-start.12 = (bf16[272,256]{1,0:T(8,128)(2,1)S(1)}, bf16[272,256]{1,0:T(8,128)(2,1)S(1)}, u32[]{:S(2)}, u32[]{:S(2)}) collective-permute-start(bf16[272,256]{1,0:T(8,128)(2,1)S(1)} %collective-permute-done.4.refs_9_), channel_id=1, source_target_pairs={{0,1},{1,0},{2,3},{3,2},{4,5},{5,4},{6,7},{7,6},{8,9},{9,8},{10,11... | collective-permute-start | bytes 417800 | tf_op jit(solution)/shard_map/ppermute | solution.py:723
  33.0 1.8 %collective-permute-start.13 = (bf16[272,256]{1,0:T(8,128)(2,1)S(1)}, bf16[272,256]{1,0:T(8,128)(2,1)S(1)}, u32[]{:S(2)}, u32[]{:S(2)}) collective-permute-start(bf16[272,256]{1,0:T(8,128)(2,1)S(1)} %collective-permute-done.9.refs_10_), channel_id=1, source_target_pairs={{0,1},{1,0},{2,3},{3,2},{4,5},{5,4},{6,7},{7,6},{8,9},{9,8},{10,11... | collective-permute-start | bytes 417800 | tf_op jit(solution)/shard_map/ppermute | solution.py:723
  33.7 2.8 %collective-permute-start.5 = (bf16[272,384]{1,0:T(8,128)(2,1)S(1)}, bf16[272,384]{1,0:T(8,128)(2,1)S(1)}, u32[]{:S(2)}, u32[]{:S(2)}) collective-permute-start(bf16[272,384]{1,0:T(8,128)(2,1)S(1)} %get-tuple-element.74.refs_0_), channel_id=1, source_target_pairs={{0,1},{1,0},{2,3},{3,2},{4,5},{5,4},{6,7},{7,6},{8,9},{9,8},{10,11... | collective-permute-start | bytes 626696 | tf_op jit(solution)/shard_map/ppermute | solution.py:723
  34.2 2.3 %collective-permute-start.6 = (bf16[272,384]{1,0:T(8,128)(2,1)S(1)}, bf16[272,384]{1,0:T(8,128)(2,1)S(1)}, u32[]{:S(2)}, u32[]{:S(2)}) collective-permute-start(bf16[272,384]{1,0:T(8,128)(2,1)S(1)} %collective-permute-done.refs_1_), channel_id=1, source_target_pairs={{0,1},{1,0},{2,3},{3,2},{4,5},{5,4},{6,7},{7,6},{8,9},{9,8},{10,11... | collective-permute-start | bytes 626696 | tf_op jit(solution)/shard_map/ppermute | solution.py:723
  34.3 2.2 %collective-permute-start.7 = (bf16[272,384]{1,0:T(8,128)(2,1)S(1)}, bf16[272,384]{1,0:T(8,128)(2,1)S(1)}, u32[]{:S(2)}, u32[]{:S(2)}) collective-permute-start(bf16[272,384]{1,0:T(8,128)(2,1)S(1)} %collective-permute-done.1.refs_2_), channel_id=1, source_target_pairs={{0,1},{1,0},{2,3},{3,2},{4,5},{5,4},{6,7},{7,6},{8,9},{9,8},{10,11... | collective-permute-start | bytes 626696 | tf_op jit(solution)/shard_map/ppermute | solution.py:723
  34.7 1.8 %collective-permute-start.8 = (bf16[272,384]{1,0:T(8,128)(2,1)S(1)}, bf16[272,384]{1,0:T(8,128)(2,1)S(1)}, u32[]{:S(2)}, u32[]{:S(2)}) collective-permute-start(bf16[272,384]{1,0:T(8,128)(2,1)S(1)} %collective-permute-done.2.refs_3_), channel_id=1, source_target_pairs={{0,1},{1,0},{2,3},{3,2},{4,5},{5,4},{6,7},{7,6},{8,9},{9,8},{10,11... | collective-permute-start | bytes 626696 | tf_op jit(solution)/shard_map/ppermute | solution.py:723
  34.8 1.7 %collective-permute-start.14 = (bf16[272,256]{1,0:T(8,128)(2,1)S(1)}, bf16[272,256]{1,0:T(8,128)(2,1)S(1)}, u32[]{:S(2)}, u32[]{:S(2)}) collective-permute-start(bf16[272,256]{1,0:T(8,128)(2,1)S(1)} %collective-permute-done.10.refs_11_), channel_id=1, source_target_pairs={{0,1},{1,0},{2,3},{3,2},{4,5},{5,4},{6,7},{7,6},{8,9},{9,8},{10,11... | collective-permute-start | bytes 417800 | tf_op jit(solution)/shard_map/ppermute | solution.py:723
  45.6 13.2 %all-to-all-start = ((f32[4,256,128]{2,1,0:T(8,128)}), f32[4,256,128]{2,1,0:T(8,128)S(1)}, u32[]{:S(2)}, u32[]{:S(2)}) async-start(f32[4,256,128]{2,1,0:T(8,128)} %get-tuple-element.82), calls=%async_computation | async-start | bytes 1048576 | tf_op jit(solution)/shard_map/all_to_all | solution.py:735
  60.0 10.1 %all-to-all-start.1 = ((bf16[4,256,128]{2,1,0:T(8,128)(2,1)}), bf16[4,256,128]{2,1,0:T(8,128)(2,1)S(1)}, u32[]{:S(2)}, u32[]{:S(2)}) async-start(bf16[4,256,128]{2,1,0:T(8,128)(2,1)} %get-tuple-element.96), calls=%async_computation.1 | async-start | bytes 524288 | tf_op jit(solution)/shard_map/all_to_all | solution.py:735
  70.0 17.2 %collective-permute-start.19 = (bf16[128,1024]{1,0:T(8,128)(2,1)S(1)}, bf16[128,1024]{1,0:T(8,128)(2,1)S(1)}, u32[]{:S(2)}, u32[]{:S(2)}) collective-permute-start(bf16[128,1024]{1,0:T(8,128)(2,1)S(1)} %get-tuple-element.109), channel_id=1, source_target_pairs={{0,48},{16,0},{32,16},{48,32},{64,112},{80,64},{96,80},{112,96},{1... | collective-permute-start | bytes 786440 | tf_op jit(solution)/shard_map/ppermute | solution.py:731
  75.0 12.2 %collective-permute-start.18 = (bf16[128,1024]{1,0:T(8,128)(2,1)S(1)}, bf16[128,1024]{1,0:T(8,128)(2,1)S(1)}, u32[]{:S(2)}, u32[]{:S(2)}) collective-permute-start(bf16[128,1024]{1,0:T(8,128)(2,1)S(1)} %get-tuple-element.108), channel_id=1, source_target_pairs={{0,32},{16,48},{32,0},{48,16},{64,96},{80,112},{96,64},{112,80},{1... | collective-permute-start | bytes 786440 | tf_op jit(solution)/shard_map/ppermute | solution.py:731
  75.0 13.7 %collective-permute-start.17 = (bf16[128,1024]{1,0:T(8,128)(2,1)S(1)}, bf16[128,1024]{1,0:T(8,128)(2,1)S(1)}, u32[]{:S(2)}, u32[]{:S(2)}) collective-permute-start(bf16[128,1024]{1,0:T(8,128)(2,1)S(1)} %get-tuple-element.107), channel_id=1, source_target_pairs={{0,16},{16,32},{32,48},{48,0},{64,80},{80,96},{96,112},{112,64},{1... | collective-permute-start | bytes 786440 | tf_op jit(solution)/shard_map/ppermute | solution.py:731
  86.6 3.7 %collective-permute-start.15 = (bf16[4,256,256]{2,1,0:T(8,128)(2,1)S(1)}, bf16[4,256,256]{2,1,0:T(8,128)(2,1)S(1)}, u32[]{:S(2)}, u32[]{:S(2)}) collective-permute-start(bf16[4,256,256]{2,1,0:T(8,128)(2,1)S(1)} %get-tuple-element.103), channel_id=1, source_target_pairs={{0,1},{1,0},{2,3},{3,2},{4,5},{5,4},{6,7},{7,6},{8,9},{9,8},{10,11... | collective-permute-start | bytes 1572872 | tf_op jit(solution)/shard_map/ppermute | solution.py:723
  86.7 3.6 %collective-permute-start.16 = (bf16[4,256,256]{2,1,0:T(8,128)(2,1)S(1)}, bf16[4,256,256]{2,1,0:T(8,128)(2,1)S(1)}, u32[]{:S(2)}, u32[]{:S(2)}) collective-permute-start(bf16[4,256,256]{2,1,0:T(8,128)(2,1)S(1)} %get-tuple-element.104), channel_id=1, source_target_pairs={{0,1},{1,0},{2,3},{3,2},{4,5},{5,4},{6,7},{7,6},{8,9},{9,8},{10,11... | collective-permute-start | bytes 1572872 | tf_op jit(solution)/shard_map/ppermute | solution.py:723
  88.9 1.4 %collective-permute-start.20 = (bf16[64,1024]{1,0:T(8,128)(2,1)S(1)}, bf16[64,1024]{1,0:T(8,128)(2,1)S(1)}, u32[]{:S(2)}, u32[]{:S(2)}) collective-permute-start(bf16[64,1024]{1,0:T(8,128)(2,1)S(1)} %slice.12), channel_id=1, source_target_pairs={{0,1},{1,0},{2,3},{3,2},{4,5},{5,4},{6,7},{7,6},{8,9},{9,8},{10,11... | collective-permute-start | bytes 393224 | tf_op jit(solution)/shard_map/ppermute | solution.py:723
  89.0 1.3 %collective-permute-start.21 = (f32[16,128]{1,0:T(8,128)S(1)}, f32[16,128]{1,0:T(8,128)S(1)}, u32[]{:S(2)}, u32[]{:S(2)}) collective-permute-start(f32[16,128]{1,0:T(8,128)S(1)} %get-tuple-element.110.rab), channel_id=1, source_target_pairs={{0,1},{1,0},{2,3},{3,2},{4,5},{5,4},{6,7},{7,6},{8,9},{9,8},{10,11... | collective-permute-start | bytes 24584 | tf_op jit(solution)/shard_map/ppermute | solution.py:723
  90.7 8.4 %collective-permute-start.25 = (bf16[304,256]{1,0:T(8,128)(2,1)S(1)}, bf16[304,256]{1,0:T(8,128)(2,1)S(1)}, u32[]{:S(2)}, u32[]{:S(2)}) collective-permute-start(bf16[304,256]{1,0:T(8,128)(2,1)S(1)} %get-tuple-element.128), channel_id=1, source_target_pairs={{0,8},{1,9},{2,10},{3,11},{4,12},{5,13},{6,14},{7,15},{8,0},{9,1},... | collective-permute-start | bytes 466952 | tf_op jit(solution)/shard_map/ppermute | solution.py:723
  90.8 11.8 %collective-permute-start.26 = (bf16[304,256]{1,0:T(8,128)(2,1)S(1)}, bf16[304,256]{1,0:T(8,128)(2,1)S(1)}, u32[]{:S(2)}, u32[]{:S(2)}) collective-permute-start(bf16[304,256]{1,0:T(8,128)(2,1)S(1)} %get-tuple-element.129), channel_id=1, source_target_pairs={{0,10},{1,11},{2,12},{3,13},{4,14},{5,15},{6,8},{7,9},{8,2},{9,3},... | collective-permute-start | bytes 466952 | tf_op jit(solution)/shard_map/ppermute | solution.py:723
  94.3 16.0 %collective-permute-start.22 = (bf16[432,256]{1,0:T(8,128)(2,1)S(1)}, bf16[432,256]{1,0:T(8,128)(2,1)S(1)}, u32[]{:S(2)}, u32[]{:S(2)}) collective-permute-start(bf16[432,256]{1,0:T(8,128)(2,1)S(1)} %get-tuple-element.125), channel_id=1, source_target_pairs={{0,2},{1,3},{2,4},{3,5},{4,6},{5,7},{6,0},{7,1},{8,10},{9,11},{10,... | collective-permute-start | bytes 663560 | tf_op jit(solution)/shard_map/ppermute | solution.py:723
  94.6 20.1 %collective-permute-start.23 = (bf16[432,256]{1,0:T(8,128)(2,1)S(1)}, bf16[432,256]{1,0:T(8,128)(2,1)S(1)}, u32[]{:S(2)}, u32[]{:S(2)}) collective-permute-start(bf16[432,256]{1,0:T(8,128)(2,1)S(1)} %get-tuple-element.126), channel_id=1, source_target_pairs={{0,4},{1,5},{2,6},{3,7},{4,0},{5,1},{6,2},{7,3},{8,12},{9,13},{10,... | collective-permute-start | bytes 663560 | tf_op jit(solution)/shard_map/ppermute | solution.py:723
  98.4 16.2 %collective-permute-start.24 = (bf16[432,256]{1,0:T(8,128)(2,1)S(1)}, bf16[432,256]{1,0:T(8,128)(2,1)S(1)}, u32[]{:S(2)}, u32[]{:S(2)}) collective-permute-start(bf16[432,256]{1,0:T(8,128)(2,1)S(1)} %get-tuple-element.127), channel_id=1, source_target_pairs={{0,6},{1,7},{2,0},{3,1},{4,2},{5,3},{6,4},{7,5},{8,14},{9,15},{10,... | collective-permute-start | bytes 663560 | tf_op jit(solution)/shard_map/ppermute | solution.py:723
  99.1 9.5 %collective-permute-start.27 = (bf16[304,256]{1,0:T(8,128)(2,1)S(1)}, bf16[304,256]{1,0:T(8,128)(2,1)S(1)}, u32[]{:S(2)}, u32[]{:S(2)}) collective-permute-start(bf16[304,256]{1,0:T(8,128)(2,1)S(1)} %get-tuple-element.130), channel_id=1, source_target_pairs={{0,12},{1,13},{2,14},{3,15},{4,8},{5,9},{6,10},{7,11},{8,4},{9,5},... | collective-permute-start | bytes 466952 | tf_op jit(solution)/shard_map/ppermute | solution.py:723
  102.5 7.7 %collective-permute-start.28 = (bf16[304,256]{1,0:T(8,128)(2,1)S(1)}, bf16[304,256]{1,0:T(8,128)(2,1)S(1)}, u32[]{:S(2)}, u32[]{:S(2)}) collective-permute-start(bf16[304,256]{1,0:T(8,128)(2,1)S(1)} %get-tuple-element.131), channel_id=1, source_target_pairs={{0,14},{1,15},{2,8},{3,9},{4,10},{5,11},{6,12},{7,13},{8,6},{9,7},... | collective-permute-start | bytes 466952 | tf_op jit(solution)/shard_map/ppermute | solution.py:723
  116.1 12.5 %all-to-all-start.2 = ((f32[8,8,1024]{2,1,0:T(8,128)}), f32[8,8,1024]{2,1,0:T(8,128)S(1)}, u32[]{:S(2)}, u32[]{:S(2)}) async-start(f32[8,8,1024]{2,1,0:T(8,128)} %collect.1), calls=%async_computation.2 | async-start | bytes 524288 | tf_op jit(solution)/shard_map/all_to_all | solution.py:779
  (3 other events, 48.1 us)

commit v5 on v4

--- a/solution.py
+++ b/solution.py
@@ -21,7 +21,7 @@
 SCALE = 1.0 / math.sqrt(128.0)
 LIST = 160
 FAR_U = 8
-NEAR_U = 4
+NEAR_U = 8
 NEAR_FLAG = 32768
 DUMMY = QT + 16 * TILES
 VM_ATTEND = 20
@@ -60,6 +60,26 @@
 
 def in_hbm(part):
     return pltpu.with_memory_space_constraint(part, pltpu.HBM)
+
+
+def pack_kernel(tokens, moments, out):
+    out[0:256, :] = tokens[...]
+    time = moments[...].reshape(1, 256)
+    rows = jnp.concatenate([time // T, time % T, jnp.zeros((14, 256), i32)], axis=0)
+    out[256:, 0:256] = rows.astype(f32).astype(bf16)
+    out[256:, 256:] = jnp.zeros((16, 768), bf16)
+
+
+def pack(tokens, moments):
+    return pl.pallas_call(
+        pack_kernel,
+        in_specs=[VMEM] * 2,
+        out_specs=VMEM,
+        out_shape=sds((272, 1024), bf16),
+        compiler_params=params(8),
+        cost_estimate=cost(1 << 16, 1 << 20),
+        name="pack",
+    )(in_hbm(tokens), in_hbm(moments))
 
 
 def project_kernel(own, tokens, *refs):
@@ -738,10 +758,15 @@
 def on_device(tokens, cotangent, in_proj, out_proj, rab_time, seq_lengths, block_mask, time_bucket):
     ctx = lax.axis_index("ctx")
     y, z, core = ctx // 8, (ctx // 2) % 4, ctx % 2
-    times = jnp.stack([time_bucket // T, time_bucket % T]).astype(bf16)
-    near_tokens = jnp.concatenate([tokens, jnp.pad(times, ((0, 14), (0, 768)))], axis=0)
+    near_tokens = pack(tokens, time_bucket)
     far_tokens = send(near_tokens, 1, 0, 0)
+    ids = jnp.stack([y, z, core, lax.axis_index("dp")]).astype(i32)
+    lengths = seq_lengths.reshape(3)
+    limits = [2.0**j - 1.0 for j in range(BUCKETS)] + [1e9] * 4
+    head_bias = lax.dynamic_slice_in_dim(rab_time, z, 1, 1).reshape(BUCKETS) * 0.5
+    table = jnp.concatenate([head_bias, jnp.zeros((4,), f32), jnp.array(limits, f32)])
     full = project(near_tokens, in_proj, block_mask)
+    full, ids, table = lax.optimization_barrier((full, ids, table))
     own = [full[0]] + [send(full[s], 0, s, 0) for s in (1, 2, 3)]
     pairs = project(far_tokens, in_proj)
     across = [pairs[0]] + [send(pairs[s], 0, s, 0) for s in (1, 2, 3)]
@@ -751,11 +776,6 @@
     across_twin = [send(part, 0, 0, 1) for part in across]
     parts = own + own_twin + across + across_twin
 
-    ids = jnp.stack([y, z, core, lax.axis_index("dp")]).astype(i32)
-    lengths = seq_lengths.reshape(3)
-    limits = [2.0**j - 1.0 for j in range(BUCKETS)] + [1e9] * 4
-    head_bias = lax.dynamic_slice_in_dim(rab_time, z, 1, 1).reshape(BUCKETS) * 0.5
-    table = jnp.concatenate([head_bias, jnp.zeros((4,), f32), jnp.array(limits, f32)])
     heads, *saved = attend(ids, table, lengths, parts)
 
     mixed, grad_gate, grads = middle(swap_z(heads), gate, slope, grad_mix)

time: 129 us -> 128 us (level)
  waiting for transfers between devices: 31.5 us -> 33.8 us
  other arithmetic: 2.77 us -> 0.99 us
    all_to_all x2, waiting for transfers between devices: 7.9 us -> 9.3 us  [swap_z(): lax.all_to_all(part, 'ctx', 0, 0, axis_index_groups=OVER_Z, tiled=True)]
  transfers between devices with their start and end apart: 32 -> 32, of which waited for: 13 -> 15; matrix products, arithmetic and copies ran while one was open for 1% -> 1% of each run, Pallas kernels for 26% -> 25%
where the time goes in v5:
time: 128 us
  starting transfers between devices  47.4 us (37%)
  Pallas kernels  45.1 us (35%)
  waiting for transfers between devices  33.8 us (26%)
    ppermute x26, starting transfers between devices, send(): return lax.ppermute(x, 'ctx', move(y_xor, z_shift, core_xor))  29 us
    ppermute x26, waiting for transfers between devices, send(): return lax.ppermute(x, 'ctx', move(y_xor, z_shift, core_xor))  21.8 us
    pallas_call x1, Pallas kernels, attend_back(): pl.pallas_call(backward_kernel, in_specs=[SMEM] * 6 + [VMEM] * 5, out_spe...  9.5 us
    all_to_all x2, waiting for transfers between devices, swap_z(): lax.all_to_all(part, 'ctx', 0, 0, axis_index_groups=OVER_Z, tiled=True)  9.3 us
    pallas_call x1, Pallas kernels, attend(): pl.pallas_call(forward_kernel, in_specs=[SMEM] * 3 + [VMEM] * 16, out_spe...  8.14 us
    pallas_call x2, Pallas kernels, project(): pl.pallas_call(functools.partial(project_kernel, int(own)), grid=(HEADS,)...  7.71 us
    all_to_all x2, starting transfers between devices, swap_z(): lax.all_to_all(part, 'ctx', 0, 0, axis_index_groups=OVER_Z, tiled=True)  6.89 us
    all_to_all x1, starting transfers between devices, on_device(): lines = lax.all_to_all(collect(ids, same, other), 'dp', 0, 0, tiled=True)  6.56 us
  transfers between devices with their start and end apart: 32, of which 15 were waited for; matrix products, arithmetic and copies ran while one was open for 1% of the time, Pallas kernels for 25%

profile of v5, /device:TPU:24, one launch (start us, length us, event | category | flops | bytes accessed | tf_op | source)
XLA Modules:
  0.0 128.2 jit_solution(3867530485170224951)
XLA Ops:
  1.7 1.3 %collective-permute-start.3 = (bf16[272,1024]{1,0:T(8,128)(2,1)S(1)}, bf16[272,1024]{1,0:T(8,128)(2,1)S(1)}, u32[]{:S(2)}, u32[]{:S(2)}) collective-permute-start(bf16[272,1024]{1,0:T(8,128)(2,1)S(1)} %pack.1.tokens), channel_id=1, source_target_pairs={{0,8},{1,9},{2,10},{3,11},{4,12},{5,13},{6,14},{7,15},{8,0},{9,1},... | collective-permute-start | bytes 1671176 | tf_op jit(solution)/shard_map/ppermute | solution.py:743
  3.0 4.2 %project_own.1 = (bf16[272,384]{1,0:T(8,128)(2,1)S(1)}, bf16[272,384]{1,0:T(8,128)(2,1)S(1)}, bf16[272,384]{1,0:T(8,128)(2,1)S(1)}, bf16[272,384]{1,0:T(8,128)(2,1)S(1)}) custom-call(bf16[272,1024]{1,0:T(8,128)(2,1)S(1)} %pack.1.tokens, s32[1,2,32]{2,1,0:T(2,128)} %refs_0_.2, bf16[1024,2048]{1,0:T(8,128)(2,1)} %in_proj.3, bf16[1024,2048]{1,0:T(8,128)(2,1)} %in_proj.3, ...), custom_call_target="tpu_custom_call" | custom-call | flops 805306368 | bytes 5242880 | tf_op jit(solution)/shard_map/project_own/pallas_call | solution.py:122
  8.1 1.9 %collective-permute-start = (bf16[272,384]{1,0:T(8,128)(2,1)S(1)}, bf16[272,384]{1,0:T(8,128)(2,1)S(1)}, u32[]{:S(2)}, u32[]{:S(2)}) collective-permute-start(bf16[272,384]{1,0:T(8,128)(2,1)S(1)} %get-tuple-element.82), channel_id=1, source_target_pairs={{0,2},{1,3},{2,4},{3,5},{4,6},{5,7},{6,0},{7,1},{8,10},{9,11},{10,... | collective-permute-start | bytes 626696 | tf_op jit(solution)/shard_map/ppermute | solution.py:743
  10.0 3.6 %collective-permute-start.1 = (bf16[272,384]{1,0:T(8,128)(2,1)S(1)}, bf16[272,384]{1,0:T(8,128)(2,1)S(1)}, u32[]{:S(2)}, u32[]{:S(2)}) collective-permute-start(bf16[272,384]{1,0:T(8,128)(2,1)S(1)} %get-tuple-element.83), channel_id=1, source_target_pairs={{0,4},{1,5},{2,6},{3,7},{4,0},{5,1},{6,2},{7,3},{8,12},{9,13},{10,... | collective-permute-start | bytes 626696 | tf_op jit(solution)/shard_map/ppermute | solution.py:743
  14.6 3.1 %collective-permute-done.3.tokens = bf16[272,1024]{1,0:T(8,128)(2,1)S(1)} collective-permute-done((bf16[272,1024]{1,0:T(8,128)(2,1)S(1)}, bf16[272,1024]{1,0:T(8,128)(2,1)S(1)}, u32[]{:S(2)}, u32[]{:S(2)}) %collective-permute-start.3) | collective-permute-done | bytes 557088 | tf_op jit(solution)/shard_map/ppermute | solution.py:743
  17.7 3.5 %project_other.1 = (bf16[272,256]{1,0:T(8,128)(2,1)S(1)}, bf16[272,256]{1,0:T(8,128)(2,1)S(1)}, bf16[272,256]{1,0:T(8,128)(2,1)S(1)}, bf16[272,256]{1,0:T(8,128)(2,1)S(1)}) custom-call(bf16[272,1024]{1,0:T(8,128)(2,1)S(1)} %collective-permute-done.3.tokens, bf16[1024,2048]{1,0:T(8,128)(2,1)} %in_proj.3, bf16[1024,2048]{1,0:T(8,128)(2,1)} %in_proj.3), custom_call_target="tpu_custom_call" | custom-call | flops 536870912 | bytes 5242880 | tf_op jit(solution)/shard_map/project_other/pallas_call | solution.py:122
  21.2 2.0 %collective-permute-start.4 = (bf16[272,256]{1,0:T(8,128)(2,1)S(1)}, bf16[272,256]{1,0:T(8,128)(2,1)S(1)}, u32[]{:S(2)}, u32[]{:S(2)}) collective-permute-start(bf16[272,256]{1,0:T(8,128)(2,1)S(1)} %get-tuple-element.85), channel_id=1, source_target_pairs={{0,2},{1,3},{2,4},{3,5},{4,6},{5,7},{6,0},{7,1},{8,10},{9,11},{10,... | collective-permute-start | bytes 417800 | tf_op jit(solution)/shard_map/ppermute | solution.py:743
  23.2 3.6 %collective-permute-start.9 = (bf16[272,256]{1,0:T(8,128)(2,1)S(1)}, bf16[272,256]{1,0:T(8,128)(2,1)S(1)}, u32[]{:S(2)}, u32[]{:S(2)}) collective-permute-start(bf16[272,256]{1,0:T(8,128)(2,1)S(1)} %get-tuple-element.92), channel_id=1, source_target_pairs={{0,4},{1,5},{2,6},{3,7},{4,0},{5,1},{6,2},{7,3},{8,12},{9,13},{10,... | collective-permute-start | bytes 417800 | tf_op jit(solution)/shard_map/ppermute | solution.py:743
  27.8 1.7 %collective-permute-done.4.refs_9_ = bf16[272,256]{1,0:T(8,128)(2,1)S(1)} collective-permute-done((bf16[272,256]{1,0:T(8,128)(2,1)S(1)}, bf16[272,256]{1,0:T(8,128)(2,1)S(1)}, u32[]{:S(2)}, u32[]{:S(2)}) %collective-permute-start.4) | collective-permute-done | bytes 139296 | tf_op jit(solution)/shard_map/ppermute | solution.py:743
  29.5 2.8 %collective-permute-done.9.refs_10_ = bf16[272,256]{1,0:T(8,128)(2,1)S(1)} collective-permute-done((bf16[272,256]{1,0:T(8,128)(2,1)S(1)}, bf16[272,256]{1,0:T(8,128)(2,1)S(1)}, u32[]{:S(2)}, u32[]{:S(2)}) %collective-permute-start.9) | collective-permute-done | bytes 139296 | tf_op jit(solution)/shard_map/ppermute | solution.py:743
  33.8 1.2 collective-permute-done.14.refs_15_
  35.1 8.1 %attend.1 = (f32[4,256,128]{2,1,0:T(8,128)}, s32[160]{0:T(256)S(1)}, s32[160]{0:T(256)S(1)}, s32[8]{0:T(128)S(1)}, bf16[33,128,128]{2,1,0:T(8,128)(2,1)}, /*inde...) custom-call(s32[4]{0:T(128)S(1)} %pad_add_fusion.ids, f32[32]{0:T(128)S(1)} %pad_maximum_fusion.table, ...), custom_call_target="tpu_custom_call" | custom-call | flops 6000000000 | bytes 6291456 | tf_op jit(solution)/shard_map/attend/pallas_call | solution.py:361
  43.2 3.5 %all-to-all-start = ((f32[4,256,128]{2,1,0:T(8,128)}), f32[4,256,128]{2,1,0:T(8,128)S(1)}, u32[]{:S(2)}, u32[]{:S(2)}) async-start(f32[4,256,128]{2,1,0:T(8,128)} %get-tuple-element.94), calls=%async_computation | async-start | bytes 1048576 | tf_op jit(solution)/shard_map/all_to_all | solution.py:755
  46.7 5.5 %gates.1 = (bf16[256,512]{1,0:T(8,128)(2,1)S(1)}, bf16[256,2048]{1,0:T(8,128)(2,1)S(1)}, f32[256,512]{1,0:T(8,128)S(1)}) custom-call(bf16[256,1024]{1,0:T(8,128)(2,1)} %tokens.7, bf16[1024,2048]{1,0:T(8,128)(2,1)} %in_proj.3, bf16[256,1024]{1,0:T(8,128)(2,1)} %cot.4, bf16[512,1024]{1,0:T(8,128)(2,1)} %out_proj.3), custom_call_target="tpu_custom_call" | custom-call | flops 1073741824 | bytes 7340032 | tf_op jit(solution)/shard_map/gates/pallas_call | solution.py:154
  52.3 5.1 %all-to-all-done.heads = f32[4,256,128]{2,1,0:T(8,128)S(1)} async-done(((f32[4,256,128]{2,1,0:T(8,128)}), f32[4,256,128]{2,1,0:T(8,128)S(1)}, u32[]{:S(2)}, u32[]{:S(2)}) %all-to-all-start) | async-done | bytes 524320 | tf_op jit(solution)/shard_map/all_to_all | solution.py:755
  58.6 3.4 %all-to-all-start.1 = ((bf16[4,256,128]{2,1,0:T(8,128)(2,1)}), bf16[4,256,128]{2,1,0:T(8,128)(2,1)S(1)}, u32[]{:S(2)}, u32[]{:S(2)}) async-start(bf16[4,256,128]{2,1,0:T(8,128)(2,1)} %get-tuple-element.108), calls=%async_computation.1 | async-start | bytes 524288 | tf_op jit(solution)/shard_map/all_to_all | solution.py:755
  62.0 2.9 %finish_output.1 = (bf16[256,1024]{1,0:T(8,128)(2,1)}, f32[128,1024]{1,0:T(8,128)S(1)}, bf16[128,1024]{1,0:T(8,128)(2,1)S(1)}, bf16[128,1024]{1,0:T(8,128)(2,1)S(1)}, bf16[128,1024]{1,0:T(8,128)(2,1)S(1)}) custom-call(s32[4]{0:T(128)S(1)} %pad_add_fusion.ids, bf16[256,1024]{1,0:T(8,128)(2,1)} %tokens.7, bf16[256,1024]{1,0:T(8,128)(2,1)} %cot.4, ...), custom_call_target="tpu_custom_call" | custom-call | flops 805306368 | bytes 5242880 | tf_op jit(solution)/shard_map/finish_output/pallas_call | solution.py:435
  64.9 4.2 %all-to-all-done.1.refs_4_ = bf16[4,256,128]{2,1,0:T(8,128)(2,1)S(1)} async-done(((bf16[4,256,128]{2,1,0:T(8,128)(2,1)}), bf16[4,256,128]{2,1,0:T(8,128)(2,1)S(1)}, u32[]{:S(2)}, u32[]{:S(2)}) %all-to-all-start.1) | async-done | bytes 262176 | tf_op jit(solution)/shard_map/all_to_all | solution.py:755
  69.1 4.1 %collective-permute-start.19 = (bf16[128,1024]{1,0:T(8,128)(2,1)S(1)}, bf16[128,1024]{1,0:T(8,128)(2,1)S(1)}, u32[]{:S(2)}, u32[]{:S(2)}) collective-permute-start(bf16[128,1024]{1,0:T(8,128)(2,1)S(1)} %get-tuple-element.121), channel_id=1, source_target_pairs={{0,48},{16,0},{32,16},{48,32},{64,112},{80,64},{96,80},{112,96},{1... | collective-permute-start | bytes 786440 | tf_op jit(solution)/shard_map/ppermute | solution.py:751
  74.0 9.5 %attend_back.1 = (bf16[4,256,256]{2,1,0:T(8,128)(2,1)S(1)}, bf16[4,256,256]{2,1,0:T(8,128)(2,1)S(1)}, bf16[4,256,256]{2,1,0:T(8,128)(2,1)S(1)}, bf16[4,256,256]{...) custom-call(s32[4]{0:T(128)S(1)} %pad_add_fusion.ids, f32[32]{0:T(128)S(1)} %pad_maximum_fusion.table, ...), custom_call_target="tpu_custom_call" | custom-call | flops 12000000000 | bytes 8388608 | tf_op jit(solution)/shard_map/attend_back/pallas_call | solution.py:554
  84.1 2.7 %collective-permute-done.17 = bf16[128,1024]{1,0:T(8,128)(2,1)S(1)} collective-permute-done((bf16[128,1024]{1,0:T(8,128)(2,1)S(1)}, bf16[128,1024]{1,0:T(8,128)(2,1)S(1)}, u32[]{:S(2)}, u32[]{:S(2)}) %collective-permute-start.17) | collective-permute-done | bytes 262176 | tf_op jit(solution)/shard_map/ppermute | solution.py:751
  88.8 3.5 %collective-permute-start.26 = (bf16[304,256]{1,0:T(8,128)(2,1)S(1)}, bf16[304,256]{1,0:T(8,128)(2,1)S(1)}, u32[]{:S(2)}, u32[]{:S(2)}) collective-permute-start(bf16[304,256]{1,0:T(8,128)(2,1)S(1)} %get-tuple-element.141), channel_id=1, source_target_pairs={{0,10},{1,11},{2,12},{3,13},{4,14},{5,15},{6,8},{7,9},{8,2},{9,3},... | collective-permute-start | bytes 466952 | tf_op jit(solution)/shard_map/ppermute | solution.py:743
  92.4 4.1 %collective-permute-start.23 = (bf16[432,256]{1,0:T(8,128)(2,1)S(1)}, bf16[432,256]{1,0:T(8,128)(2,1)S(1)}, u32[]{:S(2)}, u32[]{:S(2)}) collective-permute-start(bf16[432,256]{1,0:T(8,128)(2,1)S(1)} %get-tuple-element.138), channel_id=1, source_target_pairs={{0,4},{1,5},{2,6},{3,7},{4,0},{5,1},{6,2},{7,3},{8,12},{9,13},{10,... | collective-permute-start | bytes 663560 | tf_op jit(solution)/shard_map/ppermute | solution.py:743
  98.1 2.6 %collective-permute-done.26.refs_5_.refs_13_ = bf16[304,256]{1,0:T(8,128)(2,1)S(1)} collective-permute-done((bf16[304,256]{1,0:T(8,128)(2,1)S(1)}, bf16[304,256]{1,0:T(8,128)(2,1)S(1)}, u32[]{:S(2)}, u32[]{:S(2)}) %collective-permute-start.26) | collective-permute-done | bytes 155680 | tf_op jit(solution)/shard_map/ppermute | solution.py:743
  100.6 3.0 %collective-permute-start.28 = (bf16[304,256]{1,0:T(8,128)(2,1)S(1)}, bf16[304,256]{1,0:T(8,128)(2,1)S(1)}, u32[]{:S(2)}, u32[]{:S(2)}) collective-permute-start(bf16[304,256]{1,0:T(8,128)(2,1)S(1)} %get-tuple-element.143), channel_id=1, source_target_pairs={{0,14},{1,15},{2,8},{3,9},{4,10},{5,11},{6,12},{7,13},{8,6},{9,7},... | collective-permute-start | bytes 466952 | tf_op jit(solution)/shard_map/ppermute | solution.py:743
  103.6 3.0 %collective-permute-done.27.refs_6_.refs_14_ = bf16[304,256]{1,0:T(8,128)(2,1)S(1)} collective-permute-done((bf16[304,256]{1,0:T(8,128)(2,1)S(1)}, bf16[304,256]{1,0:T(8,128)(2,1)S(1)}, u32[]{:S(2)}, u32[]{:S(2)}) %collective-permute-start.27) | collective-permute-done | bytes 155680 | tf_op jit(solution)/shard_map/ppermute | solution.py:743
  106.6 1.7 %collective-permute-done.28.refs_7_.refs_15_ = bf16[304,256]{1,0:T(8,128)(2,1)S(1)} collective-permute-done((bf16[304,256]{1,0:T(8,128)(2,1)S(1)}, bf16[304,256]{1,0:T(8,128)(2,1)S(1)}, u32[]{:S(2)}, u32[]{:S(2)}) %collective-permute-start.28) | collective-permute-done | bytes 155680 | tf_op jit(solution)/shard_map/ppermute | solution.py:743
  108.4 4.2 %collective-permute-done.23.refs_2_.refs_10_ = bf16[432,256]{1,0:T(8,128)(2,1)S(1)} collective-permute-done((bf16[432,256]{1,0:T(8,128)(2,1)S(1)}, bf16[432,256]{1,0:T(8,128)(2,1)S(1)}, u32[]{:S(2)}, u32[]{:S(2)}) %collective-permute-start.23) | collective-permute-done | bytes 221216 | tf_op jit(solution)/shard_map/ppermute | solution.py:743
  112.8 1.4 %collect.1 = f32[8,8,1024]{2,1,0:T(8,128)} custom-call(s32[4]{0:T(128)S(1)} %pad_add_fusion.ids, bf16[432,256]{1,0:T(8,128)(2,1)S(1)} %get-tuple-element.136.refs_0_.refs_8_, bf16[432,256]{1,0:T(8,128)(2,1)S(1)} %collective-permute-done.22.refs_1_.refs_9_, bf16[432,256]{1,0:T(8,128)(2,1)S(1)} %collective-permute-done.23.refs_2_.refs_10_, ...), custom_call_target="tpu_custom_call" | custom-call | flops 65536 | bytes 262144 | tf_op jit(solution)/shard_map/collect/pallas_call | solution.py:629
  114.2 6.6 %all-to-all-start.2 = ((f32[8,8,1024]{2,1,0:T(8,128)}), f32[8,8,1024]{2,1,0:T(8,128)S(1)}, u32[]{:S(2)}, u32[]{:S(2)}) async-start(f32[8,8,1024]{2,1,0:T(8,128)} %collect.1), calls=%async_computation.2 | async-start | bytes 524288 | tf_op jit(solution)/shard_map/all_to_all | solution.py:799
  120.8 3.4 %ready.1 = (f32[256,1024]{1,0:T(8,128)S(1)}, f32[256,128]{1,0:T(8,128)S(1)}, bf16[256,1024]{1,0:T(8,128)(2,1)S(1)}, bf16[1024,2048]{1,0:T(8,128)(2,1)S(1)}) custom-call(bf16[256,1024]{1,0:T(8,128)(2,1)} %tokens.7, bf16[256,1024]{1,0:T(8,128)(2,1)} %cot.4, bf16[1024,2048]{1,0:T(8,128)(2,1)} %in_proj.3), custom_call_target="tpu_custom_call" | custom-call | flops 4194304 | bytes 6291456 | tf_op jit(solution)/shard_map/ready/pallas_call | solution.py:681
  124.2 3.4 %finish_grad.1 = bf16[256,1024]{1,0:T(8,128)(2,1)} custom-call(s32[4]{0:T(128)S(1)} %pad_add_fusion.ids, bf16[256,512]{1,0:T(8,128)(2,1)S(1)} %copy-done, bf16[256,2048]{1,0:T(8,128)(2,1)S(1)} %get-tuple-element.96.slope, f32[256,1024]{1,0:T(8,128)S(1)} %get-tuple-element.132.normed, f32[256,128]{1,0:T(8,128)S(1)} %get-tuple-element.133.inverse, ...), custom_call_target="tpu_custom_call" | custom-call | flops 1073741824 | bytes 8388608 | tf_op jit(solution)/shard_map/finish_grad/pallas_call | solution.py:721
  (58 shorter events, 12.6 us)
Async XLA Ops:
  1.7 15.9 %collective-permute-start.3 = (bf16[272,1024]{1,0:T(8,128)(2,1)S(1)}, bf16[272,1024]{1,0:T(8,128)(2,1)S(1)}, u32[]{:S(2)}, u32[]{:S(2)}) collective-permute-start(bf16[272,1024]{1,0:T(8,128)(2,1)S(1)} %pack.1.tokens), channel_id=1, source_target_pairs={{0,8},{1,9},{2,10},{3,11},{4,12},{5,13},{6,14},{7,15},{8,0},{9,1},... | collective-permute-start | bytes 1671176 | tf_op jit(solution)/shard_map/ppermute | solution.py:743
  8.1 18.7 %collective-permute-start = (bf16[272,384]{1,0:T(8,128)(2,1)S(1)}, bf16[272,384]{1,0:T(8,128)(2,1)S(1)}, u32[]{:S(2)}, u32[]{:S(2)}) collective-permute-start(bf16[272,384]{1,0:T(8,128)(2,1)S(1)} %get-tuple-element.82), channel_id=1, source_target_pairs={{0,2},{1,3},{2,4},{3,5},{4,6},{5,7},{6,0},{7,1},{8,10},{9,11},{10,... | collective-permute-start | bytes 626696 | tf_op jit(solution)/shard_map/ppermute | solution.py:743
  10.0 17.8 %collective-permute-start.1 = (bf16[272,384]{1,0:T(8,128)(2,1)S(1)}, bf16[272,384]{1,0:T(8,128)(2,1)S(1)}, u32[]{:S(2)}, u32[]{:S(2)}) collective-permute-start(bf16[272,384]{1,0:T(8,128)(2,1)S(1)} %get-tuple-element.83), channel_id=1, source_target_pairs={{0,4},{1,5},{2,6},{3,7},{4,0},{5,1},{6,2},{7,3},{8,12},{9,13},{10,... | collective-permute-start | bytes 626696 | tf_op jit(solution)/shard_map/ppermute | solution.py:743
  13.6 14.2 %collective-permute-start.2 = (bf16[272,384]{1,0:T(8,128)(2,1)S(1)}, bf16[272,384]{1,0:T(8,128)(2,1)S(1)}, u32[]{:S(2)}, u32[]{:S(2)}) collective-permute-start(bf16[272,384]{1,0:T(8,128)(2,1)S(1)} %get-tuple-element.84), channel_id=1, source_target_pairs={{0,6},{1,7},{2,0},{3,1},{4,2},{5,3},{6,4},{7,5},{8,14},{9,15},{10,... | collective-permute-start | bytes 626696 | tf_op jit(solution)/shard_map/ppermute | solution.py:743
  21.2 8.3 %collective-permute-start.4 = (bf16[272,256]{1,0:T(8,128)(2,1)S(1)}, bf16[272,256]{1,0:T(8,128)(2,1)S(1)}, u32[]{:S(2)}, u32[]{:S(2)}) collective-permute-start(bf16[272,256]{1,0:T(8,128)(2,1)S(1)} %get-tuple-element.85), channel_id=1, source_target_pairs={{0,2},{1,3},{2,4},{3,5},{4,6},{5,7},{6,0},{7,1},{8,10},{9,11},{10,... | collective-permute-start | bytes 417800 | tf_op jit(solution)/shard_map/ppermute | solution.py:743
  23.2 9.1 %collective-permute-start.9 = (bf16[272,256]{1,0:T(8,128)(2,1)S(1)}, bf16[272,256]{1,0:T(8,128)(2,1)S(1)}, u32[]{:S(2)}, u32[]{:S(2)}) collective-permute-start(bf16[272,256]{1,0:T(8,128)(2,1)S(1)} %get-tuple-element.92), channel_id=1, source_target_pairs={{0,4},{1,5},{2,6},{3,7},{4,0},{5,1},{6,2},{7,3},{8,12},{9,13},{10,... | collective-permute-start | bytes 417800 | tf_op jit(solution)/shard_map/ppermute | solution.py:743
  26.8 6.0 %collective-permute-start.10 = (bf16[272,256]{1,0:T(8,128)(2,1)S(1)}, bf16[272,256]{1,0:T(8,128)(2,1)S(1)}, u32[]{:S(2)}, u32[]{:S(2)}) collective-permute-start(bf16[272,256]{1,0:T(8,128)(2,1)S(1)} %get-tuple-element.93), channel_id=1, source_target_pairs={{0,6},{1,7},{2,0},{3,1},{4,2},{5,3},{6,4},{7,5},{8,14},{9,15},{10,... | collective-permute-start | bytes 417800 | tf_op jit(solution)/shard_map/ppermute | solution.py:743
  27.8 5.0 %collective-permute-start.11 = (bf16[272,256]{1,0:T(8,128)(2,1)S(1)}, bf16[272,256]{1,0:T(8,128)(2,1)S(1)}, u32[]{:S(2)}, u32[]{:S(2)}) collective-permute-start(bf16[272,256]{1,0:T(8,128)(2,1)S(1)} %get-tuple-element.90.refs_8_), channel_id=1, source_target_pairs={{0,1},{1,0},{2,3},{3,2},{4,5},{5,4},{6,7},{7,6},{8,9},{9,8},{10,11... | collective-permute-start | bytes 417800 | tf_op jit(solution)/shard_map/ppermute | solution.py:743
  29.5 3.8 %collective-permute-start.12 = (bf16[272,256]{1,0:T(8,128)(2,1)S(1)}, bf16[272,256]{1,0:T(8,128)(2,1)S(1)}, u32[]{:S(2)}, u32[]{:S(2)}) collective-permute-start(bf16[272,256]{1,0:T(8,128)(2,1)S(1)} %collective-permute-done.4.refs_9_), channel_id=1, source_target_pairs={{0,1},{1,0},{2,3},{3,2},{4,5},{5,4},{6,7},{7,6},{8,9},{9,8},{10,11... | collective-permute-start | bytes 417800 | tf_op jit(solution)/shard_map/ppermute | solution.py:743
  32.3 1.4 %collective-permute-start.13 = (bf16[272,256]{1,0:T(8,128)(2,1)S(1)}, bf16[272,256]{1,0:T(8,128)(2,1)S(1)}, u32[]{:S(2)}, u32[]{:S(2)}) collective-permute-start(bf16[272,256]{1,0:T(8,128)(2,1)S(1)} %collective-permute-done.9.refs_10_), channel_id=1, source_target_pairs={{0,1},{1,0},{2,3},{3,2},{4,5},{5,4},{6,7},{7,6},{8,9},{9,8},{10,11... | collective-permute-start | bytes 417800 | tf_op jit(solution)/shard_map/ppermute | solution.py:743
  32.3 2.8 %collective-permute-start.5 = (bf16[272,384]{1,0:T(8,128)(2,1)S(1)}, bf16[272,384]{1,0:T(8,128)(2,1)S(1)}, u32[]{:S(2)}, u32[]{:S(2)}) collective-permute-start(bf16[272,384]{1,0:T(8,128)(2,1)S(1)} %get-tuple-element.86.refs_0_), channel_id=1, source_target_pairs={{0,1},{1,0},{2,3},{3,2},{4,5},{5,4},{6,7},{7,6},{8,9},{9,8},{10,11... | collective-permute-start | bytes 626696 | tf_op jit(solution)/shard_map/ppermute | solution.py:743
  32.8 2.3 %collective-permute-start.6 = (bf16[272,384]{1,0:T(8,128)(2,1)S(1)}, bf16[272,384]{1,0:T(8,128)(2,1)S(1)}, u32[]{:S(2)}, u32[]{:S(2)}) collective-permute-start(bf16[272,384]{1,0:T(8,128)(2,1)S(1)} %collective-permute-done.refs_1_), channel_id=1, source_target_pairs={{0,1},{1,0},{2,3},{3,2},{4,5},{5,4},{6,7},{7,6},{8,9},{9,8},{10,11... | collective-permute-start | bytes 626696 | tf_op jit(solution)/shard_map/ppermute | solution.py:743
  32.8 2.3 %collective-permute-start.7 = (bf16[272,384]{1,0:T(8,128)(2,1)S(1)}, bf16[272,384]{1,0:T(8,128)(2,1)S(1)}, u32[]{:S(2)}, u32[]{:S(2)}) collective-permute-start(bf16[272,384]{1,0:T(8,128)(2,1)S(1)} %collective-permute-done.1.refs_2_), channel_id=1, source_target_pairs={{0,1},{1,0},{2,3},{3,2},{4,5},{5,4},{6,7},{7,6},{8,9},{9,8},{10,11... | collective-permute-start | bytes 626696 | tf_op jit(solution)/shard_map/ppermute | solution.py:743
  33.3 1.8 %collective-permute-start.8 = (bf16[272,384]{1,0:T(8,128)(2,1)S(1)}, bf16[272,384]{1,0:T(8,128)(2,1)S(1)}, u32[]{:S(2)}, u32[]{:S(2)}) collective-permute-start(bf16[272,384]{1,0:T(8,128)(2,1)S(1)} %collective-permute-done.2.refs_3_), channel_id=1, source_target_pairs={{0,1},{1,0},{2,3},{3,2},{4,5},{5,4},{6,7},{7,6},{8,9},{9,8},{10,11... | collective-permute-start | bytes 626696 | tf_op jit(solution)/shard_map/ppermute | solution.py:743
  33.6 1.4 %collective-permute-start.14 = (bf16[272,256]{1,0:T(8,128)(2,1)S(1)}, bf16[272,256]{1,0:T(8,128)(2,1)S(1)}, u32[]{:S(2)}, u32[]{:S(2)}) collective-permute-start(bf16[272,256]{1,0:T(8,128)(2,1)S(1)} %collective-permute-done.10.refs_11_), channel_id=1, source_target_pairs={{0,1},{1,0},{2,3},{3,2},{4,5},{5,4},{6,7},{7,6},{8,9},{9,8},{10,11... | collective-permute-start | bytes 417800 | tf_op jit(solution)/shard_map/ppermute | solution.py:743
  43.2 14.2 %all-to-all-start = ((f32[4,256,128]{2,1,0:T(8,128)}), f32[4,256,128]{2,1,0:T(8,128)S(1)}, u32[]{:S(2)}, u32[]{:S(2)}) async-start(f32[4,256,128]{2,1,0:T(8,128)} %get-tuple-element.94), calls=%async_computation | async-start | bytes 1048576 | tf_op jit(solution)/shard_map/all_to_all | solution.py:755
  58.6 10.4 %all-to-all-start.1 = ((bf16[4,256,128]{2,1,0:T(8,128)(2,1)}), bf16[4,256,128]{2,1,0:T(8,128)(2,1)S(1)}, u32[]{:S(2)}, u32[]{:S(2)}) async-start(bf16[4,256,128]{2,1,0:T(8,128)(2,1)} %get-tuple-element.108), calls=%async_computation.1 | async-start | bytes 524288 | tf_op jit(solution)/shard_map/all_to_all | solution.py:755
  69.1 15.1 %collective-permute-start.19 = (bf16[128,1024]{1,0:T(8,128)(2,1)S(1)}, bf16[128,1024]{1,0:T(8,128)(2,1)S(1)}, u32[]{:S(2)}, u32[]{:S(2)}) collective-permute-start(bf16[128,1024]{1,0:T(8,128)(2,1)S(1)} %get-tuple-element.121), channel_id=1, source_target_pairs={{0,48},{16,0},{32,16},{48,32},{64,112},{80,64},{96,80},{112,96},{1... | collective-permute-start | bytes 786440 | tf_op jit(solution)/shard_map/ppermute | solution.py:751
  73.2 11.0 %collective-permute-start.18 = (bf16[128,1024]{1,0:T(8,128)(2,1)S(1)}, bf16[128,1024]{1,0:T(8,128)(2,1)S(1)}, u32[]{:S(2)}, u32[]{:S(2)}) collective-permute-start(bf16[128,1024]{1,0:T(8,128)(2,1)S(1)} %get-tuple-element.120), channel_id=1, source_target_pairs={{0,32},{16,48},{32,0},{48,16},{64,96},{80,112},{96,64},{112,80},{1... | collective-permute-start | bytes 786440 | tf_op jit(solution)/shard_map/ppermute | solution.py:751
  73.8 13.0 %collective-permute-start.17 = (bf16[128,1024]{1,0:T(8,128)(2,1)S(1)}, bf16[128,1024]{1,0:T(8,128)(2,1)S(1)}, u32[]{:S(2)}, u32[]{:S(2)}) collective-permute-start(bf16[128,1024]{1,0:T(8,128)(2,1)S(1)} %get-tuple-element.119), channel_id=1, source_target_pairs={{0,16},{16,32},{32,48},{48,0},{64,80},{80,96},{96,112},{112,64},{1... | collective-permute-start | bytes 786440 | tf_op jit(solution)/shard_map/ppermute | solution.py:751
  83.5 4.9 %collective-permute-start.15 = (bf16[4,256,256]{2,1,0:T(8,128)(2,1)S(1)}, bf16[4,256,256]{2,1,0:T(8,128)(2,1)S(1)}, u32[]{:S(2)}, u32[]{:S(2)}) collective-permute-start(bf16[4,256,256]{2,1,0:T(8,128)(2,1)S(1)} %get-tuple-element.115), channel_id=1, source_target_pairs={{0,1},{1,0},{2,3},{3,2},{4,5},{5,4},{6,7},{7,6},{8,9},{9,8},{10,11... | collective-permute-start | bytes 1572872 | tf_op jit(solution)/shard_map/ppermute | solution.py:743
  83.6 4.8 %collective-permute-start.16 = (bf16[4,256,256]{2,1,0:T(8,128)(2,1)S(1)}, bf16[4,256,256]{2,1,0:T(8,128)(2,1)S(1)}, u32[]{:S(2)}, u32[]{:S(2)}) collective-permute-start(bf16[4,256,256]{2,1,0:T(8,128)(2,1)S(1)} %get-tuple-element.116), channel_id=1, source_target_pairs={{0,1},{1,0},{2,3},{3,2},{4,5},{5,4},{6,7},{7,6},{8,9},{9,8},{10,11... | collective-permute-start | bytes 1572872 | tf_op jit(solution)/shard_map/ppermute | solution.py:743
  87.0 1.4 %collective-permute-start.20 = (bf16[64,1024]{1,0:T(8,128)(2,1)S(1)}, bf16[64,1024]{1,0:T(8,128)(2,1)S(1)}, u32[]{:S(2)}, u32[]{:S(2)}) collective-permute-start(bf16[64,1024]{1,0:T(8,128)(2,1)S(1)} %slice.12), channel_id=1, source_target_pairs={{0,1},{1,0},{2,3},{3,2},{4,5},{5,4},{6,7},{7,6},{8,9},{9,8},{10,11... | collective-permute-start | bytes 393224 | tf_op jit(solution)/shard_map/ppermute | solution.py:743
  87.1 1.3 %collective-permute-start.21 = (f32[16,128]{1,0:T(8,128)S(1)}, f32[16,128]{1,0:T(8,128)S(1)}, u32[]{:S(2)}, u32[]{:S(2)}) collective-permute-start(f32[16,128]{1,0:T(8,128)S(1)} %get-tuple-element.122.rab), channel_id=1, source_target_pairs={{0,1},{1,0},{2,3},{3,2},{4,5},{5,4},{6,7},{7,6},{8,9},{9,8},{10,11... | collective-permute-start | bytes 24584 | tf_op jit(solution)/shard_map/ppermute | solution.py:743
  88.7 8.4 %collective-permute-start.25 = (bf16[304,256]{1,0:T(8,128)(2,1)S(1)}, bf16[304,256]{1,0:T(8,128)(2,1)S(1)}, u32[]{:S(2)}, u32[]{:S(2)}) collective-permute-start(bf16[304,256]{1,0:T(8,128)(2,1)S(1)} %get-tuple-element.140), channel_id=1, source_target_pairs={{0,8},{1,9},{2,10},{3,11},{4,12},{5,13},{6,14},{7,15},{8,0},{9,1},... | collective-permute-start | bytes 466952 | tf_op jit(solution)/shard_map/ppermute | solution.py:743
  88.8 11.8 %collective-permute-start.26 = (bf16[304,256]{1,0:T(8,128)(2,1)S(1)}, bf16[304,256]{1,0:T(8,128)(2,1)S(1)}, u32[]{:S(2)}, u32[]{:S(2)}) collective-permute-start(bf16[304,256]{1,0:T(8,128)(2,1)S(1)} %get-tuple-element.141), channel_id=1, source_target_pairs={{0,10},{1,11},{2,12},{3,13},{4,14},{5,15},{6,8},{7,9},{8,2},{9,3},... | collective-permute-start | bytes 466952 | tf_op jit(solution)/shard_map/ppermute | solution.py:743
  92.4 16.0 %collective-permute-start.22 = (bf16[432,256]{1,0:T(8,128)(2,1)S(1)}, bf16[432,256]{1,0:T(8,128)(2,1)S(1)}, u32[]{:S(2)}, u32[]{:S(2)}) collective-permute-start(bf16[432,256]{1,0:T(8,128)(2,1)S(1)} %get-tuple-element.137), channel_id=1, source_target_pairs={{0,2},{1,3},{2,4},{3,5},{4,6},{5,7},{6,0},{7,1},{8,10},{9,11},{10,... | collective-permute-start | bytes 663560 | tf_op jit(solution)/shard_map/ppermute | solution.py:743
  92.4 20.2 %collective-permute-start.23 = (bf16[432,256]{1,0:T(8,128)(2,1)S(1)}, bf16[432,256]{1,0:T(8,128)(2,1)S(1)}, u32[]{:S(2)}, u32[]{:S(2)}) collective-permute-start(bf16[432,256]{1,0:T(8,128)(2,1)S(1)} %get-tuple-element.138), channel_id=1, source_target_pairs={{0,4},{1,5},{2,6},{3,7},{4,0},{5,1},{6,2},{7,3},{8,12},{9,13},{10,... | collective-permute-start | bytes 663560 | tf_op jit(solution)/shard_map/ppermute | solution.py:743
  96.5 16.4 %collective-permute-start.24 = (bf16[432,256]{1,0:T(8,128)(2,1)S(1)}, bf16[432,256]{1,0:T(8,128)(2,1)S(1)}, u32[]{:S(2)}, u32[]{:S(2)}) collective-permute-start(bf16[432,256]{1,0:T(8,128)(2,1)S(1)} %get-tuple-element.139), channel_id=1, source_target_pairs={{0,6},{1,7},{2,0},{3,1},{4,2},{5,3},{6,4},{7,5},{8,14},{9,15},{10,... | collective-permute-start | bytes 663560 | tf_op jit(solution)/shard_map/ppermute | solution.py:743
  97.2 9.5 %collective-permute-start.27 = (bf16[304,256]{1,0:T(8,128)(2,1)S(1)}, bf16[304,256]{1,0:T(8,128)(2,1)S(1)}, u32[]{:S(2)}, u32[]{:S(2)}) collective-permute-start(bf16[304,256]{1,0:T(8,128)(2,1)S(1)} %get-tuple-element.142), channel_id=1, source_target_pairs={{0,12},{1,13},{2,14},{3,15},{4,8},{5,9},{6,10},{7,11},{8,4},{9,5},... | collective-permute-start | bytes 466952 | tf_op jit(solution)/shard_map/ppermute | solution.py:743
  100.6 7.7 %collective-permute-start.28 = (bf16[304,256]{1,0:T(8,128)(2,1)S(1)}, bf16[304,256]{1,0:T(8,128)(2,1)S(1)}, u32[]{:S(2)}, u32[]{:S(2)}) collective-permute-start(bf16[304,256]{1,0:T(8,128)(2,1)S(1)} %get-tuple-element.143), channel_id=1, source_target_pairs={{0,14},{1,15},{2,8},{3,9},{4,10},{5,11},{6,12},{7,13},{8,6},{9,7},... | collective-permute-start | bytes 466952 | tf_op jit(solution)/shard_map/ppermute | solution.py:743
  114.2 13.3 %all-to-all-start.2 = ((f32[8,8,1024]{2,1,0:T(8,128)}), f32[8,8,1024]{2,1,0:T(8,128)S(1)}, u32[]{:S(2)}, u32[]{:S(2)}) async-start(f32[8,8,1024]{2,1,0:T(8,128)} %collect.1), calls=%async_computation.2 | async-start | bytes 524288 | tf_op jit(solution)/shard_map/all_to_all | solution.py:799
  (3 other events, 67.3 us)

commit v6 on v5

--- a/solution.py
+++ b/solution.py
@@ -20,7 +20,7 @@
 QT = 8
 SCALE = 1.0 / math.sqrt(128.0)
 LIST = 160
-FAR_U = 8
+FAR_U = 12
 NEAR_U = 8
 NEAR_FLAG = 32768
 DUMMY = QT + 16 * TILES
@@ -781,7 +781,7 @@
     mixed, grad_gate, grads = middle(swap_z(heads), gate, slope, grad_mix)
     grads = swap_z(grads)
     output, proj, *proj_x = finish_output(ids, tokens, cotangent, out_proj, mixed)
-    grads, proj_x = lax.optimization_barrier((grads, proj_x))
+    grads, _ = lax.optimization_barrier((grads, proj_x))
     proj_x = [send_x(proj_x[s - 1], s) for s in (1, 2, 3)]
 
     mine_s, mine_o, theirs_s, theirs_o, dq, rab = attend_back(ids, table, lengths, saved, grads)

time: 128 us -> 126 us (0.984); the launches traced: 128 us -> 124 us
  waiting for transfers between devices: 33.8 us -> 26.7 us
  Pallas kernels: 45.1 us -> 47.6 us
    all_to_all x2, waiting for transfers between devices: 9.3 us -> 4.65 us  [swap_z(): lax.all_to_all(part, 'ctx', 0, 0, axis_index_groups=OVER_Z, tiled=True)]
    all_to_all x1, starting transfers between devices: 6.56 us -> 4.41 us  [on_device(): lines = lax.all_to_all(collect(ids, same, other), 'dp', 0, 0, tiled=True)]
    ppermute x26, starting transfers between devices: 29 us -> 30.8 us  [send(): return lax.ppermute(x, 'ctx', move(y_xor, z_shift, core_xor))]
    pallas_call x1, Pallas kernels: 9.5 us -> 11.3 us  [attend_back(): pl.pallas_call(backward_kernel, in_specs=[SMEM] * 6 + [VMEM] * 5, out_spe...]
    ppermute x3, waiting for transfers between devices: 2.68 us -> 1.03 us  [send_x(): lax.ppermute(part, 'dp', [(d, d // 4 * 4 + (d + shift) % 4) for d in rang...]
  transfers between devices with their start and end apart: 32 -> 32, of which waited for: 15 -> 13; matrix products, arithmetic and copies ran while one was open for 1% -> 2% of each run, Pallas kernels for 25% -> 28%
where the time goes in v6:
time: 126 us; the launch traced here: 124 us
  Pallas kernels  47.6 us (38%)
  starting transfers between devices  46.9 us (37%)
  waiting for transfers between devices  26.7 us (21%)
  other arithmetic  2.09 us (2%)
    ppermute x26, starting transfers between devices, send(): return lax.ppermute(x, 'ctx', move(y_xor, z_shift, core_xor))  30.8 us
    ppermute x26, waiting for transfers between devices, send(): return lax.ppermute(x, 'ctx', move(y_xor, z_shift, core_xor))  21 us
    pallas_call x1, Pallas kernels, attend_back(): pl.pallas_call(backward_kernel, in_specs=[SMEM] * 6 + [VMEM] * 5, out_spe...  11.3 us
    pallas_call x1, Pallas kernels, attend(): pl.pallas_call(forward_kernel, in_specs=[SMEM] * 3 + [VMEM] * 16, out_spe...  8.86 us
    pallas_call x2, Pallas kernels, project(): pl.pallas_call(functools.partial(project_kernel, int(own)), grid=(HEADS,)...  7.71 us
    all_to_all x2, starting transfers between devices, swap_z(): lax.all_to_all(part, 'ctx', 0, 0, axis_index_groups=OVER_Z, tiled=True)  6.89 us
    pallas_call x1, Pallas kernels, make_gates(): pl.pallas_call(gates_kernel, grid=(4,), in_specs=[whole((256, 1024)), pl....  5.55 us
    ppermute x3, starting transfers between devices, send_x(): lax.ppermute(part, 'dp', [(d, d // 4 * 4 + (d + shift) % 4) for d in rang...  4.81 us
  transfers between devices with their start and end apart: 32, of which 13 were waited for; matrix products, arithmetic and copies ran while one was open for 2% of the time, Pallas kernels for 28%

profile of v6, /device:TPU:24, one launch (start us, length us, event | category | flops | bytes accessed | tf_op | source)
XLA Modules:
  0.0 124.1 jit_solution(10374020658283139797)
XLA Ops:
  1.7 1.3 %collective-permute-start.3 = (bf16[272,1024]{1,0:T(8,128)(2,1)S(1)}, bf16[272,1024]{1,0:T(8,128)(2,1)S(1)}, u32[]{:S(2)}, u32[]{:S(2)}) collective-permute-start(bf16[272,1024]{1,0:T(8,128)(2,1)S(1)} %pack.1.tokens), channel_id=1, source_target_pairs={{0,8},{1,9},{2,10},{3,11},{4,12},{5,13},{6,14},{7,15},{8,0},{9,1},... | collective-permute-start | bytes 1671176 | tf_op jit(solution)/shard_map/ppermute | solution.py:743
  3.0 4.2 %project_own.1 = (bf16[272,384]{1,0:T(8,128)(2,1)S(1)}, bf16[272,384]{1,0:T(8,128)(2,1)S(1)}, bf16[272,384]{1,0:T(8,128)(2,1)S(1)}, bf16[272,384]{1,0:T(8,128)(2,1)S(1)}) custom-call(bf16[272,1024]{1,0:T(8,128)(2,1)S(1)} %pack.1.tokens, s32[1,2,32]{2,1,0:T(2,128)} %refs_0_.2, bf16[1024,2048]{1,0:T(8,128)(2,1)} %in_proj.3, bf16[1024,2048]{1,0:T(8,128)(2,1)} %in_proj.3, ...), custom_call_target="tpu_custom_call" | custom-call | flops 805306368 | bytes 5242880 | tf_op jit(solution)/shard_map/project_own/pallas_call | solution.py:122
  8.1 1.9 %collective-permute-start = (bf16[272,384]{1,0:T(8,128)(2,1)S(1)}, bf16[272,384]{1,0:T(8,128)(2,1)S(1)}, u32[]{:S(2)}, u32[]{:S(2)}) collective-permute-start(bf16[272,384]{1,0:T(8,128)(2,1)S(1)} %get-tuple-element.79), channel_id=1, source_target_pairs={{0,2},{1,3},{2,4},{3,5},{4,6},{5,7},{6,0},{7,1},{8,10},{9,11},{10,... | collective-permute-start | bytes 626696 | tf_op jit(solution)/shard_map/ppermute | solution.py:743
  10.0 3.6 %collective-permute-start.1 = (bf16[272,384]{1,0:T(8,128)(2,1)S(1)}, bf16[272,384]{1,0:T(8,128)(2,1)S(1)}, u32[]{:S(2)}, u32[]{:S(2)}) collective-permute-start(bf16[272,384]{1,0:T(8,128)(2,1)S(1)} %get-tuple-element.80), channel_id=1, source_target_pairs={{0,4},{1,5},{2,6},{3,7},{4,0},{5,1},{6,2},{7,3},{8,12},{9,13},{10,... | collective-permute-start | bytes 626696 | tf_op jit(solution)/shard_map/ppermute | solution.py:743
  14.6 3.1 %collective-permute-done.3.tokens = bf16[272,1024]{1,0:T(8,128)(2,1)S(1)} collective-permute-done((bf16[272,1024]{1,0:T(8,128)(2,1)S(1)}, bf16[272,1024]{1,0:T(8,128)(2,1)S(1)}, u32[]{:S(2)}, u32[]{:S(2)}) %collective-permute-start.3) | collective-permute-done | bytes 557088 | tf_op jit(solution)/shard_map/ppermute | solution.py:743
  17.7 3.5 %project_other.1 = (bf16[272,256]{1,0:T(8,128)(2,1)S(1)}, bf16[272,256]{1,0:T(8,128)(2,1)S(1)}, bf16[272,256]{1,0:T(8,128)(2,1)S(1)}, bf16[272,256]{1,0:T(8,128)(2,1)S(1)}) custom-call(bf16[272,1024]{1,0:T(8,128)(2,1)S(1)} %collective-permute-done.3.tokens, bf16[1024,2048]{1,0:T(8,128)(2,1)} %in_proj.3, bf16[1024,2048]{1,0:T(8,128)(2,1)} %in_proj.3), custom_call_target="tpu_custom_call" | custom-call | flops 536870912 | bytes 5242880 | tf_op jit(solution)/shard_map/project_other/pallas_call | solution.py:122
  21.2 2.0 %collective-permute-start.4 = (bf16[272,256]{1,0:T(8,128)(2,1)S(1)}, bf16[272,256]{1,0:T(8,128)(2,1)S(1)}, u32[]{:S(2)}, u32[]{:S(2)}) collective-permute-start(bf16[272,256]{1,0:T(8,128)(2,1)S(1)} %get-tuple-element.82), channel_id=1, source_target_pairs={{0,2},{1,3},{2,4},{3,5},{4,6},{5,7},{6,0},{7,1},{8,10},{9,11},{10,... | collective-permute-start | bytes 417800 | tf_op jit(solution)/shard_map/ppermute | solution.py:743
  23.2 3.6 %collective-permute-start.9 = (bf16[272,256]{1,0:T(8,128)(2,1)S(1)}, bf16[272,256]{1,0:T(8,128)(2,1)S(1)}, u32[]{:S(2)}, u32[]{:S(2)}) collective-permute-start(bf16[272,256]{1,0:T(8,128)(2,1)S(1)} %get-tuple-element.89), channel_id=1, source_target_pairs={{0,4},{1,5},{2,6},{3,7},{4,0},{5,1},{6,2},{7,3},{8,12},{9,13},{10,... | collective-permute-start | bytes 417800 | tf_op jit(solution)/shard_map/ppermute | solution.py:743
  27.8 1.7 %collective-permute-done.4.refs_9_ = bf16[272,256]{1,0:T(8,128)(2,1)S(1)} collective-permute-done((bf16[272,256]{1,0:T(8,128)(2,1)S(1)}, bf16[272,256]{1,0:T(8,128)(2,1)S(1)}, u32[]{:S(2)}, u32[]{:S(2)}) %collective-permute-start.4) | collective-permute-done | bytes 139296 | tf_op jit(solution)/shard_map/ppermute | solution.py:743
  29.5 2.8 %collective-permute-done.9.refs_10_ = bf16[272,256]{1,0:T(8,128)(2,1)S(1)} collective-permute-done((bf16[272,256]{1,0:T(8,128)(2,1)S(1)}, bf16[272,256]{1,0:T(8,128)(2,1)S(1)}, u32[]{:S(2)}, u32[]{:S(2)}) %collective-permute-start.9) | collective-permute-done | bytes 139296 | tf_op jit(solution)/shard_map/ppermute | solution.py:743
  35.1 8.9 %attend.1 = (f32[4,256,128]{2,1,0:T(8,128)}, s32[160]{0:T(256)S(1)}, s32[160]{0:T(256)S(1)}, s32[8]{0:T(128)S(1)}, bf16[33,128,128]{2,1,0:T(8,128)(2,1)}, /*inde...) custom-call(s32[4]{0:T(128)S(1)} %pad_add_fusion.ids, f32[32]{0:T(128)S(1)} %pad_maximum_fusion.table, ...), custom_call_target="tpu_custom_call" | custom-call | flops 6000000000 | bytes 6291456 | tf_op jit(solution)/shard_map/attend/pallas_call | solution.py:361
  43.9 3.5 %all-to-all-start = ((f32[4,256,128]{2,1,0:T(8,128)}), f32[4,256,128]{2,1,0:T(8,128)S(1)}, u32[]{:S(2)}, u32[]{:S(2)}) async-start(f32[4,256,128]{2,1,0:T(8,128)} %get-tuple-element.91), calls=%async_computation | async-start | bytes 1048576 | tf_op jit(solution)/shard_map/all_to_all | solution.py:755
  47.4 5.5 %gates.1 = (bf16[256,512]{1,0:T(8,128)(2,1)S(1)}, bf16[256,2048]{1,0:T(8,128)(2,1)S(1)}, f32[256,512]{1,0:T(8,128)S(1)}) custom-call(bf16[256,1024]{1,0:T(8,128)(2,1)} %tokens.7, bf16[1024,2048]{1,0:T(8,128)(2,1)} %in_proj.3, bf16[256,1024]{1,0:T(8,128)(2,1)} %cot.4, bf16[512,1024]{1,0:T(8,128)(2,1)} %out_proj.3), custom_call_target="tpu_custom_call" | custom-call | flops 1073741824 | bytes 7340032 | tf_op jit(solution)/shard_map/gates/pallas_call | solution.py:154
  53.0 4.6 %all-to-all-done.heads = f32[4,256,128]{2,1,0:T(8,128)S(1)} async-done(((f32[4,256,128]{2,1,0:T(8,128)}), f32[4,256,128]{2,1,0:T(8,128)S(1)}, u32[]{:S(2)}, u32[]{:S(2)}) %all-to-all-start) | async-done | bytes 524320 | tf_op jit(solution)/shard_map/all_to_all | solution.py:755
  58.9 3.4 %all-to-all-start.1 = ((bf16[4,256,128]{2,1,0:T(8,128)(2,1)}), bf16[4,256,128]{2,1,0:T(8,128)(2,1)S(1)}, u32[]{:S(2)}, u32[]{:S(2)}) async-start(bf16[4,256,128]{2,1,0:T(8,128)(2,1)} %get-tuple-element.105), calls=%async_computation.1 | async-start | bytes 524288 | tf_op jit(solution)/shard_map/all_to_all | solution.py:755
  62.3 2.9 %finish_output.1 = (bf16[256,1024]{1,0:T(8,128)(2,1)}, f32[128,1024]{1,0:T(8,128)S(1)}, bf16[128,1024]{1,0:T(8,128)(2,1)S(1)}, bf16[128,1024]{1,0:T(8,128)(2,1)S(1)}, bf16[128,1024]{1,0:T(8,128)(2,1)S(1)}) custom-call(s32[4]{0:T(128)S(1)} %pad_add_fusion.ids, bf16[256,1024]{1,0:T(8,128)(2,1)} %tokens.7, bf16[256,1024]{1,0:T(8,128)(2,1)} %cot.4, ...), custom_call_target="tpu_custom_call" | custom-call | flops 805306368 | bytes 5242880 | tf_op jit(solution)/shard_map/finish_output/pallas_call | solution.py:435
  65.1 2.5 %collective-permute-start.19 = (bf16[128,1024]{1,0:T(8,128)(2,1)S(1)}, bf16[128,1024]{1,0:T(8,128)(2,1)}, u32[]{:S(2)}, u32[]{:S(2)}) collective-permute-start(bf16[128,1024]{1,0:T(8,128)(2,1)S(1)} %get-tuple-element.108), channel_id=1, source_target_pairs={{0,48},{16,0},{32,16},{48,32},{64,112},{80,64},{96,80},{112,96},{1... | collective-permute-start | bytes 786440 | tf_op jit(solution)/shard_map/ppermute | solution.py:751
  68.5 1.4 %collective-permute-start.17 = (bf16[128,1024]{1,0:T(8,128)(2,1)S(1)}, bf16[128,1024]{1,0:T(8,128)(2,1)}, u32[]{:S(2)}, u32[]{:S(2)}) collective-permute-start(bf16[128,1024]{1,0:T(8,128)(2,1)S(1)} %get-tuple-element.106), channel_id=1, source_target_pairs={{0,16},{16,32},{32,48},{48,0},{64,80},{80,96},{96,112},{112,64},{1... | collective-permute-start | bytes 786440 | tf_op jit(solution)/shard_map/ppermute | solution.py:751
  70.0 11.3 %attend_back.1 = (bf16[4,256,256]{2,1,0:T(8,128)(2,1)S(1)}, bf16[4,256,256]{2,1,0:T(8,128)(2,1)S(1)}, bf16[4,256,256]{2,1,0:T(8,128)(2,1)S(1)}, bf16[4,256,256]{...) custom-call(s32[4]{0:T(128)S(1)} %pad_add_fusion.ids, f32[32]{0:T(128)S(1)} %pad_maximum_fusion.table, ...), custom_call_target="tpu_custom_call" | custom-call | flops 12000000000 | bytes 8388608 | tf_op jit(solution)/shard_map/attend_back/pallas_call | solution.py:554
  85.9 1.4 %collective-permute-start.25 = (bf16[304,256]{1,0:T(8,128)(2,1)S(1)}, bf16[304,256]{1,0:T(8,128)(2,1)S(1)}, u32[]{:S(2)}, u32[]{:S(2)}) collective-permute-start(bf16[304,256]{1,0:T(8,128)(2,1)S(1)} %get-tuple-element.134), channel_id=1, source_target_pairs={{0,8},{1,9},{2,10},{3,11},{4,12},{5,13},{6,14},{7,15},{8,0},{9,1},... | collective-permute-start | bytes 466952 | tf_op jit(solution)/shard_map/ppermute | solution.py:743
  87.3 3.4 %collective-permute-start.26 = (bf16[304,256]{1,0:T(8,128)(2,1)S(1)}, bf16[304,256]{1,0:T(8,128)(2,1)S(1)}, u32[]{:S(2)}, u32[]{:S(2)}) collective-permute-start(bf16[304,256]{1,0:T(8,128)(2,1)S(1)} %get-tuple-element.135), channel_id=1, source_target_pairs={{0,10},{1,11},{2,12},{3,13},{4,14},{5,15},{6,8},{7,9},{8,2},{9,3},... | collective-permute-start | bytes 466952 | tf_op jit(solution)/shard_map/ppermute | solution.py:743
  90.6 1.5 %collective-permute-start.22 = (bf16[432,256]{1,0:T(8,128)(2,1)S(1)}, bf16[432,256]{1,0:T(8,128)(2,1)S(1)}, u32[]{:S(2)}, u32[]{:S(2)}) collective-permute-start(bf16[432,256]{1,0:T(8,128)(2,1)S(1)} %get-tuple-element.131), channel_id=1, source_target_pairs={{0,2},{1,3},{2,4},{3,5},{4,6},{5,7},{6,0},{7,1},{8,10},{9,11},{10,... | collective-permute-start | bytes 663560 | tf_op jit(solution)/shard_map/ppermute | solution.py:743
  92.1 1.5 %collective-permute-start.23 = (bf16[432,256]{1,0:T(8,128)(2,1)S(1)}, bf16[432,256]{1,0:T(8,128)(2,1)S(1)}, u32[]{:S(2)}, u32[]{:S(2)}) collective-permute-start(bf16[432,256]{1,0:T(8,128)(2,1)S(1)} %get-tuple-element.132), channel_id=1, source_target_pairs={{0,4},{1,5},{2,6},{3,7},{4,0},{5,1},{6,2},{7,3},{8,12},{9,13},{10,... | collective-permute-start | bytes 663560 | tf_op jit(solution)/shard_map/ppermute | solution.py:743
  93.6 2.3 %collective-permute-start.24 = (bf16[432,256]{1,0:T(8,128)(2,1)S(1)}, bf16[432,256]{1,0:T(8,128)(2,1)S(1)}, u32[]{:S(2)}, u32[]{:S(2)}) collective-permute-start(bf16[432,256]{1,0:T(8,128)(2,1)S(1)} %get-tuple-element.133), channel_id=1, source_target_pairs={{0,6},{1,7},{2,0},{3,1},{4,2},{5,3},{6,4},{7,5},{8,14},{9,15},{10,... | collective-permute-start | bytes 663560 | tf_op jit(solution)/shard_map/ppermute | solution.py:743
  95.9 2.3 %collective-permute-start.27 = (bf16[304,256]{1,0:T(8,128)(2,1)S(1)}, bf16[304,256]{1,0:T(8,128)(2,1)S(1)}, u32[]{:S(2)}, u32[]{:S(2)}) collective-permute-start(bf16[304,256]{1,0:T(8,128)(2,1)S(1)} %get-tuple-element.136), channel_id=1, source_target_pairs={{0,12},{1,13},{2,14},{3,15},{4,8},{5,9},{6,10},{7,11},{8,4},{9,5},... | collective-permute-start | bytes 466952 | tf_op jit(solution)/shard_map/ppermute | solution.py:743
  99.5 1.6 %collective-permute-start.28 = (bf16[304,256]{1,0:T(8,128)(2,1)S(1)}, bf16[304,256]{1,0:T(8,128)(2,1)S(1)}, u32[]{:S(2)}, u32[]{:S(2)}) collective-permute-start(bf16[304,256]{1,0:T(8,128)(2,1)S(1)} %get-tuple-element.137), channel_id=1, source_target_pairs={{0,14},{1,15},{2,8},{3,9},{4,10},{5,11},{6,12},{7,13},{8,6},{9,7},... | collective-permute-start | bytes 466952 | tf_op jit(solution)/shard_map/ppermute | solution.py:743
  101.1 5.3 %collective-permute-done.27.refs_6_.refs_14_ = bf16[304,256]{1,0:T(8,128)(2,1)S(1)} collective-permute-done((bf16[304,256]{1,0:T(8,128)(2,1)S(1)}, bf16[304,256]{1,0:T(8,128)(2,1)S(1)}, u32[]{:S(2)}, u32[]{:S(2)}) %collective-permute-start.27) | collective-permute-done | bytes 155680 | tf_op jit(solution)/shard_map/ppermute | solution.py:743
  107.3 3.1 %collective-permute-done.22.refs_1_.refs_9_ = bf16[432,256]{1,0:T(8,128)(2,1)S(1)} collective-permute-done((bf16[432,256]{1,0:T(8,128)(2,1)S(1)}, bf16[432,256]{1,0:T(8,128)(2,1)S(1)}, u32[]{:S(2)}, u32[]{:S(2)}) %collective-permute-start.22) | collective-permute-done | bytes 221216 | tf_op jit(solution)/shard_map/ppermute | solution.py:743
  110.9 1.4 %collect.1 = f32[8,8,1024]{2,1,0:T(8,128)} custom-call(s32[4]{0:T(128)S(1)} %pad_add_fusion.ids, bf16[432,256]{1,0:T(8,128)(2,1)S(1)} %get-tuple-element.130.refs_0_.refs_8_, bf16[432,256]{1,0:T(8,128)(2,1)S(1)} %collective-permute-done.22.refs_1_.refs_9_, bf16[432,256]{1,0:T(8,128)(2,1)S(1)} %collective-permute-done.23.refs_2_.refs_10_, ...), custom_call_target="tpu_custom_call" | custom-call | flops 65536 | bytes 262144 | tf_op jit(solution)/shard_map/collect/pallas_call | solution.py:629
  112.4 4.4 %all-to-all-start.2 = ((f32[8,8,1024]{2,1,0:T(8,128)}), f32[8,8,1024]{2,1,0:T(8,128)S(1)}, u32[]{:S(2)}, u32[]{:S(2)}) async-start(f32[8,8,1024]{2,1,0:T(8,128)} %collect.1), calls=%async_computation.2 | async-start | bytes 524288 | tf_op jit(solution)/shard_map/all_to_all | solution.py:799
  116.8 3.4 %ready.1 = (f32[256,1024]{1,0:T(8,128)S(1)}, f32[256,128]{1,0:T(8,128)S(1)}, bf16[256,1024]{1,0:T(8,128)(2,1)S(1)}, bf16[1024,2048]{1,0:T(8,128)(2,1)S(1)}) custom-call(bf16[256,1024]{1,0:T(8,128)(2,1)} %tokens.7, bf16[256,1024]{1,0:T(8,128)(2,1)} %cot.4, bf16[1024,2048]{1,0:T(8,128)(2,1)} %in_proj.3), custom_call_target="tpu_custom_call" | custom-call | flops 4194304 | bytes 6291456 | tf_op jit(solution)/shard_map/ready/pallas_call | solution.py:681
  120.1 3.4 %finish_grad.1 = bf16[256,1024]{1,0:T(8,128)(2,1)} custom-call(s32[4]{0:T(128)S(1)} %pad_add_fusion.ids, bf16[256,512]{1,0:T(8,128)(2,1)S(1)} %copy-done, bf16[256,2048]{1,0:T(8,128)(2,1)S(1)} %get-tuple-element.93.slope, f32[256,1024]{1,0:T(8,128)S(1)} %get-tuple-element.126.normed, f32[256,128]{1,0:T(8,128)S(1)} %get-tuple-element.127.inverse, ...), custom_call_target="tpu_custom_call" | custom-call | flops 1073741824 | bytes 8388608 | tf_op jit(solution)/shard_map/finish_grad/pallas_call | solution.py:721
  (58 shorter events, 16.8 us)
Async XLA Ops:
  1.7 15.9 %collective-permute-start.3 = (bf16[272,1024]{1,0:T(8,128)(2,1)S(1)}, bf16[272,1024]{1,0:T(8,128)(2,1)S(1)}, u32[]{:S(2)}, u32[]{:S(2)}) collective-permute-start(bf16[272,1024]{1,0:T(8,128)(2,1)S(1)} %pack.1.tokens), channel_id=1, source_target_pairs={{0,8},{1,9},{2,10},{3,11},{4,12},{5,13},{6,14},{7,15},{8,0},{9,1},... | collective-permute-start | bytes 1671176 | tf_op jit(solution)/shard_map/ppermute | solution.py:743
  8.1 18.7 %collective-permute-start = (bf16[272,384]{1,0:T(8,128)(2,1)S(1)}, bf16[272,384]{1,0:T(8,128)(2,1)S(1)}, u32[]{:S(2)}, u32[]{:S(2)}) collective-permute-start(bf16[272,384]{1,0:T(8,128)(2,1)S(1)} %get-tuple-element.79), channel_id=1, source_target_pairs={{0,2},{1,3},{2,4},{3,5},{4,6},{5,7},{6,0},{7,1},{8,10},{9,11},{10,... | collective-permute-start | bytes 626696 | tf_op jit(solution)/shard_map/ppermute | solution.py:743
  10.0 17.8 %collective-permute-start.1 = (bf16[272,384]{1,0:T(8,128)(2,1)S(1)}, bf16[272,384]{1,0:T(8,128)(2,1)S(1)}, u32[]{:S(2)}, u32[]{:S(2)}) collective-permute-start(bf16[272,384]{1,0:T(8,128)(2,1)S(1)} %get-tuple-element.80), channel_id=1, source_target_pairs={{0,4},{1,5},{2,6},{3,7},{4,0},{5,1},{6,2},{7,3},{8,12},{9,13},{10,... | collective-permute-start | bytes 626696 | tf_op jit(solution)/shard_map/ppermute | solution.py:743
  13.6 14.2 %collective-permute-start.2 = (bf16[272,384]{1,0:T(8,128)(2,1)S(1)}, bf16[272,384]{1,0:T(8,128)(2,1)S(1)}, u32[]{:S(2)}, u32[]{:S(2)}) collective-permute-start(bf16[272,384]{1,0:T(8,128)(2,1)S(1)} %get-tuple-element.81), channel_id=1, source_target_pairs={{0,6},{1,7},{2,0},{3,1},{4,2},{5,3},{6,4},{7,5},{8,14},{9,15},{10,... | collective-permute-start | bytes 626696 | tf_op jit(solution)/shard_map/ppermute | solution.py:743
  21.2 8.3 %collective-permute-start.4 = (bf16[272,256]{1,0:T(8,128)(2,1)S(1)}, bf16[272,256]{1,0:T(8,128)(2,1)S(1)}, u32[]{:S(2)}, u32[]{:S(2)}) collective-permute-start(bf16[272,256]{1,0:T(8,128)(2,1)S(1)} %get-tuple-element.82), channel_id=1, source_target_pairs={{0,2},{1,3},{2,4},{3,5},{4,6},{5,7},{6,0},{7,1},{8,10},{9,11},{10,... | collective-permute-start | bytes 417800 | tf_op jit(solution)/shard_map/ppermute | solution.py:743
  23.2 9.1 %collective-permute-start.9 = (bf16[272,256]{1,0:T(8,128)(2,1)S(1)}, bf16[272,256]{1,0:T(8,128)(2,1)S(1)}, u32[]{:S(2)}, u32[]{:S(2)}) collective-permute-start(bf16[272,256]{1,0:T(8,128)(2,1)S(1)} %get-tuple-element.89), channel_id=1, source_target_pairs={{0,4},{1,5},{2,6},{3,7},{4,0},{5,1},{6,2},{7,3},{8,12},{9,13},{10,... | collective-permute-start | bytes 417800 | tf_op jit(solution)/shard_map/ppermute | solution.py:743
  26.8 6.0 %collective-permute-start.10 = (bf16[272,256]{1,0:T(8,128)(2,1)S(1)}, bf16[272,256]{1,0:T(8,128)(2,1)S(1)}, u32[]{:S(2)}, u32[]{:S(2)}) collective-permute-start(bf16[272,256]{1,0:T(8,128)(2,1)S(1)} %get-tuple-element.90), channel_id=1, source_target_pairs={{0,6},{1,7},{2,0},{3,1},{4,2},{5,3},{6,4},{7,5},{8,14},{9,15},{10,... | collective-permute-start | bytes 417800 | tf_op jit(solution)/shard_map/ppermute | solution.py:743
  27.8 5.0 %collective-permute-start.11 = (bf16[272,256]{1,0:T(8,128)(2,1)S(1)}, bf16[272,256]{1,0:T(8,128)(2,1)S(1)}, u32[]{:S(2)}, u32[]{:S(2)}) collective-permute-start(bf16[272,256]{1,0:T(8,128)(2,1)S(1)} %get-tuple-element.87.refs_8_), channel_id=1, source_target_pairs={{0,1},{1,0},{2,3},{3,2},{4,5},{5,4},{6,7},{7,6},{8,9},{9,8},{10,11... | collective-permute-start | bytes 417800 | tf_op jit(solution)/shard_map/ppermute | solution.py:743
  29.5 3.8 %collective-permute-start.12 = (bf16[272,256]{1,0:T(8,128)(2,1)S(1)}, bf16[272,256]{1,0:T(8,128)(2,1)S(1)}, u32[]{:S(2)}, u32[]{:S(2)}) collective-permute-start(bf16[272,256]{1,0:T(8,128)(2,1)S(1)} %collective-permute-done.4.refs_9_), channel_id=1, source_target_pairs={{0,1},{1,0},{2,3},{3,2},{4,5},{5,4},{6,7},{7,6},{8,9},{9,8},{10,11... | collective-permute-start | bytes 417800 | tf_op jit(solution)/shard_map/ppermute | solution.py:743
  32.3 1.4 %collective-permute-start.13 = (bf16[272,256]{1,0:T(8,128)(2,1)S(1)}, bf16[272,256]{1,0:T(8,128)(2,1)S(1)}, u32[]{:S(2)}, u32[]{:S(2)}) collective-permute-start(bf16[272,256]{1,0:T(8,128)(2,1)S(1)} %collective-permute-done.9.refs_10_), channel_id=1, source_target_pairs={{0,1},{1,0},{2,3},{3,2},{4,5},{5,4},{6,7},{7,6},{8,9},{9,8},{10,11... | collective-permute-start | bytes 417800 | tf_op jit(solution)/shard_map/ppermute | solution.py:743
  32.3 2.8 %collective-permute-start.5 = (bf16[272,384]{1,0:T(8,128)(2,1)S(1)}, bf16[272,384]{1,0:T(8,128)(2,1)S(1)}, u32[]{:S(2)}, u32[]{:S(2)}) collective-permute-start(bf16[272,384]{1,0:T(8,128)(2,1)S(1)} %get-tuple-element.83.refs_0_), channel_id=1, source_target_pairs={{0,1},{1,0},{2,3},{3,2},{4,5},{5,4},{6,7},{7,6},{8,9},{9,8},{10,11... | collective-permute-start | bytes 626696 | tf_op jit(solution)/shard_map/ppermute | solution.py:743
  32.8 2.3 %collective-permute-start.6 = (bf16[272,384]{1,0:T(8,128)(2,1)S(1)}, bf16[272,384]{1,0:T(8,128)(2,1)S(1)}, u32[]{:S(2)}, u32[]{:S(2)}) collective-permute-start(bf16[272,384]{1,0:T(8,128)(2,1)S(1)} %collective-permute-done.refs_1_), channel_id=1, source_target_pairs={{0,1},{1,0},{2,3},{3,2},{4,5},{5,4},{6,7},{7,6},{8,9},{9,8},{10,11... | collective-permute-start | bytes 626696 | tf_op jit(solution)/shard_map/ppermute | solution.py:743
  32.8 2.3 %collective-permute-start.7 = (bf16[272,384]{1,0:T(8,128)(2,1)S(1)}, bf16[272,384]{1,0:T(8,128)(2,1)S(1)}, u32[]{:S(2)}, u32[]{:S(2)}) collective-permute-start(bf16[272,384]{1,0:T(8,128)(2,1)S(1)} %collective-permute-done.1.refs_2_), channel_id=1, source_target_pairs={{0,1},{1,0},{2,3},{3,2},{4,5},{5,4},{6,7},{7,6},{8,9},{9,8},{10,11... | collective-permute-start | bytes 626696 | tf_op jit(solution)/shard_map/ppermute | solution.py:743
  33.3 1.8 %collective-permute-start.8 = (bf16[272,384]{1,0:T(8,128)(2,1)S(1)}, bf16[272,384]{1,0:T(8,128)(2,1)S(1)}, u32[]{:S(2)}, u32[]{:S(2)}) collective-permute-start(bf16[272,384]{1,0:T(8,128)(2,1)S(1)} %collective-permute-done.2.refs_3_), channel_id=1, source_target_pairs={{0,1},{1,0},{2,3},{3,2},{4,5},{5,4},{6,7},{7,6},{8,9},{9,8},{10,11... | collective-permute-start | bytes 626696 | tf_op jit(solution)/shard_map/ppermute | solution.py:743
  33.6 1.4 %collective-permute-start.14 = (bf16[272,256]{1,0:T(8,128)(2,1)S(1)}, bf16[272,256]{1,0:T(8,128)(2,1)S(1)}, u32[]{:S(2)}, u32[]{:S(2)}) collective-permute-start(bf16[272,256]{1,0:T(8,128)(2,1)S(1)} %collective-permute-done.10.refs_11_), channel_id=1, source_target_pairs={{0,1},{1,0},{2,3},{3,2},{4,5},{5,4},{6,7},{7,6},{8,9},{9,8},{10,11... | collective-permute-start | bytes 417800 | tf_op jit(solution)/shard_map/ppermute | solution.py:743
  43.9 13.7 %all-to-all-start = ((f32[4,256,128]{2,1,0:T(8,128)}), f32[4,256,128]{2,1,0:T(8,128)S(1)}, u32[]{:S(2)}, u32[]{:S(2)}) async-start(f32[4,256,128]{2,1,0:T(8,128)} %get-tuple-element.91), calls=%async_computation | async-start | bytes 1048576 | tf_op jit(solution)/shard_map/all_to_all | solution.py:755
  58.9 11.1 %all-to-all-start.1 = ((bf16[4,256,128]{2,1,0:T(8,128)(2,1)}), bf16[4,256,128]{2,1,0:T(8,128)(2,1)S(1)}, u32[]{:S(2)}, u32[]{:S(2)}) async-start(bf16[4,256,128]{2,1,0:T(8,128)(2,1)} %get-tuple-element.105), calls=%async_computation.1 | async-start | bytes 524288 | tf_op jit(solution)/shard_map/all_to_all | solution.py:755
  65.1 16.7 %collective-permute-start.19 = (bf16[128,1024]{1,0:T(8,128)(2,1)S(1)}, bf16[128,1024]{1,0:T(8,128)(2,1)}, u32[]{:S(2)}, u32[]{:S(2)}) collective-permute-start(bf16[128,1024]{1,0:T(8,128)(2,1)S(1)} %get-tuple-element.108), channel_id=1, source_target_pairs={{0,48},{16,0},{32,16},{48,32},{64,112},{80,64},{96,80},{112,96},{1... | collective-permute-start | bytes 786440 | tf_op jit(solution)/shard_map/ppermute | solution.py:751
  67.6 14.2 %collective-permute-start.18 = (bf16[128,1024]{1,0:T(8,128)(2,1)S(1)}, bf16[128,1024]{1,0:T(8,128)(2,1)}, u32[]{:S(2)}, u32[]{:S(2)}) collective-permute-start(bf16[128,1024]{1,0:T(8,128)(2,1)S(1)} %get-tuple-element.107), channel_id=1, source_target_pairs={{0,32},{16,48},{32,0},{48,16},{64,96},{80,112},{96,64},{112,80},{1... | collective-permute-start | bytes 786440 | tf_op jit(solution)/shard_map/ppermute | solution.py:751
  68.5 14.3 %collective-permute-start.17 = (bf16[128,1024]{1,0:T(8,128)(2,1)S(1)}, bf16[128,1024]{1,0:T(8,128)(2,1)}, u32[]{:S(2)}, u32[]{:S(2)}) collective-permute-start(bf16[128,1024]{1,0:T(8,128)(2,1)S(1)} %get-tuple-element.106), channel_id=1, source_target_pairs={{0,16},{16,32},{32,48},{48,0},{64,80},{80,96},{96,112},{112,64},{1... | collective-permute-start | bytes 786440 | tf_op jit(solution)/shard_map/ppermute | solution.py:751
  81.3 4.3 %collective-permute-start.15 = (bf16[4,256,256]{2,1,0:T(8,128)(2,1)S(1)}, bf16[4,256,256]{2,1,0:T(8,128)(2,1)S(1)}, u32[]{:S(2)}, u32[]{:S(2)}) collective-permute-start(bf16[4,256,256]{2,1,0:T(8,128)(2,1)S(1)} %get-tuple-element.112), channel_id=1, source_target_pairs={{0,1},{1,0},{2,3},{3,2},{4,5},{5,4},{6,7},{7,6},{8,9},{9,8},{10,11... | collective-permute-start | bytes 1572872 | tf_op jit(solution)/shard_map/ppermute | solution.py:743
  81.3 4.2 %collective-permute-start.16 = (bf16[4,256,256]{2,1,0:T(8,128)(2,1)S(1)}, bf16[4,256,256]{2,1,0:T(8,128)(2,1)S(1)}, u32[]{:S(2)}, u32[]{:S(2)}) collective-permute-start(bf16[4,256,256]{2,1,0:T(8,128)(2,1)S(1)} %get-tuple-element.113), channel_id=1, source_target_pairs={{0,1},{1,0},{2,3},{3,2},{4,5},{5,4},{6,7},{7,6},{8,9},{9,8},{10,11... | collective-permute-start | bytes 1572872 | tf_op jit(solution)/shard_map/ppermute | solution.py:743
  84.1 1.4 %collective-permute-start.20 = (bf16[64,1024]{1,0:T(8,128)(2,1)S(1)}, bf16[64,1024]{1,0:T(8,128)(2,1)S(1)}, u32[]{:S(2)}, u32[]{:S(2)}) collective-permute-start(bf16[64,1024]{1,0:T(8,128)(2,1)S(1)} %slice.12), channel_id=1, source_target_pairs={{0,1},{1,0},{2,3},{3,2},{4,5},{5,4},{6,7},{7,6},{8,9},{9,8},{10,11... | collective-permute-start | bytes 393224 | tf_op jit(solution)/shard_map/ppermute | solution.py:743
  84.2 1.3 %collective-permute-start.21 = (f32[16,128]{1,0:T(8,128)S(1)}, f32[16,128]{1,0:T(8,128)S(1)}, u32[]{:S(2)}, u32[]{:S(2)}) collective-permute-start(f32[16,128]{1,0:T(8,128)S(1)} %get-tuple-element.116.rab), channel_id=1, source_target_pairs={{0,1},{1,0},{2,3},{3,2},{4,5},{5,4},{6,7},{7,6},{8,9},{9,8},{10,11... | collective-permute-start | bytes 24584 | tf_op jit(solution)/shard_map/ppermute | solution.py:743
  85.9 10.1 %collective-permute-start.25 = (bf16[304,256]{1,0:T(8,128)(2,1)S(1)}, bf16[304,256]{1,0:T(8,128)(2,1)S(1)}, u32[]{:S(2)}, u32[]{:S(2)}) collective-permute-start(bf16[304,256]{1,0:T(8,128)(2,1)S(1)} %get-tuple-element.134), channel_id=1, source_target_pairs={{0,8},{1,9},{2,10},{3,11},{4,12},{5,13},{6,14},{7,15},{8,0},{9,1},... | collective-permute-start | bytes 466952 | tf_op jit(solution)/shard_map/ppermute | solution.py:743
  87.3 12.3 %collective-permute-start.26 = (bf16[304,256]{1,0:T(8,128)(2,1)S(1)}, bf16[304,256]{1,0:T(8,128)(2,1)S(1)}, u32[]{:S(2)}, u32[]{:S(2)}) collective-permute-start(bf16[304,256]{1,0:T(8,128)(2,1)S(1)} %get-tuple-element.135), channel_id=1, source_target_pairs={{0,10},{1,11},{2,12},{3,13},{4,14},{5,15},{6,8},{7,9},{8,2},{9,3},... | collective-permute-start | bytes 466952 | tf_op jit(solution)/shard_map/ppermute | solution.py:743
  90.6 19.7 %collective-permute-start.22 = (bf16[432,256]{1,0:T(8,128)(2,1)S(1)}, bf16[432,256]{1,0:T(8,128)(2,1)S(1)}, u32[]{:S(2)}, u32[]{:S(2)}) collective-permute-start(bf16[432,256]{1,0:T(8,128)(2,1)S(1)} %get-tuple-element.131), channel_id=1, source_target_pairs={{0,2},{1,3},{2,4},{3,5},{4,6},{5,7},{6,0},{7,1},{8,10},{9,11},{10,... | collective-permute-start | bytes 663560 | tf_op jit(solution)/shard_map/ppermute | solution.py:743
  92.1 18.3 %collective-permute-start.23 = (bf16[432,256]{1,0:T(8,128)(2,1)S(1)}, bf16[432,256]{1,0:T(8,128)(2,1)S(1)}, u32[]{:S(2)}, u32[]{:S(2)}) collective-permute-start(bf16[432,256]{1,0:T(8,128)(2,1)S(1)} %get-tuple-element.132), channel_id=1, source_target_pairs={{0,4},{1,5},{2,6},{3,7},{4,0},{5,1},{6,2},{7,3},{8,12},{9,13},{10,... | collective-permute-start | bytes 663560 | tf_op jit(solution)/shard_map/ppermute | solution.py:743
  93.6 17.3 %collective-permute-start.24 = (bf16[432,256]{1,0:T(8,128)(2,1)S(1)}, bf16[432,256]{1,0:T(8,128)(2,1)S(1)}, u32[]{:S(2)}, u32[]{:S(2)}) collective-permute-start(bf16[432,256]{1,0:T(8,128)(2,1)S(1)} %get-tuple-element.133), channel_id=1, source_target_pairs={{0,6},{1,7},{2,0},{3,1},{4,2},{5,3},{6,4},{7,5},{8,14},{9,15},{10,... | collective-permute-start | bytes 663560 | tf_op jit(solution)/shard_map/ppermute | solution.py:743
  95.9 10.5 %collective-permute-start.27 = (bf16[304,256]{1,0:T(8,128)(2,1)S(1)}, bf16[304,256]{1,0:T(8,128)(2,1)S(1)}, u32[]{:S(2)}, u32[]{:S(2)}) collective-permute-start(bf16[304,256]{1,0:T(8,128)(2,1)S(1)} %get-tuple-element.136), channel_id=1, source_target_pairs={{0,12},{1,13},{2,14},{3,15},{4,8},{5,9},{6,10},{7,11},{8,4},{9,5},... | collective-permute-start | bytes 466952 | tf_op jit(solution)/shard_map/ppermute | solution.py:743
  99.5 7.7 %collective-permute-start.28 = (bf16[304,256]{1,0:T(8,128)(2,1)S(1)}, bf16[304,256]{1,0:T(8,128)(2,1)S(1)}, u32[]{:S(2)}, u32[]{:S(2)}) collective-permute-start(bf16[304,256]{1,0:T(8,128)(2,1)S(1)} %get-tuple-element.137), channel_id=1, source_target_pairs={{0,14},{1,15},{2,8},{3,9},{4,10},{5,11},{6,12},{7,13},{8,6},{9,7},... | collective-permute-start | bytes 466952 | tf_op jit(solution)/shard_map/ppermute | solution.py:743
  112.4 11.1 %all-to-all-start.2 = ((f32[8,8,1024]{2,1,0:T(8,128)}), f32[8,8,1024]{2,1,0:T(8,128)S(1)}, u32[]{:S(2)}, u32[]{:S(2)}) async-start(f32[8,8,1024]{2,1,0:T(8,128)} %collect.1), calls=%async_computation.2 | async-start | bytes 524288 | tf_op jit(solution)/shard_map/all_to_all | solution.py:799
  (3 other events, 66.1 us)
